TPU v7x, 128 devices: a whole 4x4x4 slice. The times are simulated.
128 devices in a mesh: lat: 8 (over z, y_hi), lon: 16 (over y_lo, x, core).
Axes of the slice: x: 4, y: 4 (y_hi: 2, y_lo: 2; y = y_hi * 2 + y_lo), z: 4, core: 2. Of those that a mesh axis runs over, the one named last changes fastest.
Arguments:
- queries: bfloat16 [64, 768, 1024], P('lat', 'lon'), may hold values from -8 to 8
- key_vectors: bfloat16 [64, 768, 1024], P('lat', 'lon'), may hold values from -8 to 8
- value_vectors: bfloat16 [64, 768, 1024], P('lat', 'lon'), may hold values from -6 to 6
- cotangent: bfloat16 [64, 768, 1024], P('lat', 'lon'), may hold values from -6 to 6
- quad_weight: float32 [64], replicated, may hold values from 0.05 to 1
- lon_reach: int32 [64], P('lat'), may hold values from 1 to 96, as said below
Outputs:
- attended: bfloat16 [64, 768, 1024], P('lat', 'lon')
- grad_queries: bfloat16 [64, 768, 1024], P('lat', 'lon')
- grad_keys: bfloat16 [64, 768, 1024], P('lat', 'lon')
- grad_values: bfloat16 [64, 768, 1024], P('lat', 'lon')
Inputs may be any that keep to these rules, and one draw needn't show every extreme that they name: `lon_reach`: in latitude rows 0 and 63 it equals 96.
All inputs are finite; a program needn't handle non-finite values.
Results may differ from a plain program's by a relative error of at most 0.034.
Values may be sent and summed in bfloat16 or wider, within the bound.
No kernel may reach another device: no remote copies, remote signals or barrier semaphores. Data moves between devices by JAX's collectives and lax.ppermute only.
A program may use at most 384 MiB of HBM per device.

v0:
```python
import functools

import jax
import jax.numpy as jnp
from jax import lax
from jax.sharding import PartitionSpec as P

HEADS = 16
HEAD_DIM = 64
HALO = 2
SPAN = 2


def with_halo(cells, sides, width):
    for axis, dim in sides:
        count = lax.axis_size(axis)
        ends = count - 1
        head = lax.slice_in_dim(cells, 0, width, axis=dim)
        tail = lax.slice_in_dim(cells, cells.shape[dim] - width, cells.shape[dim], axis=dim)
        cells = jnp.concatenate(
            [
                lax.ppermute(tail, axis, [(i, (i + 1) % count) for i in range(ends)]),
                cells,
                lax.ppermute(head, axis, [((i + 1) % count, i) for i in range(ends)]),
            ],
            axis=dim,
        )
    return cells


def from_behind(block, axis, distance):
    devices = range(lax.axis_size(axis))
    route = [((i - distance) % len(devices), i) for i in devices]
    return lax.ppermute(block, axis, route)


def from_behind_2(value, axis, steps):
    count = lax.axis_size(axis)
    leading, last = (max(0, -steps), min(count, count - steps))
    return lax.ppermute(value, axis, [(source, source + steps) for source in range(leading, last)])


def to_slab(ext_block, row_count):
    window_rows = 2 * HALO + 1
    pieces = [ext_block[:, w : w + row_count] for w in range(window_rows)]
    stacked = jnp.stack(pieces, axis=2)
    return stacked.reshape(
        stacked.shape[0], row_count, window_rows * stacked.shape[3], stacked.shape[4]
    )


def from_slab(slab_grads, row_count, col_count):
    window_rows = 2 * HALO + 1
    shaped = slab_grads.reshape(
        slab_grads.shape[0], row_count, window_rows, col_count, slab_grads.shape[-1]
    )
    result = jnp.zeros(
        (slab_grads.shape[0], row_count + 2 * HALO, col_count, slab_grads.shape[-1]), jnp.float32
    )
    for w in range(window_rows):
        result = result.at[:, w : w + row_count].add(shaped[:, :, w])
    return result


def attend_block(carried, query_heads, kv_slab, allowed, key_weight, score_scale):
    maxima, totals, summed = carried
    row_count, key_count = (kv_slab.shape[1], kv_slab.shape[2])
    key_heads = kv_slab[0].reshape(row_count, key_count, HEADS, HEAD_DIM)
    value_heads = kv_slab[1].reshape(row_count, key_count, HEADS, HEAD_DIM)
    scores = (
        jnp.einsum("rqhd,rkhd->hrqk", query_heads, key_heads, preferred_element_type=jnp.float32)
        * score_scale
    )
    block_max = jnp.max(jnp.where(allowed[None], scores, -jnp.inf), axis=-1)
    fresh = jnp.maximum(maxima, block_max)
    weights = key_weight[None, :, None, :] * jnp.exp(
        jnp.where(allowed[None], scores - fresh[..., None], -jnp.inf)
    )
    factor = jnp.exp(maxima - fresh)
    totals = totals * factor + jnp.sum(weights, axis=-1)
    summed = summed * factor[..., None] + jnp.einsum(
        "hrqk,rkhd->hrqd",
        weights.astype(jnp.bfloat16),
        value_heads,
        preferred_element_type=jnp.float32,
    )
    return (fresh, totals, summed)


def block_grads(query_pack, kv_slab, allowed, key_weight, score_scale):
    query_flat, cot_flat, log_totals, deltas = query_pack
    row_count, col_count, feature_width = query_flat.shape
    key_count = kv_slab.shape[2]
    query_heads = query_flat.reshape(row_count, col_count, HEADS, HEAD_DIM)
    cot_heads = cot_flat.reshape(row_count, col_count, HEADS, HEAD_DIM)
    key_heads = kv_slab[0].reshape(row_count, key_count, HEADS, HEAD_DIM)
    value_heads = kv_slab[1].reshape(row_count, key_count, HEADS, HEAD_DIM)
    scores = (
        jnp.einsum("rqhd,rkhd->hrqk", query_heads, key_heads, preferred_element_type=jnp.float32)
        * score_scale
    )
    probs = key_weight[None, :, None, :] * jnp.exp(
        jnp.where(allowed[None], scores - log_totals[..., None], -jnp.inf)
    )
    prob_grads = jnp.einsum(
        "rqhd,rkhd->hrqk", cot_heads, value_heads, preferred_element_type=jnp.float32
    )
    score_grads = (probs * (prob_grads - deltas[..., None])).astype(jnp.bfloat16)
    results = []
    grad_query = (
        jnp.einsum("hrqk,rkhd->rqhd", score_grads, key_heads, preferred_element_type=jnp.float32)
        * score_scale
    )
    results.append(grad_query.reshape(row_count, col_count, feature_width))
    grad_key = (
        jnp.einsum("hrqk,rqhd->rkhd", score_grads, query_heads, preferred_element_type=jnp.float32)
        * score_scale
    )
    grad_value = jnp.einsum(
        "hrqk,rqhd->rkhd", probs.astype(jnp.bfloat16), cot_heads, preferred_element_type=jnp.float32
    )
    slab_grads = jnp.stack(
        [
            grad_key.reshape(row_count, key_count, feature_width),
            grad_value.reshape(row_count, key_count, feature_width),
        ]
    )
    results.append(from_slab(slab_grads, row_count, col_count))
    return tuple(results)


def on_device(queries, key_vectors, value_vectors, cotangent, quad_weight, lon_reach):
    row_count, col_count, feature_width = queries.shape
    ext_rows = row_count + 2 * HALO
    window_rows = 2 * HALO + 1
    score_scale = float(HEAD_DIM) ** (-0.5)
    band_index = lax.axis_index("lat")
    own_rows = jnp.arange(row_count, dtype=jnp.int32)
    slab_offsets = jnp.arange(window_rows, dtype=jnp.int32)
    ext_index = band_index * row_count + own_rows[:, None] + slab_offsets[None, :]
    global_rows = ext_index - HALO
    inside = (global_rows >= 0) & (global_rows < quad_weight.shape[0])
    inside_keys = jnp.repeat(inside, col_count, axis=1)
    padded_weight = jnp.pad(quad_weight, HALO)
    key_weight = jnp.repeat(padded_weight[ext_index], col_count, axis=1)
    query_cols = jnp.arange(col_count, dtype=jnp.int32)
    key_cols = jnp.tile(jnp.arange(col_count, dtype=jnp.int32), window_rows)

    def allowed_at(offset):
        col_gap = offset * col_count + key_cols[None, :] - query_cols[:, None]
        near = jnp.abs(col_gap)[None, :, :] <= lon_reach[:, None, None]
        return near & inside_keys[:, None, :]

    stacked = jnp.stack([key_vectors, value_vectors])
    extended = with_halo(stacked, (("lat", 1),), HALO)
    blocks = {0: extended}
    upward_block = extended
    downward_block = extended
    for stride in range(1, SPAN + 1):
        upward_block = from_behind(upward_block, "lon", 1)
        downward_block = from_behind(downward_block, "lon", -1)
        blocks[-stride] = upward_block
        blocks[stride] = downward_block
    slabs = {offset: to_slab(block, row_count) for offset, block in blocks.items()}
    visit_order = [0]
    for stride in range(1, SPAN + 1):
        visit_order = visit_order + [stride, -stride]
    query_heads = queries.reshape(row_count, col_count, HEADS, HEAD_DIM)
    carried = (
        jnp.full((HEADS, row_count, col_count), -jnp.inf, jnp.float32),
        jnp.zeros((HEADS, row_count, col_count), jnp.float32),
        jnp.zeros((HEADS, row_count, col_count, HEAD_DIM), jnp.float32),
    )
    for offset in visit_order:
        update = functools.partial(
            attend_block,
            query_heads=query_heads,
            kv_slab=slabs[offset],
            allowed=allowed_at(offset),
            key_weight=key_weight,
            score_scale=score_scale,
        )
        carried = update(carried)
    maxima, totals, summed = carried
    attended_heads = (summed / totals[..., None]).transpose(1, 2, 0, 3).astype(jnp.bfloat16)
    attended = attended_heads.reshape(row_count, col_count, feature_width)
    cot_heads = cotangent.reshape(row_count, col_count, HEADS, HEAD_DIM)
    deltas = jnp.einsum(
        "rqhd,rqhd->hrq", cot_heads, attended_heads, preferred_element_type=jnp.float32
    )
    log_totals = maxima + jnp.log(totals)
    own_pack = (queries, cotangent, log_totals, deltas)
    zero_query = jnp.zeros((row_count, col_count, feature_width), jnp.float32)
    zero_keys = jnp.zeros((2, ext_rows, col_count, feature_width), jnp.float32)

    def both_update(offset, carried_pair):
        grad_query, grad_keys = block_grads(
            own_pack, slabs[offset], allowed_at(offset), key_weight, score_scale
        )
        return (carried_pair[0] + grad_query, carried_pair[1] + grad_keys)

    grad_query = zero_query
    moving = zero_keys
    for offset in range(SPAN, 0, -1):
        grad_query, moving = both_update(offset, (grad_query, moving))
        moving = from_behind(moving.astype(jnp.bfloat16), "lon", 1).astype(moving.dtype)
    upward = moving
    moving = zero_keys
    for offset in range(-SPAN, 0):
        grad_query, moving = both_update(offset, (grad_query, moving))
        moving = from_behind(moving.astype(jnp.bfloat16), "lon", -1).astype(moving.dtype)
    grad_query, home_grads = both_update(0, (grad_query, upward + moving))
    upper_rim = home_grads[:, :HALO]
    lower_rim = home_grads[:, ext_rows - HALO :]
    center = home_grads[:, HALO : HALO + row_count]
    from_above = from_behind_2(lower_rim.astype(jnp.bfloat16), "lat", 1).astype(lower_rim.dtype)
    from_below = from_behind_2(upper_rim.astype(jnp.bfloat16), "lat", -1).astype(upper_rim.dtype)
    center = center.at[:, :HALO].add(from_above)
    center = center.at[:, row_count - HALO :].add(from_below)
    grad_queries = grad_query.astype(jnp.bfloat16)
    return (attended, grad_queries, center[0].astype(jnp.bfloat16), center[1].astype(jnp.bfloat16))


def solution(mesh):
    placed = (
        P("lat", "lon", None),
        P("lat", "lon", None),
        P("lat", "lon", None),
        P("lat", "lon", None),
        P(),
        P("lat"),
    )
    return jax.shard_map(
        on_device,
        mesh=mesh,
        in_specs=placed,
        out_specs=(
            P("lat", "lon", None),
            P("lat", "lon", None),
            P("lat", "lon", None),
            P("lat", "lon", None),
        ),
        check_vma=False,
    )
```

profile of v0, /device:TPU:0, one launch (start us, length us, event | category | flops | bytes accessed | tf_op | source)
XLA Modules:
  0.0 992.6 jit_solution(15497486257735509664)
XLA Ops:
  41.5 11.3 %reshape_squeeze.40 = bf16[8,240,16,64]{3,2,1,0:T(8,128)(2,1)} reshape(bf16[1,8,5,48,1024]{4,3,2,1,0:T(8,128)(2,1)} %copy.60) | data formatting | bytes 7864320 | tf_op jit(solution)/shard_map/reshape;squeeze | solution.py:68
  52.8 11.9 %fusion.53 = (f32[16,8,48]{2,1,0:T(8,128)S(1)}, f32[16,8,240,48]{2,3,1,0:T(8,128)}) fusion(pred[8,48,240]{2,1,0:T(8,128)(4,1)S(1)} %copy-done.30, bf16[8,240,16,64]{3,2,1,0:T(8,128)(2,1)} %reshape_squeeze.40, bf16[8,48,16,64]{3,2,1,0:T(8,128)(2,1)S(1)} %reshape.1344), kind=kOutput, calls=%fused_computation.79 | convolution fusion | flops 193161216 | bytes 10733568 | tf_op jit(solution)/shard_map/rqhd,rkhd->hrqk/dot_general | solution.py:71
  67.1 11.2 %reshape_squeeze.41 = bf16[8,240,16,64]{3,2,1,0:T(8,128)(2,1)} reshape(bf16[1,8,5,48,1024]{4,3,2,1,0:T(8,128)(2,1)} %copy.63) | data formatting | bytes 7864320 | tf_op jit(solution)/shard_map/reshape;squeeze | solution.py:69
  144.6 12.0 %fusion.46 = (f32[16,8,48]{2,1,0:T(8,128)S(1)}, f32[16,8,240,48]{2,3,1,0:T(8,128)}) fusion(pred[8,48,240]{2,1,0:T(8,128)(4,1)S(1)} %get-tuple-element.368, bf16[8,240,16,64]{3,2,1,0:T(8,128)(2,1)} %reshape_squeeze.42, bf16[8,48,16,64]{3,2,1,0:T(8,128)(2,1)S(1)} %reshape.1344), kind=kOutput, calls=%fused_computation.69 | convolution fusion | flops 193161216 | bytes 10733568 | tf_op jit(solution)/shard_map/rqhd,rkhd->hrqk/dot_general | solution.py:71
  167.2 11.2 %reshape_squeeze.43 = bf16[8,240,16,64]{3,2,1,0:T(8,128)(2,1)} reshape(bf16[1,8,5,48,1024]{4,3,2,1,0:T(8,128)(2,1)} %copy.68) | data formatting | bytes 7864320 | tf_op jit(solution)/shard_map/reshape;squeeze | solution.py:69
  192.7 11.2 %reshape_squeeze.45 = bf16[8,240,16,64]{3,2,1,0:T(8,128)(2,1)} reshape(bf16[1,8,5,48,1024]{4,3,2,1,0:T(8,128)(2,1)} %copy.73) | data formatting | bytes 7864320 | tf_op jit(solution)/shard_map/reshape;squeeze | solution.py:69
  249.6 11.4 %reshape_squeeze.48 = bf16[8,240,16,64]{3,2,1,0:T(8,128)(2,1)} reshape(bf16[1,8,5,48,1024]{4,3,2,1,0:T(8,128)(2,1)} %copy.80) | data formatting | bytes 7864320 | tf_op jit(solution)/shard_map/reshape;squeeze | solution.py:68
  261.0 11.9 %fusion.32 = (f32[16,8,48]{2,1,0:T(8,128)S(1)}, f32[16,8,240,48]{2,3,1,0:T(8,128)}) fusion(pred[8,48,240]{2,1,0:T(8,128)(4,1)S(1)} %get-tuple-element.370, bf16[8,240,16,64]{3,2,1,0:T(8,128)(2,1)} %reshape_squeeze.46, bf16[8,48,16,64]{3,2,1,0:T(8,128)(2,1)S(1)} %reshape.1344), kind=kOutput, calls=%fused_computation.49 | convolution fusion | flops 193161216 | bytes 10733568 | tf_op jit(solution)/shard_map/rqhd,rkhd->hrqk/dot_general | solution.py:71
  272.9 11.9 %fusion.25 = (f32[16,8,48]{2,1,0:T(8,128)S(1)}, f32[16,8,240,48]{2,3,1,0:T(8,128)}) fusion(pred[8,48,240]{2,1,0:T(8,128)(4,1)S(1)} %get-tuple-element.371, bf16[8,240,16,64]{3,2,1,0:T(8,128)(2,1)} %reshape_squeeze.48, bf16[8,48,16,64]{3,2,1,0:T(8,128)(2,1)S(1)} %reshape.1344), kind=kOutput, calls=%fused_computation.39 | convolution fusion | flops 193161216 | bytes 10733568 | tf_op jit(solution)/shard_map/rqhd,rkhd->hrqk/dot_general | solution.py:71
  284.8 13.6 %fusion.61 = (f32[16,8,48]{2,1,0:T(8,128)S(1)}, f32[16,8,48]{2,1,0:T(8,128)S(1)}, f32[16,8,48]{2,1,0:T(8,128)S(1)}, f32[16,8,48]{2,1,0:T(8,128)S(1)}, f32[16,8,48]{2,1,0:T(8,128)S(1)}) fusion(f32[16,8,240,48]{2,3,1,0:T(8,128)} %get-tuple-element.384, f32[16,8,48]{2,1,0:T(8,128)S(1)} %get-tuple-element.383, f32[8,240]{1,0:T(8,128)S(1)} %mul.266, ...), kind=kLoop, calls=%fused_computation.90 | loop fusion | flops 36833280 | bytes 30205440 | tf_op jit(solution)/shard_map/reduce_sum | solution.py:80
  327.8 11.2 %reshape_squeeze.49 = bf16[8,240,16,64]{3,2,1,0:T(8,128)(2,1)} reshape(bf16[1,8,5,48,1024]{4,3,2,1,0:T(8,128)(2,1)} %copy.83) | data formatting | bytes 7864320 | tf_op jit(solution)/shard_map/reshape;squeeze | solution.py:69
  407.6 15.6 %fusion.69 = (bf16[16,8,48,240]{3,2,1,0:T(8,128)(2,1)S(1)}, bf16[16,8,48,240]{3,2,1,0:T(8,128)(2,1)}, bf16[16,8,48,240]{3,2,1,0:T(8,128)(2,1)}, bf16[16,8,48,240]{3,2,1,0:T(8,128)(2,1)}, bf16[16,8,48,240]{3,2,1,0:T(8,128)(2,1)}) fusion(f32[16,8,240,48]{2,3,1,0:T(8,128)} %get-tuple-element.380, f32[16,8,48]{2,1,0:T(8,128)S(1)} %copy-done.34, ...), kind=kLoop, calls=%fused_computation.98 | loop fusion | flops 36864000 | bytes 44729856 | tf_op jit(solution)/shard_map/convert_element_type | solution.py:120
  462.8 13.9 %copy.119 = f32[8,240,16,64]{3,2,1,0:T(8,128)} copy(f32[8,240,16,64]{1,3,2,0:T(8,128)} %multiply_bitcast_fusion.3) | data formatting | bytes 15728640 | tf_op jit(solution)/shard_map/mul | solution.py:116
  476.7 14.1 %stack.170 = f32[1,8,5,48,1024]{4,3,2,1,0:T(8,128)} reshape(f32[8,240,16,64]{3,2,1,0:T(8,128)} %copy.119) | data formatting | bytes 15728640 | tf_op jit(solution)/shard_map/stack | solution.py:122
  490.8 13.9 %copy.135 = f32[8,240,16,64]{3,2,1,0:T(8,128)} copy(f32[8,240,16,64]{1,3,2,0:T(8,128)} %multiply_bitcast_fusion.1) | data formatting | bytes 15728640 | tf_op jit(solution)/shard_map/mul | solution.py:116
  504.8 14.2 %stack.176 = f32[1,8,5,48,1024]{4,3,2,1,0:T(8,128)} reshape(f32[8,240,16,64]{3,2,1,0:T(8,128)} %copy.135) | data formatting | bytes 15728640 | tf_op jit(solution)/shard_map/stack | solution.py:122
  519.0 13.9 %copy.109 = f32[8,240,16,64]{3,2,1,0:T(8,128)} copy(f32[8,240,16,64]{1,3,2,0:T(8,128)} %multiply_bitcast_fusion.4) | data formatting | bytes 15728640 | tf_op jit(solution)/shard_map/mul | solution.py:116
  532.9 14.4 %stack.167 = f32[1,8,5,48,1024]{4,3,2,1,0:T(8,128)} reshape(f32[8,240,16,64]{3,2,1,0:T(8,128)} %copy.109) | data formatting | bytes 15728640 | tf_op jit(solution)/shard_map/stack | solution.py:122
  547.2 13.9 %copy.143 = f32[8,240,16,64]{3,2,1,0:T(8,128)} copy(f32[8,240,16,64]{1,3,2,0:T(8,128)} %multiply_bitcast_fusion) | data formatting | bytes 15728640 | tf_op jit(solution)/shard_map/mul | solution.py:116
  561.2 14.2 %stack.179 = f32[1,8,5,48,1024]{4,3,2,1,0:T(8,128)} reshape(f32[8,240,16,64]{3,2,1,0:T(8,128)} %copy.143) | data formatting | bytes 15728640 | tf_op jit(solution)/shard_map/stack | solution.py:122
  575.3 13.9 %copy.127 = f32[8,240,16,64]{3,2,1,0:T(8,128)} copy(f32[8,240,16,64]{1,3,2,0:T(8,128)} %multiply_bitcast_fusion.2) | data formatting | bytes 15728640 | tf_op jit(solution)/shard_map/mul | solution.py:116
  589.3 14.2 %stack.173 = f32[1,8,5,48,1024]{4,3,2,1,0:T(8,128)} reshape(f32[8,240,16,64]{3,2,1,0:T(8,128)} %copy.127) | data formatting | bytes 15728640 | tf_op jit(solution)/shard_map/stack | solution.py:122
  603.5 13.9 %copy.112 = f32[8,240,16,64]{3,2,1,0:T(8,128)} copy(f32[8,240,16,64]{1,3,2,0:T(8,128)} %convolution_bitcast_fusion.4) | data formatting | bytes 15728640 | tf_op jit(solution)/shard_map/hrqk,rqhd->rkhd/transpose | solution.py:119
  617.4 14.2 %stack.168 = f32[1,8,5,48,1024]{4,3,2,1,0:T(8,128)} reshape(f32[8,240,16,64]{3,2,1,0:T(8,128)} %copy.112) | data formatting | bytes 15728640 | tf_op jit(solution)/shard_map/stack | solution.py:122
  672.1 14.4 %copy.146 = f32[8,240,16,64]{3,2,1,0:T(8,128)} copy(f32[8,240,16,64]{1,3,2,0:T(8,128)} %convolution_bitcast_fusion) | data formatting | bytes 15728640 | tf_op jit(solution)/shard_map/hrqk,rqhd->rkhd/transpose | solution.py:119
  686.5 14.2 %stack.180 = f32[1,8,5,48,1024]{4,3,2,1,0:T(8,128)} reshape(f32[8,240,16,64]{3,2,1,0:T(8,128)} %copy.146) | data formatting | bytes 15728640 | tf_op jit(solution)/shard_map/stack | solution.py:122
  735.1 14.0 %copy.122 = f32[8,240,16,64]{3,2,1,0:T(8,128)} copy(f32[8,240,16,64]{1,3,2,0:T(8,128)} %convolution_bitcast_fusion.3) | data formatting | bytes 15728640 | tf_op jit(solution)/shard_map/hrqk,rqhd->rkhd/transpose | solution.py:119
  749.1 14.3 %stack.171 = f32[1,8,5,48,1024]{4,3,2,1,0:T(8,128)} reshape(f32[8,240,16,64]{3,2,1,0:T(8,128)} %copy.122) | data formatting | bytes 15728640 | tf_op jit(solution)/shard_map/stack | solution.py:122
  806.7 14.0 %copy.130 = f32[8,240,16,64]{3,2,1,0:T(8,128)} copy(f32[8,240,16,64]{1,3,2,0:T(8,128)} %convolution_bitcast_fusion.2) | data formatting | bytes 15728640 | tf_op jit(solution)/shard_map/hrqk,rqhd->rkhd/transpose | solution.py:119
  820.7 14.4 %stack.174 = f32[1,8,5,48,1024]{4,3,2,1,0:T(8,128)} reshape(f32[8,240,16,64]{3,2,1,0:T(8,128)} %copy.130) | data formatting | bytes 15728640 | tf_op jit(solution)/shard_map/stack | solution.py:122
  860.1 14.2 %copy.138 = f32[8,240,16,64]{3,2,1,0:T(8,128)} copy(f32[8,240,16,64]{1,3,2,0:T(8,128)} %convolution_bitcast_fusion.1) | data formatting | bytes 15728640 | tf_op jit(solution)/shard_map/hrqk,rqhd->rkhd/transpose | solution.py:119
  874.3 14.1 %stack.177 = f32[1,8,5,48,1024]{4,3,2,1,0:T(8,128)} reshape(f32[8,240,16,64]{3,2,1,0:T(8,128)} %copy.138) | data formatting | bytes 15728640 | tf_op jit(solution)/shard_map/stack | solution.py:122
  (344 shorter events, 563.9 us)
Async XLA Ops:
  2.9 14.1 %copy-start.42 = (s32[8]{0:T(128)S(1)}, s32[8]{0:T(128)}, u32[]{:S(2)}) copy-start(s32[8]{0:T(128)} %param.65) | copy-start | bytes 100
  2.9 15.1 %collective-permute-start = (bf16[2,2,48,1024]{3,2,1,0:T(8,128)(2,1)}, bf16[2,2,48,1024]{3,2,1,0:T(8,128)(2,1)}, u32[]{:S(2)}, u32[]{:S(2)}) collective-permute-start(bf16[2,2,48,1024]{3,2,1,0:T(8,128)(2,1)} %get-tuple-element.360), channel_id=1, source_target_pairs={{0,16},{16,32},{32,48},{48,64},{64,80},{80,96},{96,112},{1,17},{17... | collective-permute-start | bytes 1179656 | tf_op jit(solution)/shard_map/ppermute | solution.py:22
  9.0 18.5 %collective-permute-start.1 = (bf16[2,2,48,1024]{3,2,1,0:T(8,128)(2,1)}, bf16[2,2,48,1024]{3,2,1,0:T(8,128)(2,1)}, u32[]{:S(2)}, u32[]{:S(2)}) collective-permute-start(bf16[2,2,48,1024]{3,2,1,0:T(8,128)(2,1)} %get-tuple-element.361), channel_id=1, source_target_pairs={{16,0},{32,16},{48,32},{64,48},{80,64},{96,80},{112,96},{17,1},{33... | collective-permute-start | bytes 1179656 | tf_op jit(solution)/shard_map/ppermute | solution.py:24
  11.2 16.2 %copy-start.24 = (bf16[8,48,1024]{2,1,0:T(8,128)(2,1)S(1)}, bf16[8,48,1024]{2,1,0:T(8,128)(2,1)}, u32[]{:S(2)}) copy-start(bf16[8,48,1024]{2,1,0:T(8,128)(2,1)} %param.61) | copy-start | bytes 2359300
  11.2 16.2 %copy-start.25 = (bf16[8,48,1024]{2,1,0:T(8,128)(2,1)S(1)}, bf16[8,48,1024]{2,1,0:T(8,128)(2,1)}, u32[]{:S(2)}) copy-start(bf16[8,48,1024]{2,1,0:T(8,128)(2,1)} %param.62) | copy-start | bytes 2359300
  30.3 67.9 %collective-permute-start.3 = (bf16[2,12,48,1024]{3,2,1,0:T(8,128)(2,1)}, bf16[2,12,48,1024]{3,2,1,0:T(8,128)(2,1)}, u32[]{:S(2)}, u32[]{:S(2)}) collective-permute-start(bf16[2,12,48,1024]{3,2,1,0:T(8,128)(2,1)} %pad_maximum_fusion), channel_id=1, source_target_pairs={{15,0},{0,1},{1,2},{2,3},{3,4},{4,5},{5,6},{6,7},{7,8},{8,9},{9,10... | collective-permute-start | bytes 7077896 | tf_op jit(solution)/shard_map/ppermute | solution.py:34
  30.3 57.5 %collective-permute-start.2 = (bf16[2,12,48,1024]{3,2,1,0:T(8,128)(2,1)}, bf16[2,12,48,1024]{3,2,1,0:T(8,128)(2,1)}, u32[]{:S(2)}, u32[]{:S(2)}) collective-permute-start(bf16[2,12,48,1024]{3,2,1,0:T(8,128)(2,1)} %pad_maximum_fusion), channel_id=1, source_target_pairs={{1,0},{2,1},{3,2},{4,3},{5,4},{6,5},{7,6},{8,7},{9,8},{10,9},{11,1... | collective-permute-start | bytes 7077896 | tf_op jit(solution)/shard_map/ppermute | solution.py:34
  52.8 11.9 %copy-start.13 = (bf16[1,8,5,48,1024]{4,3,1,0,2:T(8,128)(2,1)S(1)}, bf16[1,8,5,48,1024]{4,3,1,0,2:T(8,128)(2,1)}, u32[]{:S(2)}) copy-start(bf16[1,8,5,48,1024]{4,3,1,0,2:T(8,128)(2,1)} %get-tuple-element.344) | copy-start | bytes 11796484
  64.7 234.5 %copy-start.27 = (f32[16,8,48]{2,1,0:T(8,128)}, f32[16,8,48]{2,1,0:T(8,128)S(1)}, u32[]{:S(2)}) copy-start(f32[16,8,48]{2,1,0:T(8,128)S(1)} %get-tuple-element.383) | copy-start | bytes 73732
  87.8 125.6 %collective-permute-start.4 = (bf16[2,12,48,1024]{3,2,1,0:T(8,128)(2,1)}, bf16[2,12,48,1024]{3,2,1,0:T(8,128)(2,1)}, u32[]{:S(2)}, u32[]{:S(2)}) collective-permute-start(bf16[2,12,48,1024]{3,2,1,0:T(8,128)(2,1)} %collective-permute-done.2), channel_id=1, source_target_pairs={{1,0},{2,1},{3,2},{4,3},{5,4},{6,5},{7,6},{8,7},{9,8},{10,9},{11,1... | collective-permute-start | bytes 7077896 | tf_op jit(solution)/shard_map/ppermute | solution.py:34
  144.2 93.0 %collective-permute-start.5 = (bf16[2,12,48,1024]{3,2,1,0:T(8,128)(2,1)}, bf16[2,12,48,1024]{3,2,1,0:T(8,128)(2,1)}, u32[]{:S(2)}, u32[]{:S(2)}) collective-permute-start(bf16[2,12,48,1024]{3,2,1,0:T(8,128)(2,1)} %collective-permute-done.3), channel_id=1, source_target_pairs={{15,0},{0,1},{1,2},{2,3},{3,4},{4,5},{5,6},{6,7},{7,8},{8,9},{9,10... | collective-permute-start | bytes 7077896 | tf_op jit(solution)/shard_map/ppermute | solution.py:34
  144.6 12.0 %copy-start.1 = (bf16[8,240,16,64]{3,2,1,0:T(8,128)(2,1)S(1)}, bf16[8,240,16,64]{3,2,1,0:T(8,128)(2,1)}, u32[]{:S(2)}) copy-start(bf16[8,240,16,64]{3,2,1,0:T(8,128)(2,1)} %reshape_squeeze.44) | copy-start | bytes 11796484
  261.0 23.8 %slice-start.4 = ((s8[6291456]{0:T(1024)(128)(4,1)}), s8[4194304]{0:T(1024)(128)(4,1)S(1)}, s32[]{:S(2)}) async-start(s8[6291456]{0:T(1024)(128)(4,1)} %bitcast.653), calls=%async_computation.4 | async-start | bytes 8388608
  272.9 11.9 %slice-start = ((s8[6291456]{0:T(1024)(128)(4,1)}), s8[4194304]{0:T(1024)(128)(4,1)S(1)}, s32[]{:S(2)}) async-start(s8[6291456]{0:T(1024)(128)(4,1)} %bitcast.649), calls=%async_computation | async-start | bytes 8388608
  272.9 11.9 %slice-start.1 = ((s8[6291456]{0:T(1024)(128)(4,1)}), s8[2097152]{0:T(1024)(128)(4,1)S(1)}, s32[]{:S(2)}) async-start(s8[6291456]{0:T(1024)(128)(4,1)} %bitcast.649), calls=%async_computation.1 | async-start | bytes 4194304
  272.9 11.9 %slice-start.5 = ((s8[6291456]{0:T(1024)(128)(4,1)}), s8[2097152]{0:T(1024)(128)(4,1)S(1)}, s32[]{:S(2)}) async-start(s8[6291456]{0:T(1024)(128)(4,1)} %bitcast.653), calls=%async_computation.5 | async-start | bytes 4194304
  284.8 15.1 %copy-start.11 = (bf16[1,8,5,48,1024]{4,3,1,0,2:T(8,128)(2,1)S(1)}, bf16[1,8,5,48,1024]{4,3,1,0,2:T(8,128)(2,1)}, u32[]{:S(2)}) copy-start(bf16[1,8,5,48,1024]{4,3,1,0,2:T(8,128)(2,1)} %get-tuple-element.350) | copy-start | bytes 11796484
  348.6 12.3 %slice-start.8 = ((s8[6291456]{0:T(1024)(128)(4,1)}), s8[4194304]{0:T(1024)(128)(4,1)S(1)}, s32[]{:S(2)}) async-start(s8[6291456]{0:T(1024)(128)(4,1)} %bitcast.657), calls=%async_computation.8 | async-start | bytes 8388608
  393.9 13.7 %slice-start.2 = ((s8[6291456]{0:T(1024)(128)(4,1)}), s8[4194304]{0:T(1024)(128)(4,1)S(1)}, s32[]{:S(2)}) async-start(s8[6291456]{0:T(1024)(128)(4,1)} %bitcast.651), calls=%async_computation.2 | async-start | bytes 8388608
  393.9 13.7 %slice-start.6 = ((s8[6291456]{0:T(1024)(128)(4,1)}), s8[4194304]{0:T(1024)(128)(4,1)S(1)}, s32[]{:S(2)}) async-start(s8[6291456]{0:T(1024)(128)(4,1)} %bitcast.655), calls=%async_computation.6 | async-start | bytes 8388608
  428.8 15.7 %copy-start.16 = (bf16[16,8,48,240]{3,2,1,0:T(8,128)(2,1)}, bf16[16,8,48,240]{3,2,1,0:T(8,128)(2,1)S(1)}, u32[]{:S(2)}) copy-start(bf16[16,8,48,240]{3,2,1,0:T(8,128)(2,1)S(1)} %fusion.20) | copy-start | bytes 8847364
  435.2 13.9 %copy-start.18 = (bf16[16,8,48,240]{3,2,1,0:T(8,128)(2,1)}, bf16[16,8,48,240]{3,2,1,0:T(8,128)(2,1)S(1)}, u32[]{:S(2)}) copy-start(bf16[16,8,48,240]{3,2,1,0:T(8,128)(2,1)S(1)} %fusion.24) | copy-start | bytes 8847364
  631.5 16.0 %slice-start.28 = ((s8[7864320]{0:T(1024)(128)(4,1)}), s8[4194304]{0:T(1024)(128)(4,1)S(1)}, s32[]{:S(2)}) async-start(s8[7864320]{0:T(1024)(128)(4,1)} %bitcast.677), calls=%async_computation.28 | async-start | bytes 8388608
  659.0 255.2 %collective-permute-start.6 = (bf16[2,12,48,1024]{3,2,1,0:T(8,128)(2,1)}, bf16[2,12,48,1024]{3,2,1,0:T(8,128)(2,1)}, u32[]{:S(2)}, u32[]{:S(2)}) collective-permute-start(bf16[2,12,48,1024]{3,2,1,0:T(8,128)(2,1)} %convert_element_type.103), channel_id=1, source_target_pairs={{15,0},{0,1},{1,2},{2,3},{3,4},{4,5},{5,6},{6,7},{7,8},{8,9},{9,10... | collective-permute-start | bytes 7077896 | tf_op jit(solution)/shard_map/ppermute | solution.py:34
  856.7 62.9 %collective-permute-start.8 = (bf16[2,12,48,1024]{3,2,1,0:T(8,128)(2,1)}, bf16[2,12,48,1024]{3,2,1,0:T(8,128)(2,1)}, u32[]{:S(2)}, u32[]{:S(2)}) collective-permute-start(bf16[2,12,48,1024]{3,2,1,0:T(8,128)(2,1)} %convert_element_type.109), channel_id=1, source_target_pairs={{1,0},{2,1},{3,2},{4,3},{5,4},{6,5},{7,6},{8,7},{9,8},{10,9},{11,1... | collective-permute-start | bytes 7077896 | tf_op jit(solution)/shard_map/ppermute | solution.py:34
  919.6 30.7 %collective-permute-start.7 = (bf16[2,12,48,1024]{3,2,1,0:T(8,128)(2,1)}, bf16[2,12,48,1024]{3,2,1,0:T(8,128)(2,1)}, u32[]{:S(2)}, u32[]{:S(2)}) collective-permute-start(bf16[2,12,48,1024]{3,2,1,0:T(8,128)(2,1)} %add_convert_fusion.1), channel_id=1, source_target_pairs={{15,0},{0,1},{1,2},{2,3},{3,4},{4,5},{5,6},{6,7},{7,8},{8,9},{9,10... | collective-permute-start | bytes 7077896 | tf_op jit(solution)/shard_map/ppermute | solution.py:34
  919.6 14.2 %slice-start.14 = ((s8[7864320]{0:T(1024)(128)(4,1)}), s8[3670016]{0:T(1024)(128)(4,1)S(1)}, s32[]{:S(2)}) async-start(s8[7864320]{0:T(1024)(128)(4,1)} %bitcast.663), calls=%async_computation.14 | async-start | bytes 7340032
  923.8 31.0 %collective-permute-start.9 = (bf16[2,12,48,1024]{3,2,1,0:T(8,128)(2,1)}, bf16[2,12,48,1024]{3,2,1,0:T(8,128)(2,1)}, u32[]{:S(2)}, u32[]{:S(2)}) collective-permute-start(bf16[2,12,48,1024]{3,2,1,0:T(8,128)(2,1)} %add_convert_fusion), channel_id=1, source_target_pairs={{1,0},{2,1},{3,2},{4,3},{5,4},{6,5},{7,6},{8,7},{9,8},{10,9},{11,1... | collective-permute-start | bytes 7077896 | tf_op jit(solution)/shard_map/ppermute | solution.py:34
  945.4 25.9 %slice-start.18 = ((s8[7864320]{0:T(1024)(128)(4,1)}), s8[4194304]{0:T(1024)(128)(4,1)S(1)}, s32[]{:S(2)}) async-start(s8[7864320]{0:T(1024)(128)(4,1)} %bitcast.667), calls=%async_computation.18 | async-start | bytes 8388608
  949.9 21.4 %slice-start.19 = ((s8[7864320]{0:T(1024)(128)(4,1)}), s8[3670016]{0:T(1024)(128)(4,1)S(1)}, s32[]{:S(2)}) async-start(s8[7864320]{0:T(1024)(128)(4,1)} %bitcast.667), calls=%async_computation.19 | async-start | bytes 7340032
  963.0 26.7 %collective-permute-start.11 = (bf16[2,2,48,1024]{3,2,1,0:T(8,128)(2,1)S(1)}, bf16[2,2,48,1024]{3,2,1,0:T(8,128)(2,1)}, u32[]{:S(2)}, u32[]{:S(2)}) collective-permute-start(bf16[2,2,48,1024]{3,2,1,0:T(8,128)(2,1)S(1)} %get-tuple-element.354), channel_id=1, source_target_pairs={{16,0},{32,16},{48,32},{64,48},{80,64},{96,80},{112,96},{17,1},{33... | collective-permute-start | bytes 1179656 | tf_op jit(solution)/shard_map/ppermute | solution.py:40
  964.3 24.0 %collective-permute-start.10 = (bf16[2,2,48,1024]{3,2,1,0:T(8,128)(2,1)}, bf16[2,2,48,1024]{3,2,1,0:T(8,128)(2,1)}, u32[]{:S(2)}, u32[]{:S(2)}) collective-permute-start(bf16[2,2,48,1024]{3,2,1,0:T(8,128)(2,1)} %get-tuple-element.355), channel_id=1, source_target_pairs={{0,16},{16,32},{32,48},{48,64},{64,80},{80,96},{96,112},{1,17},{17... | collective-permute-start | bytes 1179656 | tf_op jit(solution)/shard_map/ppermute | solution.py:40
  (53 other events, 333.4 us)
where the time goes:
time: 1010 us; the launch traced here: 993 us
  local copies, waits for them, and re-layouts  629 us (62%)
  matrix products  196 us (19%)
  other arithmetic  124 us (12%)
  starting transfers between devices  28 us (3%)
  waiting for transfers between devices  14.3 us (1%)
    another operation x15, local copies, waits for them, and re-layouts, block_grads(): jnp.stack([grad_key.reshape(row_count, key_count, feature_width), grad_va...  178 us
    another operation x10, local copies, waits for them, and re-layouts, attend_block(): value_heads = kv_slab[1].reshape(row_count, key_count, HEADS, HEAD_DIM)  104 us
    transpose x5, local copies, waits for them, and re-layouts, block_grads(): jnp.einsum('hrqk,rqhd->rkhd', probs.astype(jnp.bfloat16), cot_heads, pref...  70.5 us
    mul x5, local copies, waits for them, and re-layouts, block_grads(): jnp.einsum('hrqk,rqhd->rkhd', score_grads, query_heads, preferred_element...  69.6 us
    unnamed x170, local copies, waits for them, and re-layouts  64.2 us
    scatter-add x20, other arithmetic, from_slab(): result = result.at[:, w:w + row_count].add(shaped[:, :, w])  58.6 us
    another operation x5, local copies, waits for them, and re-layouts, attend_block(): key_heads = kv_slab[0].reshape(row_count, key_count, HEADS, HEAD_DIM)  56.2 us
    dot_general x5, matrix products, attend_block(): jnp.einsum('rqhd,rkhd->hrqk', query_heads, key_heads, preferred_element_t...  55.9 us
  transfers between devices with their start and end apart: 12, of which 3 were waited for; matrix products, arithmetic and copies ran while one was open for 51% of the time, Pallas kernels for 0%

commit v1 on v0

v1 whole, which is shorter than its diff:
```python
import jax
import jax.numpy as jnp
from jax import lax
from jax.experimental import pallas as pl
from jax.experimental.pallas import tpu as pltpu
from jax.sharding import PartitionSpec as P

HEADS = 16
HEAD_DIM = 64
HALO = 2
REACH = 96
QBLOCK = 128
FAR = -1e30
VMEM_BYTES = 56 * 1024 * 1024
NT = (((1,), (1,)), ((), ()))


def vmem():
    return pl.BlockSpec(memory_space=pltpu.VMEM)


def smem():
    return pl.BlockSpec(memory_space=pltpu.SMEM)


def pack_pair(left, right):
    rows, cols, width = left.shape
    heads = width // HEAD_DIM

    def body(left_ref, right_ref, out_ref):
        for h in range(heads):
            at = slice(h * HEAD_DIM, (h + 1) * HEAD_DIM)
            out_ref[h, 0] = jnp.concatenate([left_ref[0, :, at], right_ref[0, :, at]], axis=-1)

    block = pl.BlockSpec((1, cols, width), lambda r: (r, 0, 0))
    return pl.pallas_call(
        body,
        grid=(rows,),
        in_specs=[block, block],
        out_specs=pl.BlockSpec((heads, 1, cols, 2 * HEAD_DIM), lambda r: (0, r, 0, 0)),
        out_shape=jax.ShapeDtypeStruct((heads, rows, cols, 2 * HEAD_DIM), left.dtype),
    )(left, right)


def unpack_pair(packed):
    heads, rows, cols, _ = packed.shape
    width = heads * HEAD_DIM

    def body(in_ref, left_ref, right_ref):
        for h in range(heads):
            at = slice(h * HEAD_DIM, (h + 1) * HEAD_DIM)
            left_ref[0, :, at] = in_ref[h, 0, :, :HEAD_DIM]
            right_ref[0, :, at] = in_ref[h, 0, :, HEAD_DIM:]

    block = pl.BlockSpec((1, cols, width), lambda r: (r, 0, 0))
    shape = jax.ShapeDtypeStruct((rows, cols, width), packed.dtype)
    return pl.pallas_call(
        body,
        grid=(rows,),
        in_specs=[pl.BlockSpec((heads, 1, cols, 2 * HEAD_DIM), lambda r: (0, r, 0, 0))],
        out_specs=[block, block],
        out_shape=[shape, shape],
    )(packed)


def attend(reach, log_weight, kv, kv_above, kv_below, qc):
    sectors, rows, cols, lanes = kv.shape
    ring = sectors * cols
    ext_rows = rows + 2 * HALO
    taps = 2 * HALO + 1
    padded = ring + 2 * REACH
    window = QBLOCK + 2 * REACH
    blocks = ring // QBLOCK
    scale = float(HEAD_DIM) ** -0.5

    def body(reach_ref, logw_ref, kv_ref, above_ref, below_ref, qc_ref,
             qo_ref, mid_ref, edge_ref, up_ref, down_ref,
             kvw, kvt, qcw, dkv, sd, bias, qow):
        for s in range(sectors):
            at = slice(REACH + s * cols, REACH + (s + 1) * cols)
            kvw[0:HALO, at] = above_ref[s]
            kvw[HALO:HALO + rows, at] = kv_ref[s]
            kvw[HALO + rows:ext_rows, at] = below_ref[s]
            qcw[:, s * cols:(s + 1) * cols] = qc_ref[s]
        kvw[:, 0:REACH] = kvw[:, ring:ring + REACH]
        kvw[:, REACH + ring:padded] = kvw[:, REACH:2 * REACH]

        @pl.loop(0, ext_rows)
        def _(kr):
            kvt[kr] = kvw[kr].T
            dkv[kr] = jnp.zeros((padded, lanes), jnp.float32)

        lane = lax.broadcasted_iota(jnp.int32, (QBLOCK, lanes), 1)

        @pl.loop(0, rows)
        def _(r):
            gap = (lax.broadcasted_iota(jnp.int32, (window, QBLOCK), 0) - REACH
                   - lax.broadcasted_iota(jnp.int32, (window, QBLOCK), 1))
            near = jnp.abs(gap) <= reach_ref[r]
            for w in range(taps):
                bias[w] = jnp.where(near, logw_ref[r + w], FAR)

            @pl.loop(0, blocks)
            def _(b):
                start = pl.multiple_of(b * QBLOCK, QBLOCK)
                span = pl.ds(start, window)
                rows_qc = qcw[r, pl.ds(start, QBLOCK), :]
                zero = jnp.zeros_like(rows_qc)
                qb = jnp.concatenate(
                    [jnp.where(lane < HEAD_DIM, rows_qc * scale, zero),
                     jnp.where(lane < HEAD_DIM, zero, rows_qc)], axis=0)
                top = jnp.full((8, QBLOCK), FAR, jnp.float32)
                for w in range(taps):
                    both = lax.dot_general(kvw[r + w, span, :], qb, NT,
                                           preferred_element_type=jnp.float32)
                    score = both[:, :QBLOCK] + bias[w]
                    sd[w, :, :QBLOCK] = score
                    sd[w, :, QBLOCK:] = both[:, QBLOCK:]
                    top = jnp.maximum(top, jnp.max(score.reshape(window // 8, 8, QBLOCK), axis=0))
                top = jnp.max(top, axis=0, keepdims=True)
                total = jnp.zeros((8, QBLOCK), jnp.float32)
                dot = jnp.zeros((8, QBLOCK), jnp.float32)
                for w in range(taps):
                    p = jnp.exp(sd[w, :, :QBLOCK] - top)
                    sd[w, :, :QBLOCK] = p
                    total += jnp.sum(p.reshape(window // 8, 8, QBLOCK), axis=0)
                    dot += jnp.sum((p * sd[w, :, QBLOCK:]).reshape(window // 8, 8, QBLOCK), axis=0)
                inverse = 1.0 / jnp.sum(total, axis=0, keepdims=True)
                delta = jnp.sum(dot, axis=0, keepdims=True) * inverse
                dq = jnp.zeros((HEAD_DIM, QBLOCK), jnp.float32)
                out = jnp.zeros((HEAD_DIM, QBLOCK), jnp.float32)
                for w in range(taps):
                    prob = sd[w, :, :QBLOCK] * inverse
                    ds = (prob * (sd[w, :, QBLOCK:] - delta)).astype(jnp.bfloat16)
                    pb = prob.astype(jnp.bfloat16)
                    dq += jnp.dot(kvt[r + w, :HEAD_DIM, span], ds, preferred_element_type=jnp.float32)
                    out += jnp.dot(kvt[r + w, HEAD_DIM:, span], pb, preferred_element_type=jnp.float32)
                    dkv[r + w, span, :] += jnp.dot(jnp.concatenate([ds, pb], axis=1), qb,
                                                   preferred_element_type=jnp.float32)
                qo = jnp.concatenate([dq * scale, out], axis=0)
                qow[r, pl.ds(start, QBLOCK), :] = qo.T.astype(jnp.bfloat16)

        dkv[:, ring:ring + REACH] += dkv[:, 0:REACH]
        dkv[:, REACH:2 * REACH] += dkv[:, REACH + ring:padded]
        for s in range(sectors):
            at = slice(REACH + s * cols, REACH + (s + 1) * cols)
            qo_ref[s] = qow[:, s * cols:(s + 1) * cols]
            up_ref[s] = dkv[0:HALO, at].astype(jnp.bfloat16)
            edge_ref[s, :HALO] = dkv[HALO:2 * HALO, at].astype(jnp.bfloat16)
            mid_ref[s] = dkv[2 * HALO:rows, at].astype(jnp.bfloat16)
            edge_ref[s, HALO:] = dkv[rows:rows + HALO, at].astype(jnp.bfloat16)
            down_ref[s] = dkv[rows + HALO:ext_rows, at].astype(jnp.bfloat16)

    def out(count):
        return jax.ShapeDtypeStruct((sectors, count, cols, lanes), jnp.bfloat16)

    return pl.pallas_call(
        body,
        in_specs=[smem(), smem(), vmem(), vmem(), vmem(), vmem()],
        out_specs=[vmem()] * 5,
        out_shape=[out(rows), out(rows - 2 * HALO), out(2 * HALO), out(HALO), out(HALO)],
        scratch_shapes=[
            pltpu.VMEM((ext_rows, padded, lanes), jnp.bfloat16),
            pltpu.VMEM((ext_rows, lanes, padded), jnp.bfloat16),
            pltpu.VMEM((rows, ring, lanes), jnp.bfloat16),
            pltpu.VMEM((ext_rows, padded, lanes), jnp.float32),
            pltpu.VMEM((taps, window, 2 * QBLOCK), jnp.float32),
            pltpu.VMEM((taps, window, QBLOCK), jnp.float32),
            pltpu.VMEM((rows, ring, lanes), jnp.bfloat16),
        ],
        compiler_params=pltpu.CompilerParams(vmem_limit_bytes=VMEM_BYTES),
    )(reach, log_weight, kv, kv_above, kv_below, qc)


def exchange(packed):
    return lax.all_to_all(packed, "lon", 0, 0)


def to_next_band(block, step):
    bands = lax.axis_size("lat")
    return lax.ppermute(block, "lat", [(i, i + step) for i in range(bands) if 0 <= i + step < bands])


def on_device(queries, key_vectors, value_vectors, cotangent, quad_weight, lon_reach):
    rows = queries.shape[0]
    ext = lax.axis_index("lat") * rows + jnp.arange(rows + 2 * HALO, dtype=jnp.int32) - HALO
    inside = (ext >= 0) & (ext < quad_weight.shape[0])
    log_weight = jnp.where(inside, jnp.log(quad_weight[jnp.clip(ext, 0, quad_weight.shape[0] - 1)]), FAR)

    kv = exchange(pack_pair(key_vectors, value_vectors))
    qc = exchange(pack_pair(queries, cotangent))
    above = to_next_band(kv[:, rows - HALO:], 1)
    below = to_next_band(kv[:, :HALO], -1)
    qo, mid, edge, up, down = attend(lon_reach, log_weight, kv, above, below, qc)
    from_below = to_next_band(up, -1)
    from_above = to_next_band(down, 1)
    grad_queries, attended = unpack_pair(exchange(qo))
    mid = exchange(mid)
    home = jnp.concatenate([from_above, from_below], axis=1).astype(jnp.float32)
    edge = exchange((edge.astype(jnp.float32) + home).astype(jnp.bfloat16))
    whole = jnp.concatenate([edge[:, :HALO], mid, edge[:, HALO:]], axis=1)
    grad_keys, grad_values = unpack_pair(whole)
    return attended, grad_queries, grad_keys, grad_values


def solution(mesh):
    cells = P("lat", "lon", None)
    return jax.shard_map(
        on_device,
        mesh=mesh,
        in_specs=(cells, cells, cells, cells, P(), P("lat")),
        out_specs=(cells, cells, cells, cells),
        check_vma=False,
    )
```

time: 1010 us -> 234 us (0.23); the launches traced: 993 us -> 231 us
  local copies, waits for them, and re-layouts: 629 us -> 4.21 us
  matrix products: 196 us -> 0 us
  other arithmetic: 124 us -> 2.1 us
  Pallas kernels: 0 us -> 94.8 us
  waiting for transfers between devices: 14.3 us -> 75.8 us
  blocking collectives: 0 us -> 17.2 us
    another operation x37 -> x0, local copies, waits for them, and re-layouts: 347 us -> none  [the longest x15 178 us: block_grads(): jnp.stack([grad_key.reshape(row_count, key_count, feature_width), grad_va...]
    dot_general x30 -> x0, matrix products: 196 us -> none  [the longest x5 55.9 us: attend_block(): jnp.einsum('rqhd,rkhd->hrqk', query_heads, key_heads, preferred_element_t...]
    pallas_call x0 -> x5, Pallas kernels: none -> 94.8 us  [the longest x1 71.1 us: attend(): pl.pallas_call(body, in_specs=[smem(), smem(), vmem(), vmem(), vmem(), vm...]
    transpose x5 -> x0, local copies, waits for them, and re-layouts: 70.5 us -> none  [block_grads(): jnp.einsum('hrqk,rqhd->rkhd', probs.astype(jnp.bfloat16), cot_heads, pref...]
    mul x6 -> x0, local copies, waits for them, and re-layouts: 69.7 us -> none  [the longest x5 69.6 us: block_grads(): jnp.einsum('hrqk,rqhd->rkhd', score_grads, query_heads, preferred_element...]
    unnamed x170 -> x18, local copies, waits for them, and re-layouts: 64.2 us -> 2.68 us
    scatter-add x22 -> x0, other arithmetic: 61.1 us -> none  [the longest x20 58.6 us: from_slab(): result = result.at[:, w:w + row_count].add(shaped[:, :, w])]
    slice x17 -> x2, local copies, waits for them, and re-layouts: 46.2 us -> 0.87 us  [the longest x1 0.82 us: on_device(): below = to_next_band(kv[:, :HALO], -1)]
  transfers between devices with their start and end apart: 12 -> 8, of which waited for: 3 -> 6; matrix products, arithmetic and copies ran while one was open for 51% -> 2% of each run, Pallas kernels for 0% -> 5%
where the time goes in v1:
time: 234 us; the launch traced here: 231 us
  Pallas kernels  94.8 us (41%)
  waiting for transfers between devices  75.8 us (32%)
  starting transfers between devices  36.1 us (15%)
  blocking collectives  17.2 us (7%)
  local copies, waits for them, and re-layouts  4.21 us (2%)
    pallas_call x1, Pallas kernels, attend(): pl.pallas_call(body, in_specs=[smem(), smem(), vmem(), vmem(), vmem(), vm...  71.1 us
    all_to_all x4, waiting for transfers between devices, exchange(): return lax.all_to_all(packed, 'lon', 0, 0)  43.7 us
    ppermute x4, waiting for transfers between devices, to_next_band(): lax.ppermute(block, 'lat', [(i, i + step) for i in range(bands) if 0 <= i...  32.1 us
    all_to_all x4, starting transfers between devices, exchange(): return lax.all_to_all(packed, 'lon', 0, 0)  18.1 us
    ppermute x4, starting transfers between devices, to_next_band(): lax.ppermute(block, 'lat', [(i, i + step) for i in range(bands) if 0 <= i...  18 us
    all_to_all x1, blocking collectives, exchange(): return lax.all_to_all(packed, 'lon', 0, 0)  17.2 us
    pallas_call x2, Pallas kernels, pack_pair(): pl.pallas_call(body, grid=(rows,), in_specs=[block, block], out_specs=pl....  11.8 us
    pallas_call x2, Pallas kernels, unpack_pair(): pl.pallas_call(body, grid=(rows,), in_specs=[pl.BlockSpec((heads, 1, cols...  11.8 us
  transfers between devices with their start and end apart: 8, of which 6 were waited for; matrix products, arithmetic and copies ran while one was open for 2% of the time, Pallas kernels for 5%

profile of v1, /device:TPU:0, one launch (start us, length us, event | category | flops | bytes accessed | tf_op | source)
XLA Modules:
  0.0 231.0 jit_solution(7753494992166311390)
XLA Ops:
  0.6 0.0 copy-start
  0.6 5.9 %shard_map.93 = bf16[16,8,48,128]{3,2,1,0:T(8,128)(2,1)} custom-call(bf16[8,48,1024]{2,1,0:T(8,128)(2,1)} %left_ref.2, bf16[8,48,1024]{2,1,0:T(8,128)(2,1)} %right_ref.2), custom_call_target="tpu_custom_call" | custom-call | tf_op jit(solution)/shard_map/pallas_call | solution.py:36
  6.6 5.5 %all-to-all-start = ((bf16[16,8,48,128]{3,2,1,0:T(8,128)(2,1)}), bf16[16,8,48,128]{3,2,1,0:T(8,128)(2,1)S(1)}, u32[]{:S(2)}, u32[]{:S(2)}) async-start(bf16[16,8,48,128]{3,2,1,0:T(8,128)(2,1)} %shard_map.93), calls=%async_computation | async-start | bytes 3145728 | tf_op jit(solution)/shard_map/all_to_all | solution.py:176
  12.1 5.9 %shard_map.94 = bf16[16,8,48,128]{3,2,1,0:T(8,128)(2,1)} custom-call(bf16[8,48,1024]{2,1,0:T(8,128)(2,1)} %left_ref.3, bf16[8,48,1024]{2,1,0:T(8,128)(2,1)} %right_ref.3), custom_call_target="tpu_custom_call" | custom-call | tf_op jit(solution)/shard_map/pallas_call | solution.py:36
  18.0 16.2 %all-to-all-done.kv_ref = bf16[16,8,48,128]{3,2,1,0:T(8,128)(2,1)S(1)} async-done(((bf16[16,8,48,128]{3,2,1,0:T(8,128)(2,1)}), bf16[16,8,48,128]{3,2,1,0:T(8,128)(2,1)S(1)}, u32[]{:S(2)}, u32[]{:S(2)}) %all-to-all-start) | async-done | bytes 1572896 | tf_op jit(solution)/shard_map/all_to_all | solution.py:176
  34.2 3.7 %all-to-all-start.1 = ((bf16[16,8,48,128]{3,2,1,0:T(8,128)(2,1)}), bf16[16,8,48,128]{3,2,1,0:T(8,128)(2,1)S(1)}, u32[]{:S(2)}, u32[]{:S(2)}) async-start(bf16[16,8,48,128]{3,2,1,0:T(8,128)(2,1)} %shard_map.94), calls=%async_computation.1 | async-start | bytes 3145728 | tf_op jit(solution)/shard_map/all_to_all | solution.py:176
  37.9 0.8 fusion.1
  38.7 1.3 collective-permute-start.1
  40.0 6.1 %collective-permute-start = (bf16[16,2,48,128]{3,2,1,0:T(8,128)(2,1)S(1)}, bf16[16,2,48,128]{3,2,1,0:T(8,128)(2,1)S(1)}, u32[]{:S(2)}, u32[]{:S(2)}) collective-permute-start(bf16[16,2,48,128]{3,2,1,0:T(8,128)(2,1)S(1)} %get-tuple-element.23), channel_id=1, source_target_pairs={{0,16},{16,32},{32,48},{48,64},{64,80},{80,96},{96,112},{1,17},{17... | collective-permute-start | bytes 1179656 | tf_op jit(solution)/shard_map/ppermute | solution.py:181
  46.1 0.7 gather_fusion
  46.8 0.5 and_select_fusion.logw_ref
  47.3 12.7 %all-to-all-done.1.qc_ref = bf16[16,8,48,128]{3,2,1,0:T(8,128)(2,1)S(1)} async-done(((bf16[16,8,48,128]{3,2,1,0:T(8,128)(2,1)}), bf16[16,8,48,128]{3,2,1,0:T(8,128)(2,1)S(1)}, u32[]{:S(2)}, u32[]{:S(2)}) %all-to-all-start.1) | async-done | bytes 1572896 | tf_op jit(solution)/shard_map/all_to_all | solution.py:176
  60.1 7.7 %collective-permute-done.1.below_ref = bf16[16,2,48,128]{3,2,1,0:T(8,128)(2,1)S(1)} collective-permute-done((bf16[16,2,48,128]{3,2,1,0:T(8,128)(2,1)}, bf16[16,2,48,128]{3,2,1,0:T(8,128)(2,1)S(1)}, u32[]{:S(2)}, u32[]{:S(2)}) %collective-permute-start.1) | collective-permute-done | bytes 393248 | tf_op jit(solution)/shard_map/ppermute | solution.py:181
  67.7 0.0 collective-permute-done.above_ref
  67.7 0.7 copy-done.5
  68.5 0.7 copy-done.6
  69.2 71.1 %shard_map.95 = (bf16[16,8,48,128]{3,2,1,0:T(8,128)(2,1)}, bf16[16,4,48,128]{3,2,1,0:T(8,128)(2,1)}, bf16[16,4,48,128]{3,2,1,0:T(8,128)(2,1)}, bf16[16,2,48,128]{3,2,1,0:T(8,128)(2,1)}, bf16[16,2,48,128]{3,2,1,0:T(8,128)(2,1)}) custom-call(s32[8]{0:T(128)} %reach_ref.1, f32[12]{0:T(128)} %and_select_fusion.logw_ref, bf16[16,8,48,128]{3,2,1,0:T(8,128)(2,1)} %copy-done.1, ...), custom_call_target="tpu_custom_call" | custom-call | tf_op jit(solution)/shard_map/pallas_call | solution.py:157
  140.4 5.2 %all-to-all-start.4 = ((bf16[16,4,48,128]{3,2,1,0:T(8,128)(2,1)}), bf16[16,4,48,128]{3,2,1,0:T(8,128)(2,1)S(1)}, u32[]{:S(2)}, u32[]{:S(2)}) async-start(bf16[16,4,48,128]{3,2,1,0:T(8,128)(2,1)} %get-tuple-element.19), calls=%async_computation.4 | async-start | bytes 1572864 | tf_op jit(solution)/shard_map/all_to_all | solution.py:176
  145.5 9.4 %collective-permute-start.2 = (bf16[16,2,48,128]{3,2,1,0:T(8,128)(2,1)S(1)}, bf16[16,2,48,128]{3,2,1,0:T(8,128)(2,1)S(1)}, u32[]{:S(2)}, u32[]{:S(2)}) collective-permute-start(bf16[16,2,48,128]{3,2,1,0:T(8,128)(2,1)S(1)} %copy-done.8), channel_id=1, source_target_pairs={{0,16},{16,32},{32,48},{48,64},{64,80},{80,96},{96,112},{1,17},{17... | collective-permute-start | bytes 1179656 | tf_op jit(solution)/shard_map/ppermute | solution.py:181
  154.9 1.3 collective-permute-start.3
  156.2 8.5 %collective-permute-done.2 = bf16[16,2,48,128]{3,2,1,0:T(8,128)(2,1)S(1)} collective-permute-done((bf16[16,2,48,128]{3,2,1,0:T(8,128)(2,1)S(1)}, bf16[16,2,48,128]{3,2,1,0:T(8,128)(2,1)S(1)}, u32[]{:S(2)}, u32[]{:S(2)}) %collective-permute-start.2) | collective-permute-done | bytes 393248 | tf_op jit(solution)/shard_map/ppermute | solution.py:181
  164.7 16.0 %collective-permute-done.3 = bf16[16,2,48,128]{3,2,1,0:T(8,128)(2,1)S(1)} collective-permute-done((bf16[16,2,48,128]{3,2,1,0:T(8,128)(2,1)S(1)}, bf16[16,2,48,128]{3,2,1,0:T(8,128)(2,1)S(1)}, u32[]{:S(2)}, u32[]{:S(2)}) %collective-permute-start.3) | collective-permute-done | bytes 393248 | tf_op jit(solution)/shard_map/ppermute | solution.py:181
  180.7 0.2 add_convert_fusion
  180.9 0.0 all-to-all-done.4
  180.9 17.2 %all_to_all.25 = bf16[16,4,48,128]{3,2,1,0:T(8,128)(2,1)S(1)} all-to-all(bf16[16,4,48,128]{3,2,1,0:T(8,128)(2,1)S(1)} %add_convert_fusion), channel_id=1, replica_groups=mesh['lat'=8,'lon'=16] {'lon'}, dimensions={0} | all-to-all | bytes 1572864 | tf_op jit(solution)/shard_map/all_to_all | solution.py:176
  198.1 3.7 %all-to-all-start.2 = ((bf16[16,8,48,128]{3,2,1,0:T(8,128)(2,1)}), bf16[16,8,48,128]{3,2,1,0:T(8,128)(2,1)S(1)}, u32[]{:S(2)}, u32[]{:S(2)}) async-start(bf16[16,8,48,128]{3,2,1,0:T(8,128)(2,1)} %get-tuple-element.13), calls=%async_computation.2 | async-start | bytes 3145728 | tf_op jit(solution)/shard_map/all_to_all | solution.py:176
  201.8 0.1 fusion.2
  201.9 1.3 pad_maximum_fusion.in_ref
  203.2 5.9 %shard_map.97 = (bf16[8,48,1024]{2,1,0:T(8,128)(2,1)}, bf16[8,48,1024]{2,1,0:T(8,128)(2,1)}) custom-call(bf16[16,8,48,128]{3,2,1,0:T(8,128)(2,1)} %pad_maximum_fusion.in_ref), custom_call_target="tpu_custom_call" | custom-call | tf_op jit(solution)/shard_map/pallas_call | solution.py:57
  209.1 14.8 %all-to-all-done.2.in_ref = bf16[16,8,48,128]{3,2,1,0:T(8,128)(2,1)S(1)} async-done(((bf16[16,8,48,128]{3,2,1,0:T(8,128)(2,1)}), bf16[16,8,48,128]{3,2,1,0:T(8,128)(2,1)S(1)}, u32[]{:S(2)}, u32[]{:S(2)}) %all-to-all-start.2) | async-done | bytes 1572896 | tf_op jit(solution)/shard_map/all_to_all | solution.py:176
  223.9 1.2 copy-done.3
  225.0 5.9 %shard_map.96 = (bf16[8,48,1024]{2,1,0:T(8,128)(2,1)}, bf16[8,48,1024]{2,1,0:T(8,128)(2,1)}) custom-call(bf16[16,8,48,128]{3,2,1,0:T(8,128)(2,1)} %copy-done.3), custom_call_target="tpu_custom_call" | custom-call | tf_op jit(solution)/shard_map/pallas_call | solution.py:57
  (16 shorter events, 0.0 us)
Async XLA Ops:
  0.6 45.5 %copy-start = (f32[64]{0:T(128)S(1)}, f32[64]{0:T(128)}, u32[]{:S(2)}) copy-start(f32[64]{0:T(128)} %param.10) | copy-start | bytes 772
  6.6 27.6 %all-to-all-start = ((bf16[16,8,48,128]{3,2,1,0:T(8,128)(2,1)}), bf16[16,8,48,128]{3,2,1,0:T(8,128)(2,1)S(1)}, u32[]{:S(2)}, u32[]{:S(2)}) async-start(bf16[16,8,48,128]{3,2,1,0:T(8,128)(2,1)} %shard_map.93), calls=%async_computation | async-start | bytes 3145728 | tf_op jit(solution)/shard_map/all_to_all | solution.py:176
  34.2 3.7 %copy-start.1 = (bf16[16,8,48,128]{3,2,1,0:T(8,128)(2,1)}, bf16[16,8,48,128]{3,2,1,0:T(8,128)(2,1)S(1)}, u32[]{:S(2)}) copy-start(bf16[16,8,48,128]{3,2,1,0:T(8,128)(2,1)S(1)} %all-to-all-done.kv_ref) | copy-start | bytes 4718596
  34.2 25.9 %all-to-all-start.1 = ((bf16[16,8,48,128]{3,2,1,0:T(8,128)(2,1)}), bf16[16,8,48,128]{3,2,1,0:T(8,128)(2,1)S(1)}, u32[]{:S(2)}, u32[]{:S(2)}) async-start(bf16[16,8,48,128]{3,2,1,0:T(8,128)(2,1)} %shard_map.94), calls=%async_computation.1 | async-start | bytes 3145728 | tf_op jit(solution)/shard_map/all_to_all | solution.py:176
  38.7 29.0 %collective-permute-start.1 = (bf16[16,2,48,128]{3,2,1,0:T(8,128)(2,1)}, bf16[16,2,48,128]{3,2,1,0:T(8,128)(2,1)S(1)}, u32[]{:S(2)}, u32[]{:S(2)}) collective-permute-start(bf16[16,2,48,128]{3,2,1,0:T(8,128)(2,1)} %get-tuple-element.22), channel_id=1, source_target_pairs={{16,0},{32,16},{48,32},{64,48},{80,64},{96,80},{112,96},{17,1},{33... | collective-permute-start | bytes 1179656 | tf_op jit(solution)/shard_map/ppermute | solution.py:181
  40.0 27.7 %collective-permute-start = (bf16[16,2,48,128]{3,2,1,0:T(8,128)(2,1)S(1)}, bf16[16,2,48,128]{3,2,1,0:T(8,128)(2,1)S(1)}, u32[]{:S(2)}, u32[]{:S(2)}) collective-permute-start(bf16[16,2,48,128]{3,2,1,0:T(8,128)(2,1)S(1)} %get-tuple-element.23), channel_id=1, source_target_pairs={{0,16},{16,32},{32,48},{48,64},{64,80},{80,96},{96,112},{1,17},{17... | collective-permute-start | bytes 1179656 | tf_op jit(solution)/shard_map/ppermute | solution.py:181
  60.0 7.7 %copy-start.2 = (bf16[16,8,48,128]{3,2,1,0:T(8,128)(2,1)}, bf16[16,8,48,128]{3,2,1,0:T(8,128)(2,1)S(1)}, u32[]{:S(2)}) copy-start(bf16[16,8,48,128]{3,2,1,0:T(8,128)(2,1)S(1)} %all-to-all-done.1.qc_ref) | copy-start | bytes 4718596
  67.7 0.7 copy-start.5
  68.5 0.7 copy-start.6
  140.3 5.2 %copy-start.8 = (bf16[16,2,48,128]{3,2,1,0:T(8,128)(2,1)S(1)}, bf16[16,2,48,128]{3,2,1,0:T(8,128)(2,1)}, u32[]{:S(2)}) copy-start(bf16[16,2,48,128]{3,2,1,0:T(8,128)(2,1)} %get-tuple-element.17) | copy-start | bytes 1179652
  140.3 14.6 %copy-start.7 = (bf16[16,2,48,128]{3,2,1,0:T(8,128)(2,1)S(1)}, bf16[16,2,48,128]{3,2,1,0:T(8,128)(2,1)}, u32[]{:S(2)}) copy-start(bf16[16,2,48,128]{3,2,1,0:T(8,128)(2,1)} %get-tuple-element.18) | copy-start | bytes 1179652
  140.3 40.3 %copy-start.4 = (bf16[16,4,48,128]{3,2,1,0:T(8,128)(2,1)S(1)}, bf16[16,4,48,128]{3,2,1,0:T(8,128)(2,1)}, u32[]{:S(2)}) copy-start(bf16[16,4,48,128]{3,2,1,0:T(8,128)(2,1)} %get-tuple-element.16) | copy-start | bytes 2359300
  140.4 40.6 %all-to-all-start.4 = ((bf16[16,4,48,128]{3,2,1,0:T(8,128)(2,1)}), bf16[16,4,48,128]{3,2,1,0:T(8,128)(2,1)S(1)}, u32[]{:S(2)}, u32[]{:S(2)}) async-start(bf16[16,4,48,128]{3,2,1,0:T(8,128)(2,1)} %get-tuple-element.19), calls=%async_computation.4 | async-start | bytes 1572864 | tf_op jit(solution)/shard_map/all_to_all | solution.py:176
  145.5 19.2 %collective-permute-start.2 = (bf16[16,2,48,128]{3,2,1,0:T(8,128)(2,1)S(1)}, bf16[16,2,48,128]{3,2,1,0:T(8,128)(2,1)S(1)}, u32[]{:S(2)}, u32[]{:S(2)}) collective-permute-start(bf16[16,2,48,128]{3,2,1,0:T(8,128)(2,1)S(1)} %copy-done.8), channel_id=1, source_target_pairs={{0,16},{16,32},{32,48},{48,64},{64,80},{80,96},{96,112},{1,17},{17... | collective-permute-start | bytes 1179656 | tf_op jit(solution)/shard_map/ppermute | solution.py:181
  154.9 25.8 %collective-permute-start.3 = (bf16[16,2,48,128]{3,2,1,0:T(8,128)(2,1)S(1)}, bf16[16,2,48,128]{3,2,1,0:T(8,128)(2,1)S(1)}, u32[]{:S(2)}, u32[]{:S(2)}) collective-permute-start(bf16[16,2,48,128]{3,2,1,0:T(8,128)(2,1)S(1)} %copy-done.7), channel_id=1, source_target_pairs={{16,0},{32,16},{48,32},{64,48},{80,64},{96,80},{112,96},{17,1},{33... | collective-permute-start | bytes 1179656 | tf_op jit(solution)/shard_map/ppermute | solution.py:181
  198.1 25.8 %all-to-all-start.2 = ((bf16[16,8,48,128]{3,2,1,0:T(8,128)(2,1)}), bf16[16,8,48,128]{3,2,1,0:T(8,128)(2,1)S(1)}, u32[]{:S(2)}, u32[]{:S(2)}) async-start(bf16[16,8,48,128]{3,2,1,0:T(8,128)(2,1)} %get-tuple-element.13), calls=%async_computation.2 | async-start | bytes 3145728 | tf_op jit(solution)/shard_map/all_to_all | solution.py:176
  223.9 1.2 copy-start.3

commit v2 on v1

v2 whole, which is shorter than its diff:
```python
import jax
import jax.numpy as jnp
from jax import lax
from jax.experimental import pallas as pl
from jax.experimental.pallas import tpu as pltpu
from jax.sharding import PartitionSpec as P

HEADS = 16
HEAD_DIM = 64
HALO = 2
REACH = 96
HALF = 64
TAPS = 2 * HALO + 2
WINDOW = HALF + 2 * REACH
INTERLEAVE = 4
FAR = -1e30
VMEM_BYTES = 56 * 1024 * 1024
NT = (((1,), (1,)), ((), ()))


def vmem():
    return pl.BlockSpec(memory_space=pltpu.VMEM)


def smem():
    return pl.BlockSpec(memory_space=pltpu.SMEM)


def pack_pair(left, right, row_block, step):
    _, cols, width = left.shape
    heads = width // HEAD_DIM

    def body(left_ref, right_ref, out_ref):
        for i in range(step):
            for h in range(heads):
                at = slice(h * HEAD_DIM, (h + 1) * HEAD_DIM)
                out_ref[h, i] = jnp.concatenate([left_ref[i, :, at], right_ref[i, :, at]], axis=-1)

    count = len(row_block)

    def source(i):
        row = jnp.int32(row_block[0])
        for n in range(1, count):
            row = jnp.where(i == n, row_block[n], row)
        return (row, 0, 0)

    block = pl.BlockSpec((step, cols, width), source)
    return pl.pallas_call(
        body,
        grid=(count,),
        in_specs=[block, block],
        out_specs=pl.BlockSpec((heads, step, cols, 2 * HEAD_DIM), lambda i: (0, i, 0, 0)),
        out_shape=jax.ShapeDtypeStruct((heads, count * step, cols, 2 * HEAD_DIM), left.dtype),
    )(left, right)


def split_heads(in_ref, left_ref, right_ref):
    heads, step = in_ref.shape[:2]
    for i in range(step):
        for pair in range(heads // 2):
            first, second = in_ref[2 * pair, i], in_ref[2 * pair + 1, i]
            at = slice(pair * 2 * HEAD_DIM, (pair + 1) * 2 * HEAD_DIM)
            left_ref[i, :, at] = jnp.concatenate([first[:, :HEAD_DIM], second[:, :HEAD_DIM]], axis=1)
            right_ref[i, :, at] = jnp.concatenate([first[:, HEAD_DIM:], second[:, HEAD_DIM:]], axis=1)


def unpack_edge(packed, rows):
    heads, _, cols, lanes = packed.shape
    width = heads * HEAD_DIM
    out = pl.BlockSpec((HALO, cols, width), lambda i: (i * (rows // HALO - 1), 0, 0))
    shape = jax.ShapeDtypeStruct((rows, cols, width), packed.dtype)
    return pl.pallas_call(
        split_heads,
        grid=(2,),
        in_specs=[pl.BlockSpec((heads, HALO, cols, lanes), lambda i: (0, i, 0, 0))],
        out_specs=[out, out],
        out_shape=[shape, shape],
    )(packed)


def unpack_rest(packed, grad_queries, attended):
    heads, _, cols, lanes = packed.shape
    rows, _, width = attended.shape
    half = (rows - 2 * HALO) // HALO

    def body(in_ref, _, __, dq_ref, out_ref, dk_ref, dv_ref):
        step = pl.program_id(0)

        @pl.when(step < half)
        def _():
            split_heads(in_ref, dq_ref, out_ref)

        @pl.when(step >= half)
        def _():
            split_heads(in_ref, dk_ref, dv_ref)

    def query_row(i):
        return (jnp.minimum(i, half - 1) + 1, 0, 0)

    def key_row(i):
        mid = jnp.maximum(i, half) - half + 1
        return (jnp.where(i < 2 * half, mid, jnp.where(i == 2 * half, 0, half + 1)), 0, 0)

    shape = jax.ShapeDtypeStruct((rows, cols, width), packed.dtype)
    query_block = pl.BlockSpec((HALO, cols, width), query_row)
    key_block = pl.BlockSpec((HALO, cols, width), key_row)
    held = pl.BlockSpec(memory_space=pl.ANY)
    return pl.pallas_call(
        body,
        grid=(2 * half + 2,),
        in_specs=[pl.BlockSpec((heads, HALO, cols, lanes), lambda i: (0, i, 0, 0)), held, held],
        out_specs=[query_block, query_block, key_block, key_block],
        out_shape=[shape] * 4,
        input_output_aliases={1: 0, 2: 1},
    )(packed, grad_queries, attended)


def two_pairs(reach_ref, logw_ref, kvw, kvt, qcw, dkv, sd, bias, qow, key_stride, own_first, own_stride, ext_first):
    lanes = kvw.shape[-1]
    blocks = qcw.shape[1] // HALF
    both = 2 * HALF
    scale = float(HEAD_DIM) ** -0.5
    lane = lax.broadcasted_iota(jnp.int32, (both, lanes), 1)

    @pl.loop(0, 2)
    def _(pair):
        base = pair * key_stride
        own = own_first + pair * own_stride
        r = 2 * pair
        key = lax.broadcasted_iota(jnp.int32, (WINDOW, both), 0) - REACH
        query = lax.broadcasted_iota(jnp.int32, (WINDOW, both), 1)
        second = query >= HALF
        gap = jnp.abs(key - jnp.where(second, query - HALF, query))
        near = gap <= jnp.where(second, reach_ref[own + 1], reach_ref[own])
        for w in range(TAPS):
            ok = near
            if w == 0:
                ok = near & jnp.logical_not(second)
            if w == TAPS - 1:
                ok = near & second
            bias[w] = jnp.where(ok, logw_ref[ext_first + base + w], FAR)

        @pl.loop(0, blocks // INTERLEAVE)
        def _(group):
            held = []
            for j in range(INTERLEAVE):
                block = group * INTERLEAVE + j
                start = pl.multiple_of(block * HALF, HALF)
                span = pl.ds(start, WINDOW)
                turned = pl.ds(pl.multiple_of(start - (j % 2) * HALF, both), WINDOW)
                rows_qc = jnp.concatenate(
                    [qcw[r, pl.ds(start, HALF), :], qcw[r + 1, pl.ds(start, HALF), :]], axis=0)
                zero = jnp.zeros_like(rows_qc)
                qb = jnp.concatenate(
                    [jnp.where(lane < HEAD_DIM, rows_qc * scale, zero),
                     jnp.where(lane < HEAD_DIM, zero, rows_qc)], axis=0)
                held.append((start, span, turned, qb))
            tops = []
            for j in range(INTERLEAVE):
                _, span, _, qb = held[j]
                top = jnp.full((8, both), FAR, jnp.float32)
                for w in range(TAPS):
                    product = lax.dot_general(kvw[base + w, span, :], qb, NT,
                                              preferred_element_type=jnp.float32)
                    score = product[:, :both] + bias[w]
                    sd[j, w, :, :both] = score
                    sd[j, w, :, both:] = product[:, both:]
                    top = jnp.maximum(top, jnp.max(score.reshape(WINDOW // 8, 8, both), axis=0))
                tops.append(jnp.max(top, axis=0, keepdims=True))
            sums = []
            for j in range(INTERLEAVE):
                total = jnp.zeros((8, both), jnp.float32)
                dot = jnp.zeros((8, both), jnp.float32)
                for w in range(TAPS):
                    p = jnp.exp(sd[j, w, :, :both] - tops[j])
                    sd[j, w, :, :both] = p
                    total += jnp.sum(p.reshape(WINDOW // 8, 8, both), axis=0)
                    dot += jnp.sum((p * sd[j, w, :, both:]).reshape(WINDOW // 8, 8, both), axis=0)
                inverse = 1.0 / jnp.sum(total, axis=0, keepdims=True)
                sums.append((inverse, jnp.sum(dot, axis=0, keepdims=True) * inverse))
            for j in range(INTERLEAVE):
                start, span, turned, qb = held[j]
                inverse, delta = sums[j]
                acc = jnp.zeros((lanes, 2 * both), jnp.float32)
                for w in range(TAPS):
                    prob = sd[j, w, :, :both] * inverse
                    ds = (prob * (sd[j, w, :, both:] - delta)).astype(jnp.bfloat16)
                    dp = jnp.concatenate([ds, prob.astype(jnp.bfloat16)], axis=1)
                    acc += jnp.dot(kvt[j % 2, base + w, :, turned], dp, preferred_element_type=jnp.float32)
                    dkv[base + w, span, :] += jnp.dot(dp, qb, preferred_element_type=jnp.float32)
                qo = jnp.concatenate([acc[:HEAD_DIM, :both] * scale, acc[HEAD_DIM:, both:]], axis=0)
                qo = qo.T.astype(jnp.bfloat16)
                qow[r, pl.ds(start, HALF), :] = qo[:HALF]
                qow[r + 1, pl.ds(start, HALF), :] = qo[HALF:]


def wrap_and_turn(kvw, kvt):
    key_rows, padded, _ = kvw.shape
    ring = padded - 2 * REACH
    kvw[:, 0:REACH] = kvw[:, ring:ring + REACH]
    kvw[:, REACH + ring:padded] = kvw[:, REACH:2 * REACH]

    @pl.loop(0, key_rows)
    def _(kr):
        kvt[0, kr] = kvw[kr].T
        kvt[1, kr, :, 0:padded - HALF] = kvw[kr, HALF:].T


def fold(dkv):
    padded = dkv.shape[1]
    ring = padded - 2 * REACH
    dkv[:, ring:ring + REACH] += dkv[:, 0:REACH]
    dkv[:, REACH:2 * REACH] += dkv[:, REACH + ring:padded]


def scratch(key_rows, ring, lanes):
    padded = ring + 2 * REACH
    return [
        pltpu.VMEM((key_rows, padded, lanes), jnp.bfloat16),
        pltpu.VMEM((2, key_rows, lanes, padded), jnp.bfloat16),
        pltpu.VMEM((4, ring, lanes), jnp.bfloat16),
        pltpu.VMEM((key_rows, padded, lanes), jnp.float32),
        pltpu.VMEM((INTERLEAVE, TAPS, WINDOW, 4 * HALF), jnp.float32),
        pltpu.VMEM((TAPS, WINDOW, 2 * HALF), jnp.float32),
        pltpu.VMEM((4, ring, lanes), jnp.bfloat16),
    ]


def params():
    return pltpu.CompilerParams(vmem_limit_bytes=VMEM_BYTES)


def cost():
    return pl.CostEstimate(flops=20_000_000_000, bytes_accessed=8_000_000, transcendentals=5_000_000)


def attend_edge(reach, log_weight, kv, kv_above, kv_below, qc):
    sectors, rows, cols, lanes = kv.shape
    ring = sectors * cols
    ext_rows = rows + 2 * HALO

    def body(reach_ref, logw_ref, kv_ref, above_ref, below_ref, qc_ref, qo_ref, up_ref, down_ref, part_ref,
             kvw, kvt, qcw, dkv, sd, bias, qow):
        for s in range(sectors):
            at = slice(REACH + s * cols, REACH + (s + 1) * cols)
            kvw[0:HALO, at] = above_ref[s]
            kvw[HALO:HALO + rows, at] = kv_ref[s]
            kvw[HALO + rows:ext_rows, at] = below_ref[s]
            qcw[:, s * cols:(s + 1) * cols] = qc_ref[s]
        wrap_and_turn(kvw, kvt)

        @pl.loop(0, ext_rows)
        def _(kr):
            dkv[kr] = jnp.zeros(dkv.shape[1:], jnp.float32)

        two_pairs(reach_ref, logw_ref, kvw, kvt, qcw, dkv, sd, bias, qow,
                  rows - HALO, 0, rows - HALO, 0)
        fold(dkv)
        part_ref[...] = dkv[HALO:HALO + rows, REACH:REACH + ring]
        for s in range(sectors):
            at = slice(REACH + s * cols, REACH + (s + 1) * cols)
            qo_ref[s] = qow[:, s * cols:(s + 1) * cols]
            up_ref[s] = dkv[0:HALO, at].astype(jnp.bfloat16)
            down_ref[s] = dkv[rows + HALO:ext_rows, at].astype(jnp.bfloat16)

    def out(count):
        return jax.ShapeDtypeStruct((sectors, count, cols, lanes), jnp.bfloat16)

    return pl.pallas_call(
        body,
        in_specs=[smem(), smem(), vmem(), vmem(), vmem(), vmem()],
        out_specs=[vmem()] * 4,
        out_shape=[out(4), out(HALO), out(HALO), jax.ShapeDtypeStruct((rows, ring, lanes), jnp.float32)],
        scratch_shapes=scratch(ext_rows, ring, lanes),
        compiler_params=params(),
        cost_estimate=cost(),
    )(reach, log_weight, kv, kv_above, kv_below, qc)


def attend_mid(reach, log_weight, kv, qc, part):
    sectors, rows, cols, lanes = kv.shape
    ring = sectors * cols
    padded = ring + 2 * REACH

    def body(reach_ref, logw_ref, kv_ref, qc_ref, part_ref, out_ref, kvw, kvt, qcw, dkv, sd, bias, qow):
        for s in range(sectors):
            at = slice(REACH + s * cols, REACH + (s + 1) * cols)
            kvw[:, at] = kv_ref[s]
            qcw[:, s * cols:(s + 1) * cols] = qc_ref[s]
        wrap_and_turn(kvw, kvt)

        @pl.loop(0, rows)
        def _(kr):
            dkv[kr, 0:REACH] = jnp.zeros((REACH, lanes), jnp.float32)
            dkv[kr, REACH:REACH + ring] = part_ref[kr]
            dkv[kr, REACH + ring:padded] = jnp.zeros((REACH, lanes), jnp.float32)

        two_pairs(reach_ref, logw_ref, kvw, kvt, qcw, dkv, sd, bias, qow, HALO, HALO, HALO, HALO)
        fold(dkv)
        for s in range(sectors):
            at = slice(REACH + s * cols, REACH + (s + 1) * cols)
            out_ref[s, 0:4] = qow[:, s * cols:(s + 1) * cols]
            out_ref[s, 4:8] = dkv[HALO:rows - HALO, at].astype(jnp.bfloat16)
            out_ref[s, 8:10] = dkv[0:HALO, at].astype(jnp.bfloat16)
            out_ref[s, 10:12] = dkv[rows - HALO:rows, at].astype(jnp.bfloat16)

    return pl.pallas_call(
        body,
        in_specs=[smem(), smem(), vmem(), vmem(), vmem()],
        out_specs=vmem(),
        out_shape=jax.ShapeDtypeStruct((sectors, 12, cols, lanes), jnp.bfloat16),
        scratch_shapes=scratch(rows, ring, lanes),
        compiler_params=params(),
        cost_estimate=cost(),
    )(reach, log_weight, kv, qc, part)


def exchange(packed):
    return lax.all_to_all(packed, "lon", 0, 0)


def to_next_band(block, step):
    bands = lax.axis_size("lat")
    return lax.ppermute(block, "lat", [(i, i + step) for i in range(bands) if 0 <= i + step < bands])


def on_device(queries, key_vectors, value_vectors, cotangent, quad_weight, lon_reach):
    rows = queries.shape[0]
    ext = lax.axis_index("lat") * rows + jnp.arange(rows + 2 * HALO, dtype=jnp.int32) - HALO
    inside = (ext >= 0) & (ext < quad_weight.shape[0])
    log_weight = jnp.where(inside, jnp.log(quad_weight[jnp.clip(ext, 0, quad_weight.shape[0] - 1)]), FAR)

    kv = exchange(pack_pair(key_vectors, value_vectors, (0, 1), rows // 2))
    qc_edge = exchange(pack_pair(queries, cotangent, (0, rows // HALO - 1), HALO))
    above = to_next_band(kv[:, rows - HALO:], 1)
    below = to_next_band(kv[:, :HALO], -1)
    qc_mid = exchange(pack_pair(queries, cotangent, (1, 2), HALO))
    qo_edge, up, down, part = attend_edge(lon_reach, log_weight, kv, above, below, qc_edge)
    from_below = to_next_band(up, -1)
    from_above = to_next_band(down, 1)
    grad_queries, attended = unpack_edge(exchange(qo_edge), rows)
    rest = attend_mid(lon_reach, log_weight, kv, qc_mid, part)
    home = jnp.concatenate([from_above, from_below], axis=1).astype(jnp.float32)
    edge = (rest[:, 8:].astype(jnp.float32) + home).astype(jnp.bfloat16)
    rest = exchange(lax.dynamic_update_slice(rest, edge, (0, 8, 0, 0)))
    grad_queries, attended, grad_keys, grad_values = unpack_rest(rest, grad_queries, attended)
    return attended, grad_queries, grad_keys, grad_values


def solution(mesh):
    cells = P("lat", "lon", None)
    return jax.shard_map(
        on_device,
        mesh=mesh,
        in_specs=(cells, cells, cells, cells, P(), P("lat")),
        out_specs=(cells, cells, cells, cells),
        check_vma=False,
    )
```

time: 234 us -> 189 us (0.81)
  the two profiles are of different devices: /device:TPU:0 before, /device:TPU:99 now
where the time goes in v2:
time: 189 us; the launch traced here: 188 us
  Pallas kernels  69.7 us (37%)
  waiting for transfers between devices  67.7 us (36%)
  starting transfers between devices  43.5 us (23%)
  local copies, waits for them, and re-layouts  3.8 us (2%)
  other arithmetic  2.92 us (2%)
    all_to_all x5, waiting for transfers between devices, exchange(): return lax.all_to_all(packed, 'lon', 0, 0)  49.9 us
    all_to_all x5, starting transfers between devices, exchange(): return lax.all_to_all(packed, 'lon', 0, 0)  29 us
    pallas_call x1, Pallas kernels, attend_edge(): pl.pallas_call(body, in_specs=[smem(), smem(), vmem(), vmem(), vmem(), vm...  28.1 us
    pallas_call x1, Pallas kernels, attend_mid(): pl.pallas_call(body, in_specs=[smem(), smem(), vmem(), vmem(), vmem()], o...  27.2 us
    ppermute x4, waiting for transfers between devices, to_next_band(): lax.ppermute(block, 'lat', [(i, i + step) for i in range(bands) if 0 <= i...  17.8 us
    ppermute x4, starting transfers between devices, to_next_band(): lax.ppermute(block, 'lat', [(i, i + step) for i in range(bands) if 0 <= i...  14.5 us
    pallas_call x3, Pallas kernels, pack_pair(): pl.pallas_call(body, grid=(count,), in_specs=[block, block], out_specs=pl...  6.94 us
    pallas_call x1, Pallas kernels, unpack_rest(): pl.pallas_call(body, grid=(2 * half + 2,), in_specs=[pl.BlockSpec((heads,...  5.35 us
  transfers between devices with their start and end apart: 9, of which 5 were waited for; matrix products, arithmetic and copies ran while one was open for 2% of the time, Pallas kernels for 33%

profile of v2, /device:TPU:99, one launch (start us, length us, event | category | flops | bytes accessed | tf_op | source)
XLA Modules:
  0.0 188.3 jit_solution(6466095896849547036)
XLA Ops:
  0.6 0.0 copy-start
  0.6 2.6 %shard_map.93 = bf16[16,8,48,128]{3,2,1,0:T(8,128)(2,1)} custom-call(bf16[8,48,1024]{2,1,0:T(8,128)(2,1)} %left_ref.3, bf16[8,48,1024]{2,1,0:T(8,128)(2,1)} %right_ref.3), custom_call_target="tpu_custom_call" | custom-call | tf_op jit(solution)/shard_map/pallas_call | solution.py:48
  3.3 6.2 %all-to-all-start = ((bf16[16,8,48,128]{3,2,1,0:T(8,128)(2,1)}), bf16[16,8,48,128]{3,2,1,0:T(8,128)(2,1)S(1)}, u32[]{:S(2)}, u32[]{:S(2)}) async-start(bf16[16,8,48,128]{3,2,1,0:T(8,128)(2,1)} %shard_map.93), calls=%async_computation | async-start | bytes 3145728 | tf_op jit(solution)/shard_map/all_to_all | solution.py:319
  9.4 2.2 %shard_map.95 = bf16[16,4,48,128]{3,2,1,0:T(8,128)(2,1)} custom-call(bf16[8,48,1024]{2,1,0:T(8,128)(2,1)} %left_ref.5, bf16[8,48,1024]{2,1,0:T(8,128)(2,1)} %right_ref.5), custom_call_target="tpu_custom_call" | custom-call | tf_op jit(solution)/shard_map/pallas_call | solution.py:48
  11.6 19.0 %all-to-all-done.kv_ref = bf16[16,8,48,128]{3,2,1,0:T(8,128)(2,1)S(1)} async-done(((bf16[16,8,48,128]{3,2,1,0:T(8,128)(2,1)}), bf16[16,8,48,128]{3,2,1,0:T(8,128)(2,1)S(1)}, u32[]{:S(2)}, u32[]{:S(2)}) %all-to-all-start) | async-done | bytes 1572896 | tf_op jit(solution)/shard_map/all_to_all | solution.py:319
  30.6 4.5 %all-to-all-start.2 = ((bf16[16,4,48,128]{3,2,1,0:T(8,128)(2,1)}), bf16[16,4,48,128]{3,2,1,0:T(8,128)(2,1)S(1)}, u32[]{:S(2)}, u32[]{:S(2)}) async-start(bf16[16,4,48,128]{3,2,1,0:T(8,128)(2,1)} %shard_map.95), calls=%async_computation.2 | async-start | bytes 1572864 | tf_op jit(solution)/shard_map/all_to_all | solution.py:319
  35.1 2.2 %shard_map.94 = bf16[16,4,48,128]{3,2,1,0:T(8,128)(2,1)} custom-call(bf16[8,48,1024]{2,1,0:T(8,128)(2,1)} %left_ref.5, bf16[8,48,1024]{2,1,0:T(8,128)(2,1)} %right_ref.5), custom_call_target="tpu_custom_call" | custom-call | tf_op jit(solution)/shard_map/pallas_call | solution.py:48
  37.2 0.1 fusion.2
  37.3 4.4 %collective-permute-start.1 = (bf16[16,2,48,128]{3,2,1,0:T(8,128)(2,1)S(1)}, bf16[16,2,48,128]{3,2,1,0:T(8,128)(2,1)S(1)}, u32[]{:S(2)}, u32[]{:S(2)}) collective-permute-start(bf16[16,2,48,128]{3,2,1,0:T(8,128)(2,1)S(1)} %get-tuple-element.24), channel_id=1, source_target_pairs={{16,0},{32,16},{48,32},{64,48},{80,64},{96,80},{112,96},{17,1},{33... | collective-permute-start | bytes 1179656 | tf_op jit(solution)/shard_map/ppermute | solution.py:324
  41.7 2.4 %collective-permute-start = (bf16[16,2,48,128]{3,2,1,0:T(8,128)(2,1)S(1)}, bf16[16,2,48,128]{3,2,1,0:T(8,128)(2,1)S(1)}, u32[]{:S(2)}, u32[]{:S(2)}) collective-permute-start(bf16[16,2,48,128]{3,2,1,0:T(8,128)(2,1)S(1)} %get-tuple-element.25), channel_id=1, source_target_pairs={{0,16},{16,32},{32,48},{48,64},{64,80},{80,96},{96,112},{1,17},{17... | collective-permute-start | bytes 1179656 | tf_op jit(solution)/shard_map/ppermute | solution.py:324
  44.1 0.7 gather_fusion
  44.8 0.6 and_select_fusion.logw_ref
  45.4 0.9 all-to-all-done.2.qc_ref
  46.3 6.0 %all-to-all-start.1 = ((bf16[16,4,48,128]{3,2,1,0:T(8,128)(2,1)}), bf16[16,4,48,128]{3,2,1,0:T(8,128)(2,1)S(1)}, u32[]{:S(2)}, u32[]{:S(2)}) async-start(bf16[16,4,48,128]{3,2,1,0:T(8,128)(2,1)} %shard_map.94), calls=%async_computation.1 | async-start | bytes 1572864 | tf_op jit(solution)/shard_map/all_to_all | solution.py:319
  52.3 3.2 %collective-permute-done.1.below_ref = bf16[16,2,48,128]{3,2,1,0:T(8,128)(2,1)S(1)} collective-permute-done((bf16[16,2,48,128]{3,2,1,0:T(8,128)(2,1)S(1)}, bf16[16,2,48,128]{3,2,1,0:T(8,128)(2,1)S(1)}, u32[]{:S(2)}, u32[]{:S(2)}) %collective-permute-start.1) | collective-permute-done | bytes 393248 | tf_op jit(solution)/shard_map/ppermute | solution.py:324
  55.5 14.6 %collective-permute-done.above_ref = bf16[16,2,48,128]{3,2,1,0:T(8,128)(2,1)S(1)} collective-permute-done((bf16[16,2,48,128]{3,2,1,0:T(8,128)(2,1)S(1)}, bf16[16,2,48,128]{3,2,1,0:T(8,128)(2,1)S(1)}, u32[]{:S(2)}, u32[]{:S(2)}) %collective-permute-start) | collective-permute-done | bytes 393248 | tf_op jit(solution)/shard_map/ppermute | solution.py:324
  70.1 0.7 copy-done.7
  70.8 28.1 %shard_map.96 = (bf16[16,4,48,128]{3,2,1,0:T(8,128)(2,1)}, bf16[16,2,48,128]{3,2,1,0:T(8,128)(2,1)}, bf16[16,2,48,128]{3,2,1,0:T(8,128)(2,1)}, f32[8,768,128]{2,1,0:T(8,128)}) custom-call(s32[8]{0:T(128)} %reach_ref.3, f32[12]{0:T(128)} %and_select_fusion.logw_ref, bf16[16,8,48,128]{3,2,1,0:T(8,128)(2,1)} %copy-done.2, bf16[16,2,48,128]{3,2,1,0:T(8,128)(2,1)} %copy-done.7, ...), custom_call_target="tpu_custom_call" | custom-call | flops 20000000000 | bytes 8000000 | tf_op jit(solution)/shard_map/pallas_call | solution.py:269
  98.9 2.4 %collective-permute-start.2 = (bf16[16,2,48,128]{3,2,1,0:T(8,128)(2,1)}, bf16[16,2,48,128]{3,2,1,0:T(8,128)(2,1)S(1)}, u32[]{:S(2)}, u32[]{:S(2)}) collective-permute-start(bf16[16,2,48,128]{3,2,1,0:T(8,128)(2,1)} %get-tuple-element.15), channel_id=1, source_target_pairs={{0,16},{16,32},{32,48},{48,64},{64,80},{80,96},{96,112},{1,17},{17... | collective-permute-start | bytes 1179656 | tf_op jit(solution)/shard_map/ppermute | solution.py:324
  101.3 5.3 %collective-permute-start.3 = (bf16[16,2,48,128]{3,2,1,0:T(8,128)(2,1)}, bf16[16,2,48,128]{3,2,1,0:T(8,128)(2,1)S(1)}, u32[]{:S(2)}, u32[]{:S(2)}) collective-permute-start(bf16[16,2,48,128]{3,2,1,0:T(8,128)(2,1)} %get-tuple-element.16), channel_id=1, source_target_pairs={{16,0},{32,16},{48,32},{64,48},{80,64},{96,80},{112,96},{17,1},{33... | collective-permute-start | bytes 1179656 | tf_op jit(solution)/shard_map/ppermute | solution.py:324
  106.6 0.0 all-to-all-done.1.qc_ref
  106.6 0.0 copy-start.5
  106.6 6.7 %all-to-all-start.4 = ((bf16[16,4,48,128]{3,2,1,0:T(8,128)(2,1)}), bf16[16,4,48,128]{3,2,1,0:T(8,128)(2,1)S(1)}, u32[]{:S(2)}, u32[]{:S(2)}) async-start(bf16[16,4,48,128]{3,2,1,0:T(8,128)(2,1)} %get-tuple-element.17), calls=%async_computation.4 | async-start | bytes 1572864 | tf_op jit(solution)/shard_map/all_to_all | solution.py:319
  113.3 27.2 %shard_map.97 = bf16[16,12,48,128]{3,2,1,0:T(8,128)(2,1)} custom-call(s32[8]{0:T(128)} %reach_ref.3, f32[12]{0:T(128)} %and_select_fusion.logw_ref, bf16[16,8,48,128]{3,2,1,0:T(8,128)(2,1)} %copy-done.2, bf16[16,4,48,128]{3,2,1,0:T(8,128)(2,1)} %copy-done.5, f32[8,768,128]{2,1,0:T(8,128)} %get-tuple-element.14.part_ref), custom_call_target="tpu_custom_call" | custom-call | flops 20000000000 | bytes 8000000 | tf_op jit(solution)/shard_map/pallas_call | solution.py:307
  140.5 0.0 collective-permute-done.2
  140.5 2.3 %fusion = bf16[16,12,48,128]{3,2,1,0:T(8,128)(2,1)} fusion(bf16[16,12,48,128]{3,2,1,0:T(8,128)(2,1)} %shard_map.97, bf16[16,2,48,128]{3,2,1,0:T(8,128)(2,1)S(1)} %collective-permute-done.3, bf16[16,2,48,128]{3,2,1,0:T(8,128)(2,1)S(1)} %collective-permute-done.2), kind=kLoop, calls=%fused_computation.2 | loop fusion | flops 2752512 | bytes 2359296 | tf_op jit(solution)/shard_map/dynamic_update_slice | solution.py:345
  142.8 0.9 copy-done.3
  143.7 5.7 %all-to-all-start.3 = ((bf16[16,12,48,128]{3,2,1,0:T(8,128)(2,1)}), bf16[16,12,48,128]{3,2,1,0:T(8,128)(2,1)S(1)}, u32[]{:S(2)}, u32[]{:S(2)}) async-start(bf16[16,12,48,128]{3,2,1,0:T(8,128)(2,1)} %fusion), calls=%async_computation.3 | async-start | bytes 4718592 | tf_op jit(solution)/shard_map/all_to_all | solution.py:319
  149.4 2.1 %shard_map.98 = (bf16[8,48,1024]{2,1,0:T(8,128)(2,1)}, bf16[8,48,1024]{2,1,0:T(8,128)(2,1)}) custom-call(bf16[16,4,48,128]{3,2,1,0:T(8,128)(2,1)} %copy-done.3), custom_call_target="tpu_custom_call" | custom-call | tf_op jit(solution)/shard_map/pallas_call | solution.py:72
  151.5 30.0 %all-to-all-done.3.in_ref = bf16[16,12,48,128]{3,2,1,0:T(8,128)(2,1)S(1)} async-done(((bf16[16,12,48,128]{3,2,1,0:T(8,128)(2,1)}), bf16[16,12,48,128]{3,2,1,0:T(8,128)(2,1)S(1)}, u32[]{:S(2)}, u32[]{:S(2)}) %all-to-all-start.3) | async-done | bytes 2359328 | tf_op jit(solution)/shard_map/all_to_all | solution.py:319
  181.5 1.4 copy-done.1
  182.9 5.4 %shard_map.99 = (bf16[8,48,1024]{2,1,0:T(8,128)(2,1)}, bf16[8,48,1024]{2,1,0:T(8,128)(2,1)}, bf16[8,48,1024]{2,1,0:T(8,128)(2,1)}, bf16[8,48,1024]{2,1,0:T(8,128)(2,1)}) custom-call(bf16[16,12,48,128]{3,2,1,0:T(8,128)(2,1)} %copy-done.1, bf16[8,48,1024]{2,1,0:T(8,128)(2,1)} %get-tuple-element.18._, ...), custom_call_target="tpu_custom_call", output_to_operand_aliasing={{0}: (1, {}), {1}: (2, {})} | custom-call | tf_op jit(solution)/shard_map/pallas_call | solution.py:108
  (15 shorter events, 0.0 us)
Async XLA Ops:
  0.6 43.5 %copy-start = (f32[64]{0:T(128)S(1)}, f32[64]{0:T(128)}, u32[]{:S(2)}) copy-start(f32[64]{0:T(128)} %param.10) | copy-start | bytes 772
  3.3 27.3 %all-to-all-start = ((bf16[16,8,48,128]{3,2,1,0:T(8,128)(2,1)}), bf16[16,8,48,128]{3,2,1,0:T(8,128)(2,1)S(1)}, u32[]{:S(2)}, u32[]{:S(2)}) async-start(bf16[16,8,48,128]{3,2,1,0:T(8,128)(2,1)} %shard_map.93), calls=%async_computation | async-start | bytes 3145728 | tf_op jit(solution)/shard_map/all_to_all | solution.py:319
  30.6 6.6 %copy-start.2 = (bf16[16,8,48,128]{3,2,1,0:T(8,128)(2,1)}, bf16[16,8,48,128]{3,2,1,0:T(8,128)(2,1)S(1)}, u32[]{:S(2)}) copy-start(bf16[16,8,48,128]{3,2,1,0:T(8,128)(2,1)S(1)} %all-to-all-done.kv_ref) | copy-start | bytes 4718596
  30.6 15.7 %all-to-all-start.2 = ((bf16[16,4,48,128]{3,2,1,0:T(8,128)(2,1)}), bf16[16,4,48,128]{3,2,1,0:T(8,128)(2,1)S(1)}, u32[]{:S(2)}, u32[]{:S(2)}) async-start(bf16[16,4,48,128]{3,2,1,0:T(8,128)(2,1)} %shard_map.95), calls=%async_computation.2 | async-start | bytes 1572864 | tf_op jit(solution)/shard_map/all_to_all | solution.py:319
  37.3 18.2 %collective-permute-start.1 = (bf16[16,2,48,128]{3,2,1,0:T(8,128)(2,1)S(1)}, bf16[16,2,48,128]{3,2,1,0:T(8,128)(2,1)S(1)}, u32[]{:S(2)}, u32[]{:S(2)}) collective-permute-start(bf16[16,2,48,128]{3,2,1,0:T(8,128)(2,1)S(1)} %get-tuple-element.24), channel_id=1, source_target_pairs={{16,0},{32,16},{48,32},{64,48},{80,64},{96,80},{112,96},{17,1},{33... | collective-permute-start | bytes 1179656 | tf_op jit(solution)/shard_map/ppermute | solution.py:324
  41.7 28.4 %collective-permute-start = (bf16[16,2,48,128]{3,2,1,0:T(8,128)(2,1)S(1)}, bf16[16,2,48,128]{3,2,1,0:T(8,128)(2,1)S(1)}, u32[]{:S(2)}, u32[]{:S(2)}) collective-permute-start(bf16[16,2,48,128]{3,2,1,0:T(8,128)(2,1)S(1)} %get-tuple-element.25), channel_id=1, source_target_pairs={{0,16},{16,32},{32,48},{48,64},{64,80},{80,96},{96,112},{1,17},{17... | collective-permute-start | bytes 1179656 | tf_op jit(solution)/shard_map/ppermute | solution.py:324
  46.3 23.8 %copy-start.4 = (bf16[16,4,48,128]{3,2,1,0:T(8,128)(2,1)}, bf16[16,4,48,128]{3,2,1,0:T(8,128)(2,1)S(1)}, u32[]{:S(2)}) copy-start(bf16[16,4,48,128]{3,2,1,0:T(8,128)(2,1)S(1)} %all-to-all-done.2.qc_ref) | copy-start | bytes 2359300
  46.3 60.3 %all-to-all-start.1 = ((bf16[16,4,48,128]{3,2,1,0:T(8,128)(2,1)}), bf16[16,4,48,128]{3,2,1,0:T(8,128)(2,1)S(1)}, u32[]{:S(2)}, u32[]{:S(2)}) async-start(bf16[16,4,48,128]{3,2,1,0:T(8,128)(2,1)} %shard_map.94), calls=%async_computation.1 | async-start | bytes 1572864 | tf_op jit(solution)/shard_map/all_to_all | solution.py:319
  55.5 14.6 %copy-start.6 = (bf16[16,2,48,128]{3,2,1,0:T(8,128)(2,1)}, bf16[16,2,48,128]{3,2,1,0:T(8,128)(2,1)S(1)}, u32[]{:S(2)}) copy-start(bf16[16,2,48,128]{3,2,1,0:T(8,128)(2,1)S(1)} %collective-permute-done.1.below_ref) | copy-start | bytes 1179652
  70.1 0.7 copy-start.7
  98.9 41.6 %collective-permute-start.2 = (bf16[16,2,48,128]{3,2,1,0:T(8,128)(2,1)}, bf16[16,2,48,128]{3,2,1,0:T(8,128)(2,1)S(1)}, u32[]{:S(2)}, u32[]{:S(2)}) collective-permute-start(bf16[16,2,48,128]{3,2,1,0:T(8,128)(2,1)} %get-tuple-element.15), channel_id=1, source_target_pairs={{0,16},{16,32},{32,48},{48,64},{64,80},{80,96},{96,112},{1,17},{17... | collective-permute-start | bytes 1179656 | tf_op jit(solution)/shard_map/ppermute | solution.py:324
  101.3 39.2 %collective-permute-start.3 = (bf16[16,2,48,128]{3,2,1,0:T(8,128)(2,1)}, bf16[16,2,48,128]{3,2,1,0:T(8,128)(2,1)S(1)}, u32[]{:S(2)}, u32[]{:S(2)}) collective-permute-start(bf16[16,2,48,128]{3,2,1,0:T(8,128)(2,1)} %get-tuple-element.16), channel_id=1, source_target_pairs={{16,0},{32,16},{48,32},{64,48},{80,64},{96,80},{112,96},{17,1},{33... | collective-permute-start | bytes 1179656 | tf_op jit(solution)/shard_map/ppermute | solution.py:324
  106.6 6.7 %copy-start.5 = (bf16[16,4,48,128]{3,2,1,0:T(8,128)(2,1)}, bf16[16,4,48,128]{3,2,1,0:T(8,128)(2,1)S(1)}, u32[]{:S(2)}) copy-start(bf16[16,4,48,128]{3,2,1,0:T(8,128)(2,1)S(1)} %all-to-all-done.1.qc_ref) | copy-start | bytes 2359300
  106.6 36.2 %all-to-all-start.4 = ((bf16[16,4,48,128]{3,2,1,0:T(8,128)(2,1)}), bf16[16,4,48,128]{3,2,1,0:T(8,128)(2,1)S(1)}, u32[]{:S(2)}, u32[]{:S(2)}) async-start(bf16[16,4,48,128]{3,2,1,0:T(8,128)(2,1)} %get-tuple-element.17), calls=%async_computation.4 | async-start | bytes 1572864 | tf_op jit(solution)/shard_map/all_to_all | solution.py:319
  142.8 0.9 copy-start.3
  143.7 37.8 %all-to-all-start.3 = ((bf16[16,12,48,128]{3,2,1,0:T(8,128)(2,1)}), bf16[16,12,48,128]{3,2,1,0:T(8,128)(2,1)S(1)}, u32[]{:S(2)}, u32[]{:S(2)}) async-start(bf16[16,12,48,128]{3,2,1,0:T(8,128)(2,1)} %fusion), calls=%async_computation.3 | async-start | bytes 4718592 | tf_op jit(solution)/shard_map/all_to_all | solution.py:319
  181.5 1.4 copy-start.1

commit v3 on v2

--- a/solution.py
+++ b/solution.py
@@ -13,6 +13,7 @@
 TAPS = 2 * HALO + 2
 WINDOW = HALF + 2 * REACH
 INTERLEAVE = 4
+CLASSES = (48, 64, 80, 96)
 FAR = -1e30
 VMEM_BYTES = 56 * 1024 * 1024
 NT = (((1,), (1,)), ((), ()))
@@ -115,12 +116,72 @@
     )(packed, grad_queries, attended)
 
 
-def two_pairs(reach_ref, logw_ref, kvw, kvt, qcw, dkv, sd, bias, qow, key_stride, own_first, own_stride, ext_first):
+def block_group(group, r, base, reach_class, w_first, w_last, kvw, kvt, qcw, dkv, sd, bias, qow):
     lanes = kvw.shape[-1]
-    blocks = qcw.shape[1] // HALF
     both = 2 * HALF
     scale = float(HEAD_DIM) ** -0.5
     lane = lax.broadcasted_iota(jnp.int32, (both, lanes), 1)
+    off = REACH - reach_class
+    width = HALF + 2 * reach_class
+    taps = range(w_first, w_last)
+    held = []
+    for j in range(INTERLEAVE):
+        block = group * INTERLEAVE + j
+        start = pl.multiple_of(block * HALF, HALF)
+        span = pl.ds(pl.multiple_of(start + off, 16), width)
+        turned = pl.ds(pl.multiple_of(start - (j % 2) * HALF, both), WINDOW)
+        rows_qc = jnp.concatenate(
+            [qcw[r, pl.ds(start, HALF), :], qcw[r + 1, pl.ds(start, HALF), :]], axis=0)
+        zero = jnp.zeros_like(rows_qc)
+        qb = jnp.concatenate(
+            [jnp.where(lane < HEAD_DIM, rows_qc * scale, zero),
+             jnp.where(lane < HEAD_DIM, zero, rows_qc)], axis=0)
+        held.append((start, span, turned, qb))
+    tops = []
+    for j in range(INTERLEAVE):
+        _, span, _, qb = held[j]
+        top = jnp.full((8, both), FAR, jnp.float32)
+        for w in taps:
+            product = lax.dot_general(kvw[base + w, span, :], qb, NT, preferred_element_type=jnp.float32)
+            score = product[:, :both] + bias[w, off:off + width]
+            sd[j, w, :width, :both] = score
+            sd[j, w, :width, both:] = product[:, both:]
+            top = jnp.maximum(top, jnp.max(score.reshape(width // 8, 8, both), axis=0))
+        tops.append(jnp.max(top, axis=0, keepdims=True))
+    sums = []
+    for j in range(INTERLEAVE):
+        total = jnp.zeros((8, both), jnp.float32)
+        dot = jnp.zeros((8, both), jnp.float32)
+        for w in taps:
+            p = jnp.exp(sd[j, w, :width, :both] - tops[j])
+            sd[j, w, :width, :both] = p
+            total += jnp.sum(p.reshape(width // 8, 8, both), axis=0)
+            dot += jnp.sum((p * sd[j, w, :width, both:]).reshape(width // 8, 8, both), axis=0)
+        inverse = 1.0 / jnp.sum(total, axis=0, keepdims=True)
+        sums.append((inverse, jnp.sum(dot, axis=0, keepdims=True) * inverse))
+    edge = jnp.zeros((off, 2 * both), jnp.bfloat16)
+    for j in range(INTERLEAVE):
+        start, span, turned, qb = held[j]
+        inverse, delta = sums[j]
+        acc = jnp.zeros((lanes, 2 * both), jnp.float32)
+        for w in taps:
+            prob = sd[j, w, :width, :both] * inverse
+            ds = (prob * (sd[j, w, :width, both:] - delta)).astype(jnp.bfloat16)
+            dp = jnp.concatenate([ds, prob.astype(jnp.bfloat16)], axis=1)
+            dkv[base + w, span, :] += jnp.dot(dp, qb, preferred_element_type=jnp.float32)
+            if off:
+                dp = jnp.concatenate([edge, dp, edge], axis=0)
+            acc += jnp.dot(kvt[j % 2, base + w, :, turned], dp, preferred_element_type=jnp.float32)
+        qo = jnp.concatenate([acc[:HEAD_DIM, :both] * scale, acc[HEAD_DIM:, both:]], axis=0)
+        qo = qo.T.astype(jnp.bfloat16)
+        qow[r, pl.ds(start, HALF), :] = qo[:HALF]
+        qow[r + 1, pl.ds(start, HALF), :] = qo[HALF:]
+
+
+def two_pairs(reach_ref, logw_ref, kvw, kvt, qcw, dkv, sd, bias, qow, key_stride, own_first, own_stride, ext_first,
+              at_edge):
+    blocks = qcw.shape[1] // HALF
+    both = 2 * HALF
 
     @pl.loop(0, 2)
     def _(pair):
@@ -140,58 +201,27 @@
                 ok = near & second
             bias[w] = jnp.where(ok, logw_ref[ext_first + base + w], FAR)
 
-        @pl.loop(0, blocks // INTERLEAVE)
-        def _(group):
-            held = []
-            for j in range(INTERLEAVE):
-                block = group * INTERLEAVE + j
-                start = pl.multiple_of(block * HALF, HALF)
-                span = pl.ds(start, WINDOW)
-                turned = pl.ds(pl.multiple_of(start - (j % 2) * HALF, both), WINDOW)
-                rows_qc = jnp.concatenate(
-                    [qcw[r, pl.ds(start, HALF), :], qcw[r + 1, pl.ds(start, HALF), :]], axis=0)
-                zero = jnp.zeros_like(rows_qc)
-                qb = jnp.concatenate(
-                    [jnp.where(lane < HEAD_DIM, rows_qc * scale, zero),
-                     jnp.where(lane < HEAD_DIM, zero, rows_qc)], axis=0)
-                held.append((start, span, turned, qb))
-            tops = []
-            for j in range(INTERLEAVE):
-                _, span, _, qb = held[j]
-                top = jnp.full((8, both), FAR, jnp.float32)
-                for w in range(TAPS):
-                    product = lax.dot_general(kvw[base + w, span, :], qb, NT,
-                                              preferred_element_type=jnp.float32)
-                    score = product[:, :both] + bias[w]
-                    sd[j, w, :, :both] = score
-                    sd[j, w, :, both:] = product[:, both:]
-                    top = jnp.maximum(top, jnp.max(score.reshape(WINDOW // 8, 8, both), axis=0))
-                tops.append(jnp.max(top, axis=0, keepdims=True))
-            sums = []
-            for j in range(INTERLEAVE):
-                total = jnp.zeros((8, both), jnp.float32)
-                dot = jnp.zeros((8, both), jnp.float32)
-                for w in range(TAPS):
-                    p = jnp.exp(sd[j, w, :, :both] - tops[j])
-                    sd[j, w, :, :both] = p
-                    total += jnp.sum(p.reshape(WINDOW // 8, 8, both), axis=0)
-                    dot += jnp.sum((p * sd[j, w, :, both:]).reshape(WINDOW // 8, 8, both), axis=0)
-                inverse = 1.0 / jnp.sum(total, axis=0, keepdims=True)
-                sums.append((inverse, jnp.sum(dot, axis=0, keepdims=True) * inverse))
-            for j in range(INTERLEAVE):
-                start, span, turned, qb = held[j]
-                inverse, delta = sums[j]
-                acc = jnp.zeros((lanes, 2 * both), jnp.float32)
-                for w in range(TAPS):
-                    prob = sd[j, w, :, :both] * inverse
-                    ds = (prob * (sd[j, w, :, both:] - delta)).astype(jnp.bfloat16)
-                    dp = jnp.concatenate([ds, prob.astype(jnp.bfloat16)], axis=1)
-                    acc += jnp.dot(kvt[j % 2, base + w, :, turned], dp, preferred_element_type=jnp.float32)
-                    dkv[base + w, span, :] += jnp.dot(dp, qb, preferred_element_type=jnp.float32)
-                qo = jnp.concatenate([acc[:HEAD_DIM, :both] * scale, acc[HEAD_DIM:, both:]], axis=0)
-                qo = qo.T.astype(jnp.bfloat16)
-                qow[r, pl.ds(start, HALF), :] = qo[:HALF]
-                qow[r + 1, pl.ds(start, HALF), :] = qo[HALF:]
+        widest = jnp.maximum(reach_ref[own], reach_ref[own + 1])
+
+        def run(when, reach_class, w_first, w_last):
+            @pl.when(when)
+            def _():
+                @pl.loop(0, blocks // INTERLEAVE)
+                def _(group):
+                    block_group(group, r, base, reach_class, w_first, w_last,
+                                kvw, kvt, qcw, dkv, sd, bias, qow)
+
+        rest = widest <= REACH
+        if at_edge:
+            no_above = logw_ref[ext_first + base + HALO - 1] < 0.5 * FAR
+            no_below = logw_ref[ext_first + base + TAPS - HALO] < 0.5 * FAR
+            run(no_above, REACH, HALO, TAPS)
+            run(no_below, REACH, 0, TAPS - HALO)
+            rest = jnp.logical_not(no_above | no_below)
+        below = 0
+        for reach_class in CLASSES:
+            run(rest & (widest > below) & (widest <= reach_class), reach_class, 0, TAPS)
+            below = reach_class
 
 
 def wrap_and_turn(kvw, kvt):
@@ -254,7 +284,7 @@
             dkv[kr] = jnp.zeros(dkv.shape[1:], jnp.float32)
 
         two_pairs(reach_ref, logw_ref, kvw, kvt, qcw, dkv, sd, bias, qow,
-                  rows - HALO, 0, rows - HALO, 0)
+                  rows - HALO, 0, rows - HALO, 0, True)
         fold(dkv)
         part_ref[...] = dkv[HALO:HALO + rows, REACH:REACH + ring]
         for s in range(sectors):
@@ -295,7 +325,7 @@
             dkv[kr, REACH:REACH + ring] = part_ref[kr]
             dkv[kr, REACH + ring:padded] = jnp.zeros((REACH, lanes), jnp.float32)
 
-        two_pairs(reach_ref, logw_ref, kvw, kvt, qcw, dkv, sd, bias, qow, HALO, HALO, HALO, HALO)
+        two_pairs(reach_ref, logw_ref, kvw, kvt, qcw, dkv, sd, bias, qow, HALO, HALO, HALO, HALO, False)
         fold(dkv)
         for s in range(sectors):
             at = slice(REACH + s * cols, REACH + (s + 1) * cols)
@@ -334,7 +364,8 @@
     qc_edge = exchange(pack_pair(queries, cotangent, (0, rows // HALO - 1), HALO))
     above = to_next_band(kv[:, rows - HALO:], 1)
     below = to_next_band(kv[:, :HALO], -1)
-    qc_mid = exchange(pack_pair(queries, cotangent, (1, 2), HALO))
+    qc_mid, above, below = lax.optimization_barrier((pack_pair(queries, cotangent, (1, 2), HALO), above, below))
+    qc_mid = exchange(qc_mid)
     qo_edge, up, down, part = attend_edge(lon_reach, log_weight, kv, above, below, qc_edge)
     from_below = to_next_band(up, -1)
     from_above = to_next_band(down, 1)

time: 189 us -> 174 us (0.921)
  Pallas kernels: 69.7 us -> 55.2 us
    pallas_call x1, Pallas kernels: 27.2 us -> 19.7 us  [attend_mid(): pl.pallas_call(body, in_specs=[smem(), smem(), vmem(), vmem(), vmem()], o...]
    pallas_call x1, Pallas kernels: 28.1 us -> 21 us  [attend_edge(): pl.pallas_call(body, in_specs=[smem(), smem(), vmem(), vmem(), vmem(), vm...]
  transfers between devices with their start and end apart: 9 -> 9, of which waited for: 5 -> 4; matrix products, arithmetic and copies ran while one was open for 2% -> 2% of each run, Pallas kernels for 33% -> 27%
where the time goes in v3:
time: 174 us; the launch traced here: 172 us
  waiting for transfers between devices  67.3 us (39%)
  Pallas kernels  55.2 us (32%)
  starting transfers between devices  42.8 us (25%)
  local copies, waits for them, and re-layouts  3.06 us (2%)
  other arithmetic  2.92 us (2%)
    all_to_all x5, waiting for transfers between devices, exchange(): return lax.all_to_all(packed, 'lon', 0, 0)  49 us
    all_to_all x5, starting transfers between devices, exchange(): return lax.all_to_all(packed, 'lon', 0, 0)  28.3 us
    pallas_call x1, Pallas kernels, attend_edge(): pl.pallas_call(body, in_specs=[smem(), smem(), vmem(), vmem(), vmem(), vm...  21 us
    pallas_call x1, Pallas kernels, attend_mid(): pl.pallas_call(body, in_specs=[smem(), smem(), vmem(), vmem(), vmem()], o...  19.7 us
    ppermute x4, waiting for transfers between devices, to_next_band(): lax.ppermute(block, 'lat', [(i, i + step) for i in range(bands) if 0 <= i...  18.4 us
    ppermute x4, starting transfers between devices, to_next_band(): lax.ppermute(block, 'lat', [(i, i + step) for i in range(bands) if 0 <= i...  14.5 us
    pallas_call x3, Pallas kernels, pack_pair(): pl.pallas_call(body, grid=(count,), in_specs=[block, block], out_specs=pl...  6.94 us
    pallas_call x1, Pallas kernels, unpack_rest(): pl.pallas_call(body, grid=(2 * half + 2,), in_specs=[pl.BlockSpec((heads,...  5.35 us
  transfers between devices with their start and end apart: 9, of which 4 were waited for; matrix products, arithmetic and copies ran while one was open for 2% of the time, Pallas kernels for 27%

profile of v3, /device:TPU:99, one launch (start us, length us, event | category | flops | bytes accessed | tf_op | source)
XLA Modules:
  0.0 172.1 jit_solution(17029894349520557024)
XLA Ops:
  0.6 0.0 copy-start
  0.6 2.6 %shard_map.93 = bf16[16,8,48,128]{3,2,1,0:T(8,128)(2,1)} custom-call(bf16[8,48,1024]{2,1,0:T(8,128)(2,1)} %left_ref.3, bf16[8,48,1024]{2,1,0:T(8,128)(2,1)} %right_ref.3), custom_call_target="tpu_custom_call" | custom-call | tf_op jit(solution)/shard_map/pallas_call | solution.py:49
  3.3 6.2 %all-to-all-start = ((bf16[16,8,48,128]{3,2,1,0:T(8,128)(2,1)}), bf16[16,8,48,128]{3,2,1,0:T(8,128)(2,1)S(1)}, u32[]{:S(2)}, u32[]{:S(2)}) async-start(bf16[16,8,48,128]{3,2,1,0:T(8,128)(2,1)} %shard_map.93), calls=%async_computation | async-start | bytes 3145728 | tf_op jit(solution)/shard_map/all_to_all | solution.py:349
  9.4 2.2 %shard_map.95 = bf16[16,4,48,128]{3,2,1,0:T(8,128)(2,1)} custom-call(bf16[8,48,1024]{2,1,0:T(8,128)(2,1)} %left_ref.5, bf16[8,48,1024]{2,1,0:T(8,128)(2,1)} %right_ref.5), custom_call_target="tpu_custom_call" | custom-call | tf_op jit(solution)/shard_map/pallas_call | solution.py:49
  11.6 19.0 %all-to-all-done.kv_ref = bf16[16,8,48,128]{3,2,1,0:T(8,128)(2,1)S(1)} async-done(((bf16[16,8,48,128]{3,2,1,0:T(8,128)(2,1)}), bf16[16,8,48,128]{3,2,1,0:T(8,128)(2,1)S(1)}, u32[]{:S(2)}, u32[]{:S(2)}) %all-to-all-start) | async-done | bytes 1572896 | tf_op jit(solution)/shard_map/all_to_all | solution.py:349
  30.6 4.5 %all-to-all-start.2 = ((bf16[16,4,48,128]{3,2,1,0:T(8,128)(2,1)}), bf16[16,4,48,128]{3,2,1,0:T(8,128)(2,1)S(1)}, u32[]{:S(2)}, u32[]{:S(2)}) async-start(bf16[16,4,48,128]{3,2,1,0:T(8,128)(2,1)} %shard_map.95), calls=%async_computation.2 | async-start | bytes 1572864 | tf_op jit(solution)/shard_map/all_to_all | solution.py:349
  35.1 2.2 %shard_map.94 = bf16[16,4,48,128]{3,2,1,0:T(8,128)(2,1)} custom-call(bf16[8,48,1024]{2,1,0:T(8,128)(2,1)} %left_ref.5, bf16[8,48,1024]{2,1,0:T(8,128)(2,1)} %right_ref.5), custom_call_target="tpu_custom_call" | custom-call | tf_op jit(solution)/shard_map/pallas_call | solution.py:49
  37.2 0.1 fusion.2
  37.3 4.4 %collective-permute-start.1 = (bf16[16,2,48,128]{3,2,1,0:T(8,128)(2,1)S(1)}, bf16[16,2,48,128]{3,2,1,0:T(8,128)(2,1)S(1)}, u32[]{:S(2)}, u32[]{:S(2)}) collective-permute-start(bf16[16,2,48,128]{3,2,1,0:T(8,128)(2,1)S(1)} %get-tuple-element.30), channel_id=1, source_target_pairs={{16,0},{32,16},{48,32},{64,48},{80,64},{96,80},{112,96},{17,1},{33... | collective-permute-start | bytes 1179656 | tf_op jit(solution)/shard_map/ppermute | solution.py:354
  41.7 2.4 %collective-permute-start = (bf16[16,2,48,128]{3,2,1,0:T(8,128)(2,1)S(1)}, bf16[16,2,48,128]{3,2,1,0:T(8,128)(2,1)S(1)}, u32[]{:S(2)}, u32[]{:S(2)}) collective-permute-start(bf16[16,2,48,128]{3,2,1,0:T(8,128)(2,1)S(1)} %get-tuple-element.31), channel_id=1, source_target_pairs={{0,16},{16,32},{32,48},{48,64},{64,80},{80,96},{96,112},{1,17},{17... | collective-permute-start | bytes 1179656 | tf_op jit(solution)/shard_map/ppermute | solution.py:354
  44.1 0.7 gather_fusion
  44.8 0.6 and_select_fusion.logw_ref
  45.4 10.1 %collective-permute-done.1.below_ref = bf16[16,2,48,128]{3,2,1,0:T(8,128)(2,1)S(1)} collective-permute-done((bf16[16,2,48,128]{3,2,1,0:T(8,128)(2,1)S(1)}, bf16[16,2,48,128]{3,2,1,0:T(8,128)(2,1)S(1)}, u32[]{:S(2)}, u32[]{:S(2)}) %collective-permute-start.1) | collective-permute-done | bytes 393248 | tf_op jit(solution)/shard_map/ppermute | solution.py:354
  55.5 8.3 %collective-permute-done.above_ref = bf16[16,2,48,128]{3,2,1,0:T(8,128)(2,1)S(1)} collective-permute-done((bf16[16,2,48,128]{3,2,1,0:T(8,128)(2,1)S(1)}, bf16[16,2,48,128]{3,2,1,0:T(8,128)(2,1)S(1)}, u32[]{:S(2)}, u32[]{:S(2)}) %collective-permute-start) | collective-permute-done | bytes 393248 | tf_op jit(solution)/shard_map/ppermute | solution.py:354
  63.8 0.0 all-to-all-done.2.qc_ref
  63.8 5.7 %all-to-all-start.1 = ((bf16[16,4,48,128]{3,2,1,0:T(8,128)(2,1)}), bf16[16,4,48,128]{3,2,1,0:T(8,128)(2,1)S(1)}, u32[]{:S(2)}, u32[]{:S(2)}) async-start(bf16[16,4,48,128]{3,2,1,0:T(8,128)(2,1)} %shard_map.94), calls=%async_computation.1 | async-start | bytes 1572864 | tf_op jit(solution)/shard_map/all_to_all | solution.py:349
  69.5 21.0 %shard_map.96 = (bf16[16,4,48,128]{3,2,1,0:T(8,128)(2,1)}, bf16[16,2,48,128]{3,2,1,0:T(8,128)(2,1)}, bf16[16,2,48,128]{3,2,1,0:T(8,128)(2,1)}, f32[8,768,128]{2,1,0:T(8,128)}) custom-call(s32[8]{0:T(128)} %reach_ref.3, f32[12]{0:T(128)} %and_select_fusion.logw_ref, bf16[16,8,48,128]{3,2,1,0:T(8,128)(2,1)} %copy-done.2, bf16[16,2,48,128]{3,2,1,0:T(8,128)(2,1)} %copy-done.7, ...), custom_call_target="tpu_custom_call" | custom-call | flops 20000000000 | bytes 8000000 | tf_op jit(solution)/shard_map/pallas_call | solution.py:299
  90.5 3.7 %collective-permute-start.2 = (bf16[16,2,48,128]{3,2,1,0:T(8,128)(2,1)}, bf16[16,2,48,128]{3,2,1,0:T(8,128)(2,1)S(1)}, u32[]{:S(2)}, u32[]{:S(2)}) collective-permute-start(bf16[16,2,48,128]{3,2,1,0:T(8,128)(2,1)} %get-tuple-element.21), channel_id=1, source_target_pairs={{0,16},{16,32},{32,48},{48,64},{64,80},{80,96},{96,112},{1,17},{17... | collective-permute-start | bytes 1179656 | tf_op jit(solution)/shard_map/ppermute | solution.py:354
  94.3 3.9 %collective-permute-start.3 = (bf16[16,2,48,128]{3,2,1,0:T(8,128)(2,1)}, bf16[16,2,48,128]{3,2,1,0:T(8,128)(2,1)S(1)}, u32[]{:S(2)}, u32[]{:S(2)}) collective-permute-start(bf16[16,2,48,128]{3,2,1,0:T(8,128)(2,1)} %get-tuple-element.22), channel_id=1, source_target_pairs={{16,0},{32,16},{48,32},{64,48},{80,64},{96,80},{112,96},{17,1},{33... | collective-permute-start | bytes 1179656 | tf_op jit(solution)/shard_map/ppermute | solution.py:354
  98.2 0.0 all-to-all-done.1.qc_ref
  98.2 0.0 copy-start.5
  98.2 6.3 %all-to-all-start.4 = ((bf16[16,4,48,128]{3,2,1,0:T(8,128)(2,1)}), bf16[16,4,48,128]{3,2,1,0:T(8,128)(2,1)S(1)}, u32[]{:S(2)}, u32[]{:S(2)}) async-start(bf16[16,4,48,128]{3,2,1,0:T(8,128)(2,1)} %get-tuple-element.23), calls=%async_computation.4 | async-start | bytes 1572864 | tf_op jit(solution)/shard_map/all_to_all | solution.py:349
  104.5 19.7 %shard_map.97 = bf16[16,12,48,128]{3,2,1,0:T(8,128)(2,1)} custom-call(s32[8]{0:T(128)} %reach_ref.3, f32[12]{0:T(128)} %and_select_fusion.logw_ref, bf16[16,8,48,128]{3,2,1,0:T(8,128)(2,1)} %copy-done.2, bf16[16,4,48,128]{3,2,1,0:T(8,128)(2,1)} %copy-done.5, f32[8,768,128]{2,1,0:T(8,128)} %get-tuple-element.20.part_ref), custom_call_target="tpu_custom_call" | custom-call | flops 20000000000 | bytes 8000000 | tf_op jit(solution)/shard_map/pallas_call | solution.py:337
  124.3 0.0 collective-permute-done.2
  124.3 2.3 %fusion = bf16[16,12,48,128]{3,2,1,0:T(8,128)(2,1)} fusion(bf16[16,12,48,128]{3,2,1,0:T(8,128)(2,1)} %shard_map.97, bf16[16,2,48,128]{3,2,1,0:T(8,128)(2,1)S(1)} %collective-permute-done.3, bf16[16,2,48,128]{3,2,1,0:T(8,128)(2,1)S(1)} %collective-permute-done.2), kind=kLoop, calls=%fused_computation.2 | loop fusion | flops 2752512 | bytes 2359296 | tf_op jit(solution)/shard_map/dynamic_update_slice | solution.py:376
  126.6 0.0 all-to-all-done.4.in_ref
  126.6 0.9 copy-done.3
  127.5 5.7 %all-to-all-start.3 = ((bf16[16,12,48,128]{3,2,1,0:T(8,128)(2,1)}), bf16[16,12,48,128]{3,2,1,0:T(8,128)(2,1)S(1)}, u32[]{:S(2)}, u32[]{:S(2)}) async-start(bf16[16,12,48,128]{3,2,1,0:T(8,128)(2,1)} %fusion), calls=%async_computation.3 | async-start | bytes 4718592 | tf_op jit(solution)/shard_map/all_to_all | solution.py:349
  133.2 2.1 %shard_map.98 = (bf16[8,48,1024]{2,1,0:T(8,128)(2,1)}, bf16[8,48,1024]{2,1,0:T(8,128)(2,1)}) custom-call(bf16[16,4,48,128]{3,2,1,0:T(8,128)(2,1)} %copy-done.3), custom_call_target="tpu_custom_call" | custom-call | tf_op jit(solution)/shard_map/pallas_call | solution.py:73
  135.3 30.0 %all-to-all-done.3.in_ref = bf16[16,12,48,128]{3,2,1,0:T(8,128)(2,1)S(1)} async-done(((bf16[16,12,48,128]{3,2,1,0:T(8,128)(2,1)}), bf16[16,12,48,128]{3,2,1,0:T(8,128)(2,1)S(1)}, u32[]{:S(2)}, u32[]{:S(2)}) %all-to-all-start.3) | async-done | bytes 2359328 | tf_op jit(solution)/shard_map/all_to_all | solution.py:349
  165.3 1.4 copy-done.1
  166.7 5.4 %shard_map.99 = (bf16[8,48,1024]{2,1,0:T(8,128)(2,1)}, bf16[8,48,1024]{2,1,0:T(8,128)(2,1)}, bf16[8,48,1024]{2,1,0:T(8,128)(2,1)}, bf16[8,48,1024]{2,1,0:T(8,128)(2,1)}) custom-call(bf16[16,12,48,128]{3,2,1,0:T(8,128)(2,1)} %copy-done.1, bf16[8,48,1024]{2,1,0:T(8,128)(2,1)} %get-tuple-element.24._, ...), custom_call_target="tpu_custom_call", output_to_operand_aliasing={{0}: (1, {}), {1}: (2, {})} | custom-call | tf_op jit(solution)/shard_map/pallas_call | solution.py:109
  (15 shorter events, 0.0 us)
Async XLA Ops:
  0.6 43.5 %copy-start = (f32[64]{0:T(128)S(1)}, f32[64]{0:T(128)}, u32[]{:S(2)}) copy-start(f32[64]{0:T(128)} %param.10) | copy-start | bytes 772
  3.3 27.3 %all-to-all-start = ((bf16[16,8,48,128]{3,2,1,0:T(8,128)(2,1)}), bf16[16,8,48,128]{3,2,1,0:T(8,128)(2,1)S(1)}, u32[]{:S(2)}, u32[]{:S(2)}) async-start(bf16[16,8,48,128]{3,2,1,0:T(8,128)(2,1)} %shard_map.93), calls=%async_computation | async-start | bytes 3145728 | tf_op jit(solution)/shard_map/all_to_all | solution.py:349
  30.6 6.6 %copy-start.2 = (bf16[16,8,48,128]{3,2,1,0:T(8,128)(2,1)}, bf16[16,8,48,128]{3,2,1,0:T(8,128)(2,1)S(1)}, u32[]{:S(2)}) copy-start(bf16[16,8,48,128]{3,2,1,0:T(8,128)(2,1)S(1)} %all-to-all-done.kv_ref) | copy-start | bytes 4718596
  30.6 33.2 %all-to-all-start.2 = ((bf16[16,4,48,128]{3,2,1,0:T(8,128)(2,1)}), bf16[16,4,48,128]{3,2,1,0:T(8,128)(2,1)S(1)}, u32[]{:S(2)}, u32[]{:S(2)}) async-start(bf16[16,4,48,128]{3,2,1,0:T(8,128)(2,1)} %shard_map.95), calls=%async_computation.2 | async-start | bytes 1572864 | tf_op jit(solution)/shard_map/all_to_all | solution.py:349
  37.3 18.2 %collective-permute-start.1 = (bf16[16,2,48,128]{3,2,1,0:T(8,128)(2,1)S(1)}, bf16[16,2,48,128]{3,2,1,0:T(8,128)(2,1)S(1)}, u32[]{:S(2)}, u32[]{:S(2)}) collective-permute-start(bf16[16,2,48,128]{3,2,1,0:T(8,128)(2,1)S(1)} %get-tuple-element.30), channel_id=1, source_target_pairs={{16,0},{32,16},{48,32},{64,48},{80,64},{96,80},{112,96},{17,1},{33... | collective-permute-start | bytes 1179656 | tf_op jit(solution)/shard_map/ppermute | solution.py:354
  41.7 22.1 %collective-permute-start = (bf16[16,2,48,128]{3,2,1,0:T(8,128)(2,1)S(1)}, bf16[16,2,48,128]{3,2,1,0:T(8,128)(2,1)S(1)}, u32[]{:S(2)}, u32[]{:S(2)}) collective-permute-start(bf16[16,2,48,128]{3,2,1,0:T(8,128)(2,1)S(1)} %get-tuple-element.31), channel_id=1, source_target_pairs={{0,16},{16,32},{32,48},{48,64},{64,80},{80,96},{96,112},{1,17},{17... | collective-permute-start | bytes 1179656 | tf_op jit(solution)/shard_map/ppermute | solution.py:354
  55.5 14.0 %copy-start.6 = (bf16[16,2,48,128]{3,2,1,0:T(8,128)(2,1)}, bf16[16,2,48,128]{3,2,1,0:T(8,128)(2,1)S(1)}, u32[]{:S(2)}) copy-start(bf16[16,2,48,128]{3,2,1,0:T(8,128)(2,1)S(1)} %collective-permute-done.1.below_ref) | copy-start | bytes 1179652
  63.8 5.7 %copy-start.7 = (bf16[16,2,48,128]{3,2,1,0:T(8,128)(2,1)}, bf16[16,2,48,128]{3,2,1,0:T(8,128)(2,1)S(1)}, u32[]{:S(2)}) copy-start(bf16[16,2,48,128]{3,2,1,0:T(8,128)(2,1)S(1)} %collective-permute-done.above_ref) | copy-start | bytes 1179652
  63.8 5.7 %copy-start.4 = (bf16[16,4,48,128]{3,2,1,0:T(8,128)(2,1)}, bf16[16,4,48,128]{3,2,1,0:T(8,128)(2,1)S(1)}, u32[]{:S(2)}) copy-start(bf16[16,4,48,128]{3,2,1,0:T(8,128)(2,1)S(1)} %all-to-all-done.2.qc_ref) | copy-start | bytes 2359300
  63.8 34.4 %all-to-all-start.1 = ((bf16[16,4,48,128]{3,2,1,0:T(8,128)(2,1)}), bf16[16,4,48,128]{3,2,1,0:T(8,128)(2,1)S(1)}, u32[]{:S(2)}, u32[]{:S(2)}) async-start(bf16[16,4,48,128]{3,2,1,0:T(8,128)(2,1)} %shard_map.94), calls=%async_computation.1 | async-start | bytes 1572864 | tf_op jit(solution)/shard_map/all_to_all | solution.py:349
  90.5 33.8 %collective-permute-start.2 = (bf16[16,2,48,128]{3,2,1,0:T(8,128)(2,1)}, bf16[16,2,48,128]{3,2,1,0:T(8,128)(2,1)S(1)}, u32[]{:S(2)}, u32[]{:S(2)}) collective-permute-start(bf16[16,2,48,128]{3,2,1,0:T(8,128)(2,1)} %get-tuple-element.21), channel_id=1, source_target_pairs={{0,16},{16,32},{32,48},{48,64},{64,80},{80,96},{96,112},{1,17},{17... | collective-permute-start | bytes 1179656 | tf_op jit(solution)/shard_map/ppermute | solution.py:354
  94.3 30.0 %collective-permute-start.3 = (bf16[16,2,48,128]{3,2,1,0:T(8,128)(2,1)}, bf16[16,2,48,128]{3,2,1,0:T(8,128)(2,1)S(1)}, u32[]{:S(2)}, u32[]{:S(2)}) collective-permute-start(bf16[16,2,48,128]{3,2,1,0:T(8,128)(2,1)} %get-tuple-element.22), channel_id=1, source_target_pairs={{16,0},{32,16},{48,32},{64,48},{80,64},{96,80},{112,96},{17,1},{33... | collective-permute-start | bytes 1179656 | tf_op jit(solution)/shard_map/ppermute | solution.py:354
  98.2 6.3 %copy-start.5 = (bf16[16,4,48,128]{3,2,1,0:T(8,128)(2,1)}, bf16[16,4,48,128]{3,2,1,0:T(8,128)(2,1)S(1)}, u32[]{:S(2)}) copy-start(bf16[16,4,48,128]{3,2,1,0:T(8,128)(2,1)S(1)} %all-to-all-done.1.qc_ref) | copy-start | bytes 2359300
  98.2 28.4 %all-to-all-start.4 = ((bf16[16,4,48,128]{3,2,1,0:T(8,128)(2,1)}), bf16[16,4,48,128]{3,2,1,0:T(8,128)(2,1)S(1)}, u32[]{:S(2)}, u32[]{:S(2)}) async-start(bf16[16,4,48,128]{3,2,1,0:T(8,128)(2,1)} %get-tuple-element.23), calls=%async_computation.4 | async-start | bytes 1572864 | tf_op jit(solution)/shard_map/all_to_all | solution.py:349
  126.6 0.9 copy-start.3
  127.5 37.8 %all-to-all-start.3 = ((bf16[16,12,48,128]{3,2,1,0:T(8,128)(2,1)}), bf16[16,12,48,128]{3,2,1,0:T(8,128)(2,1)S(1)}, u32[]{:S(2)}, u32[]{:S(2)}) async-start(bf16[16,12,48,128]{3,2,1,0:T(8,128)(2,1)} %fusion), calls=%async_computation.3 | async-start | bytes 4718592 | tf_op jit(solution)/shard_map/all_to_all | solution.py:349
  165.3 1.4 copy-start.1

commit v4 on v3

v4 whole, which is shorter than its diff:
```python
import jax
import jax.numpy as jnp
from jax import lax
from jax.experimental import pallas as pl
from jax.experimental.pallas import tpu as pltpu
from jax.sharding import Mesh, PartitionSpec as P

HEADS = 16
HEAD_DIM = 64
HALO = 2
REACH = 96
HALF = 64
TAPS = 2 * HALO + 2
WINDOW = HALF + 2 * REACH
INTERLEAVE = 4
CLASSES = (48, 64, 80, 96)
FAR = -1e30
VMEM_BYTES = 56 * 1024 * 1024
NT = (((1,), (1,)), ((), ()))


def vmem():
    return pl.BlockSpec(memory_space=pltpu.VMEM)


def smem():
    return pl.BlockSpec(memory_space=pltpu.SMEM)


def pack_pair(left, right):
    rows, cols, width = left.shape
    heads = width // HEAD_DIM
    step = rows // 2

    def body(left_ref, right_ref, out_ref):
        for i in range(step):
            for h in range(heads):
                at = slice(h * HEAD_DIM, (h + 1) * HEAD_DIM)
                out_ref[h, i] = jnp.concatenate([left_ref[i, :, at], right_ref[i, :, at]], axis=-1)

    block = pl.BlockSpec((step, cols, width), lambda i: (i, 0, 0))
    return pl.pallas_call(
        body,
        grid=(2,),
        in_specs=[block, block],
        out_specs=pl.BlockSpec((heads, step, cols, 2 * HEAD_DIM), lambda i: (0, i, 0, 0)),
        out_shape=jax.ShapeDtypeStruct((heads, rows, cols, 2 * HEAD_DIM), left.dtype),
    )(left, right)


def unpack_pair(packed):
    heads, rows, cols, lanes = packed.shape
    width = heads * HEAD_DIM
    step = rows // 2

    def body(in_ref, left_ref, right_ref):
        for i in range(step):
            for pair in range(heads // 2):
                first, second = in_ref[2 * pair, i], in_ref[2 * pair + 1, i]
                at = slice(pair * 2 * HEAD_DIM, (pair + 1) * 2 * HEAD_DIM)
                left_ref[i, :, at] = jnp.concatenate([first[:, :HEAD_DIM], second[:, :HEAD_DIM]], axis=1)
                right_ref[i, :, at] = jnp.concatenate([first[:, HEAD_DIM:], second[:, HEAD_DIM:]], axis=1)

    out = pl.BlockSpec((step, cols, width), lambda i: (i, 0, 0))
    shape = jax.ShapeDtypeStruct((rows, cols, width), packed.dtype)
    return pl.pallas_call(
        body,
        grid=(2,),
        in_specs=[pl.BlockSpec((heads, step, cols, lanes), lambda i: (0, i, 0, 0))],
        out_specs=[out, out],
        out_shape=[shape, shape],
    )(packed)


def block_group(group, r, base, reach_class, w_first, w_last, kvw, kvt, qcw, dkv, sd, bias, qow):
    lanes = kvw.shape[-1]
    both = 2 * HALF
    scale = float(HEAD_DIM) ** -0.5
    lane = lax.broadcasted_iota(jnp.int32, (both, lanes), 1)
    off = REACH - reach_class
    width = HALF + 2 * reach_class
    taps = range(w_first, w_last)
    held = []
    for j in range(INTERLEAVE):
        block = group * INTERLEAVE + j
        start = pl.multiple_of(block * HALF, HALF)
        span = pl.ds(pl.multiple_of(start + off, 16), width)
        turned = pl.ds(pl.multiple_of(start - (j % 2) * HALF, both), WINDOW)
        rows_qc = jnp.concatenate(
            [qcw[r, pl.ds(start, HALF), :], qcw[r + 1, pl.ds(start, HALF), :]], axis=0)
        zero = jnp.zeros_like(rows_qc)
        qb = jnp.concatenate(
            [jnp.where(lane < HEAD_DIM, rows_qc * scale, zero),
             jnp.where(lane < HEAD_DIM, zero, rows_qc)], axis=0)
        held.append((start, span, turned, qb))
    tops = []
    for j in range(INTERLEAVE):
        _, span, _, qb = held[j]
        top = jnp.full((8, both), FAR, jnp.float32)
        for w in taps:
            product = lax.dot_general(kvw[base + w, span, :], qb, NT, preferred_element_type=jnp.float32)
            score = product[:, :both] + bias[w, off:off + width]
            sd[j, w, :width, :both] = score
            sd[j, w, :width, both:] = product[:, both:]
            top = jnp.maximum(top, jnp.max(score.reshape(width // 8, 8, both), axis=0))
        tops.append(jnp.max(top, axis=0, keepdims=True))
    sums = []
    for j in range(INTERLEAVE):
        total = jnp.zeros((8, both), jnp.float32)
        dot = jnp.zeros((8, both), jnp.float32)
        for w in taps:
            p = jnp.exp(sd[j, w, :width, :both] - tops[j])
            sd[j, w, :width, :both] = p
            total += jnp.sum(p.reshape(width // 8, 8, both), axis=0)
            dot += jnp.sum((p * sd[j, w, :width, both:]).reshape(width // 8, 8, both), axis=0)
        inverse = 1.0 / jnp.sum(total, axis=0, keepdims=True)
        sums.append((inverse, jnp.sum(dot, axis=0, keepdims=True) * inverse))
    edge = jnp.zeros((off, 2 * both), jnp.bfloat16)
    for j in range(INTERLEAVE):
        start, span, turned, qb = held[j]
        inverse, delta = sums[j]
        acc = jnp.zeros((lanes, 2 * both), jnp.float32)
        for w in taps:
            prob = sd[j, w, :width, :both] * inverse
            ds = (prob * (sd[j, w, :width, both:] - delta)).astype(jnp.bfloat16)
            dp = jnp.concatenate([ds, prob.astype(jnp.bfloat16)], axis=1)
            dkv[base + w, span, :] += jnp.dot(dp, qb, preferred_element_type=jnp.float32)
            if off:
                dp = jnp.concatenate([edge, dp, edge], axis=0)
            acc += jnp.dot(kvt[j % 2, base + w, :, turned], dp, preferred_element_type=jnp.float32)
        qo = jnp.concatenate([acc[:HEAD_DIM, :both] * scale, acc[HEAD_DIM:, both:]], axis=0)
        qo = qo.T.astype(jnp.bfloat16)
        qow[r, pl.ds(start, HALF), :] = qo[:HALF]
        qow[r + 1, pl.ds(start, HALF), :] = qo[HALF:]


def row_pairs(reach_ref, logw_ref, kvw, kvt, qcw, dkv, sd, bias, qow):
    blocks = qcw.shape[1] // HALF
    both = 2 * HALF

    @pl.loop(0, 4)
    def _(pair):
        r = 2 * pair
        base = r + jnp.where(pair >= 2, 2 * HALO, 0)
        key = lax.broadcasted_iota(jnp.int32, (WINDOW, both), 0) - REACH
        query = lax.broadcasted_iota(jnp.int32, (WINDOW, both), 1)
        second = query >= HALF
        gap = jnp.abs(key - jnp.where(second, query - HALF, query))
        near = gap <= jnp.where(second, reach_ref[r + 1], reach_ref[r])
        for w in range(TAPS):
            ok = near
            if w == 0:
                ok = near & jnp.logical_not(second)
            if w == TAPS - 1:
                ok = near & second
            bias[w] = jnp.where(ok, logw_ref[base + w], FAR)

        widest = jnp.maximum(reach_ref[r], reach_ref[r + 1])

        def run(when, reach_class, w_first, w_last):
            @pl.when(when)
            def _():
                @pl.loop(0, blocks // INTERLEAVE)
                def _(group):
                    block_group(group, r, base, reach_class, w_first, w_last,
                                kvw, kvt, qcw, dkv, sd, bias, qow)

        no_above = logw_ref[base + HALO - 1] < 0.5 * FAR
        no_below = logw_ref[base + TAPS - HALO] < 0.5 * FAR
        run(no_above, REACH, HALO, TAPS)
        run(no_below, REACH, 0, TAPS - HALO)
        rest = jnp.logical_not(no_above | no_below)
        below = 0
        for reach_class in CLASSES:
            run(rest & (widest > below) & (widest <= reach_class), reach_class, 0, TAPS)
            below = reach_class


def attend(second_half, reach, log_weight, kv, kv_partner, kv_plane, qc):
    _, sectors, rows, cols, lanes = kv.shape
    ring = sectors * cols
    padded = ring + 2 * REACH
    run = rows + 2 * HALO

    def body(half_ref, reach_ref, logw_ref, kv_ref, partner_ref, plane_ref, qc_ref,
             qo_ref, own_ref, to_partner_ref, to_plane_ref, kvw, kvt, qcw, dkv, sd, bias, qow):
        first = half_ref[0] == 0
        for s in range(sectors):
            at = slice(REACH + s * cols, REACH + (s + 1) * cols)
            for n in range(2):
                kvw[n * run + HALO:n * run + HALO + rows, at] = kv_ref[n, s]
                qcw[n * rows:(n + 1) * rows, s * cols:(s + 1) * cols] = qc_ref[n, s]

        @pl.when(first)
        def _():
            for s in range(sectors):
                at = slice(REACH + s * cols, REACH + (s + 1) * cols)
                kvw[0:2, at] = plane_ref[s]
                kvw[6:8, at] = partner_ref[0, s, 0:2]
                kvw[8:10, at] = partner_ref[0, s, 2:4]
                kvw[14:16, at] = partner_ref[1, s, 0:2]

        @pl.when(jnp.logical_not(first))
        def _():
            for s in range(sectors):
                at = slice(REACH + s * cols, REACH + (s + 1) * cols)
                kvw[0:2, at] = partner_ref[0, s, 2:4]
                kvw[6:8, at] = partner_ref[1, s, 0:2]
                kvw[8:10, at] = partner_ref[1, s, 2:4]
                kvw[14:16, at] = plane_ref[s]

        kvw[:, 0:REACH] = kvw[:, ring:ring + REACH]
        kvw[:, REACH + ring:padded] = kvw[:, REACH:2 * REACH]

        @pl.loop(0, 2 * run)
        def _(kr):
            kvt[0, kr] = kvw[kr].T
            kvt[1, kr, :, 0:padded - HALF] = kvw[kr, HALF:].T
            dkv[kr] = jnp.zeros((padded, lanes), jnp.float32)

        row_pairs(reach_ref, logw_ref, kvw, kvt, qcw, dkv, sd, bias, qow)

        dkv[:, ring:ring + REACH] += dkv[:, 0:REACH]
        dkv[:, REACH:2 * REACH] += dkv[:, REACH + ring:padded]
        for s in range(sectors):
            at = slice(REACH + s * cols, REACH + (s + 1) * cols)
            for n in range(2):
                qo_ref[n, s] = qow[n * rows:(n + 1) * rows, s * cols:(s + 1) * cols]
                own_ref[n, s] = dkv[n * run + HALO:n * run + HALO + rows, at].astype(jnp.bfloat16)

        @pl.when(first)
        def _():
            for s in range(sectors):
                at = slice(REACH + s * cols, REACH + (s + 1) * cols)
                to_partner_ref[s, 0:4] = dkv[6:10, at].astype(jnp.bfloat16)
                to_partner_ref[s, 4:6] = dkv[14:16, at].astype(jnp.bfloat16)
                to_plane_ref[s] = dkv[0:2, at].astype(jnp.bfloat16)

        @pl.when(jnp.logical_not(first))
        def _():
            for s in range(sectors):
                at = slice(REACH + s * cols, REACH + (s + 1) * cols)
                to_partner_ref[s, 0:2] = dkv[0:2, at].astype(jnp.bfloat16)
                to_partner_ref[s, 2:6] = dkv[6:10, at].astype(jnp.bfloat16)
                to_plane_ref[s] = dkv[14:16, at].astype(jnp.bfloat16)

    whole = jax.ShapeDtypeStruct(kv.shape, jnp.bfloat16)

    def out(count):
        return jax.ShapeDtypeStruct((sectors, count, cols, lanes), jnp.bfloat16)

    return pl.pallas_call(
        body,
        in_specs=[smem(), smem(), smem(), vmem(), vmem(), vmem(), vmem()],
        out_specs=[vmem()] * 4,
        out_shape=[whole, whole, out(3 * HALO), out(HALO)],
        scratch_shapes=[
            pltpu.VMEM((2 * run, padded, lanes), jnp.bfloat16),
            pltpu.VMEM((2, 2 * run, lanes, padded), jnp.bfloat16),
            pltpu.VMEM((2 * rows, ring, lanes), jnp.bfloat16),
            pltpu.VMEM((2 * run, padded, lanes), jnp.float32),
            pltpu.VMEM((INTERLEAVE, TAPS, WINDOW, 4 * HALF), jnp.float32),
            pltpu.VMEM((TAPS, WINDOW, 2 * HALF), jnp.float32),
            pltpu.VMEM((2 * rows, ring, lanes), jnp.bfloat16),
        ],
        compiler_params=pltpu.CompilerParams(vmem_limit_bytes=VMEM_BYTES),
        cost_estimate=pl.CostEstimate(flops=40_000_000_000, bytes_accessed=10_000_000, transcendentals=5_000_000),
    )(second_half, reach, log_weight, kv, kv_partner, kv_plane, qc)


def add_home(second_half, own, partner, plane):
    runs, sectors, rows, cols, lanes = own.shape
    step = sectors // 4

    def body(half_ref, own_ref, partner_ref, plane_ref, out_ref):
        def add(order):
            for n, (ref, row) in enumerate(order):
                at = slice((n % 2) * HALO, (n % 2 + 1) * HALO)
                other = ref[:, row:row + HALO].astype(jnp.float32)
                out_ref[n // 2, :, at] = (own_ref[n // 2, :, at].astype(jnp.float32) + other).astype(out_ref.dtype)

        @pl.when(half_ref[0] == 0)
        def _():
            add([(plane_ref, 0), (partner_ref, 0), (partner_ref, 2), (partner_ref, 4)])

        @pl.when(half_ref[0] != 0)
        def _():
            add([(partner_ref, 0), (partner_ref, 2), (partner_ref, 4), (plane_ref, 0)])

    block = pl.BlockSpec((runs, step, rows, cols, lanes), lambda i: (0, i, 0, 0, 0))

    def side(count):
        return pl.BlockSpec((step, count, cols, lanes), lambda i: (i, 0, 0, 0))

    return pl.pallas_call(
        body,
        grid=(4,),
        in_specs=[smem(), block, side(3 * HALO), side(HALO)],
        out_specs=block,
        out_shape=jax.ShapeDtypeStruct(own.shape, own.dtype),
    )(second_half, own, partner, plane)


def exchange(packed):
    return lax.all_to_all(packed, ("band", "lon"), 0, 0)


def to_partner(block):
    return lax.ppermute(block, "lon", [(i, i ^ 1) for i in range(lax.axis_size("lon"))])


def to_next_plane(block):
    planes, columns = lax.axis_size("plane"), lax.axis_size("lon")
    route = []
    for plane in range(planes - 1):
        for i in range(1, columns, 2):
            here, there = plane * columns + i, (plane + 1) * columns + i - 1
            route += [(here, there), (there, here)]
    return lax.ppermute(block, ("plane", "lon"), route)


def on_device(queries, key_vectors, value_vectors, cotangent, quad_weight, lon_reach):
    rows, cols, _ = queries.shape
    half_rows = rows // 2
    bands, sectors = lax.axis_size("band"), lax.axis_size("lon")
    half = lax.axis_index("lon") % 2
    parted = (bands * sectors, half_rows, cols, 2 * HEAD_DIM)
    by_band = (bands, sectors, half_rows, cols, 2 * HEAD_DIM)

    other_reach = lax.ppermute(lon_reach, "band", [(0, 1), (1, 0)])
    lower = lax.axis_index("band") == 0
    reach = jnp.stack([jnp.where(lower, lon_reach, other_reach), jnp.where(lower, other_reach, lon_reach)])
    reach = lax.dynamic_slice_in_dim(reach, half * half_rows, half_rows, axis=1).reshape(-1)
    ext = (lax.axis_index("plane") * bands + jnp.arange(bands)[:, None]) * rows + half * half_rows - HALO
    ext = (ext + jnp.arange(half_rows + 2 * HALO)[None, :]).reshape(-1)
    inside = (ext >= 0) & (ext < quad_weight.shape[0])
    log_weight = jnp.where(inside, jnp.log(quad_weight[jnp.clip(ext, 0, quad_weight.shape[0] - 1)]), FAR)
    second_half = half.astype(jnp.int32).reshape(1)

    kv = exchange(pack_pair(key_vectors, value_vectors).reshape(parted)).reshape(by_band)
    rim = jnp.where(half == 0, kv[0, :, :HALO], kv[1, :, half_rows - HALO:])
    kv_plane = to_next_plane(rim)
    kv_partner = to_partner(kv)
    qc = exchange(pack_pair(queries, cotangent).reshape(parted)).reshape(by_band)
    qo, own, partner, plane = attend(second_half, reach, log_weight, kv, kv_partner, kv_plane, qc)
    plane = to_next_plane(plane)
    partner = to_partner(partner)
    packed = (HEADS, rows, cols, 2 * HEAD_DIM)
    grad_queries, attended = unpack_pair(exchange(qo.reshape(parted)).reshape(packed))
    total = add_home(second_half, own, partner, plane)
    grad_keys, grad_values = unpack_pair(exchange(total.reshape(parted)).reshape(packed))
    return attended, grad_queries, grad_keys, grad_values


def solution(mesh):
    bands, sectors = mesh.devices.shape
    planes = Mesh(mesh.devices.reshape(bands // 2, 2, sectors), ("plane", "band", "lon"))
    cells = P(("plane", "band"), "lon", None)
    return jax.shard_map(
        on_device,
        mesh=planes,
        in_specs=(cells, cells, cells, cells, P(), P(("plane", "band"))),
        out_specs=(cells, cells, cells, cells),
        check_vma=False,
    )
```

time: 174 us -> 163 us (0.937)
  the two profiles are of different devices: /device:TPU:99 before, /device:TPU:0 now
where the time goes in v4:
time: 163 us; the launch traced here: 161 us
  waiting for transfers between devices  77.3 us (47%)
  Pallas kernels  50.4 us (31%)
  starting transfers between devices  25.5 us (16%)
  local copies, waits for them, and re-layouts  6.05 us (4%)
    all_to_all x4, waiting for transfers between devices, exchange(): return lax.all_to_all(packed, ('band', 'lon'), 0, 0)  75.1 us
    pallas_call x1, Pallas kernels, attend(): pl.pallas_call(body, in_specs=[smem(), smem(), smem(), vmem(), vmem(), vm...  36.1 us
    all_to_all x4, starting transfers between devices, exchange(): return lax.all_to_all(packed, ('band', 'lon'), 0, 0)  19.6 us
    pallas_call x2, Pallas kernels, unpack_pair(): pl.pallas_call(body, grid=(2,), in_specs=[pl.BlockSpec((heads, step, cols...  5.22 us
    pallas_call x2, Pallas kernels, pack_pair(): pl.pallas_call(body, grid=(2,), in_specs=[block, block], out_specs=pl.Blo...  5.22 us
    unnamed x18, local copies, waits for them, and re-layouts  4.55 us
    pallas_call x1, Pallas kernels, add_home(): pl.pallas_call(body, grid=(4,), in_specs=[smem(), block, side(3 * HALO),...  3.95 us
    ppermute x1, starting transfers between devices, on_device(): other_reach = lax.ppermute(lon_reach, 'band', [(0, 1), (1, 0)])  3.38 us
  transfers between devices with their start and end apart: 9, of which 5 were waited for; matrix products, arithmetic and copies ran while one was open for 1% of the time, Pallas kernels for 6%

profile of v4, /device:TPU:0, one launch (start us, length us, event | category | flops | bytes accessed | tf_op | source)
XLA Modules:
  0.0 160.8 jit_solution(13361417059917542787)
XLA Ops:
  0.6 2.6 %shard_map.93 = bf16[16,8,48,128]{3,2,1,0:T(8,128)(2,1)} custom-call(bf16[8,48,1024]{2,1,0:T(8,128)(2,1)} %left_ref.2, bf16[8,48,1024]{2,1,0:T(8,128)(2,1)} %right_ref.2), custom_call_target="tpu_custom_call" | custom-call | tf_op jit(solution)/shard_map/pallas_call | solution.py:42
  3.3 7.5 %all-to-all-start = ((bf16[32,4,48,128]{3,2,1,0:T(8,128)(2,1)}), bf16[32,4,48,128]{3,2,1,0:T(8,128)(2,1)S(1)}, u32[]{:S(2)}, u32[]{:S(2)}) async-start(bf16[32,4,48,128]{3,2,1,0:T(8,128)(2,1)} %bitcast.18), calls=%async_computation | async-start | bytes 3145728 | tf_op jit(solution)/shard_map/all_to_all | solution.py:305
  10.8 3.4 %collective-permute-start = (s32[8]{0:T(128)S(1)}, s32[8]{0:T(128)S(1)}, u32[]{:S(2)}, u32[]{:S(2)}) collective-permute-start(s32[8]{0:T(128)S(1)} %copy-done.7), channel_id=1, source_target_pairs={{0,16},{16,0},{1,17},{17,1},{2,18},{18,2},{3,19},{19,3},{4,20},{20... | collective-permute-start | bytes 104 | tf_op jit(solution)/shard_map/ppermute | solution.py:330
  14.2 2.6 %shard_map.94 = bf16[16,8,48,128]{3,2,1,0:T(8,128)(2,1)} custom-call(bf16[8,48,1024]{2,1,0:T(8,128)(2,1)} %left_ref.3, bf16[8,48,1024]{2,1,0:T(8,128)(2,1)} %right_ref.3), custom_call_target="tpu_custom_call" | custom-call | tf_op jit(solution)/shard_map/pallas_call | solution.py:42
  16.8 17.9 %all-to-all-done = bf16[32,4,48,128]{3,2,1,0:T(8,128)(2,1)S(1)} async-done(((bf16[32,4,48,128]{3,2,1,0:T(8,128)(2,1)}), bf16[32,4,48,128]{3,2,1,0:T(8,128)(2,1)S(1)}, u32[]{:S(2)}, u32[]{:S(2)}) %all-to-all-start) | async-done | bytes 1572896 | tf_op jit(solution)/shard_map/all_to_all | solution.py:305
  34.7 4.0 %all-to-all-start.1 = ((bf16[32,4,48,128]{3,2,1,0:T(8,128)(2,1)}), bf16[32,4,48,128]{3,2,1,0:T(8,128)(2,1)S(1)}, u32[]{:S(2)}, u32[]{:S(2)}) async-start(bf16[32,4,48,128]{3,2,1,0:T(8,128)(2,1)} %bitcast.17), calls=%async_computation.1 | async-start | bytes 3145728 | tf_op jit(solution)/shard_map/all_to_all | solution.py:305
  38.7 0.2 collective-permute-start.1
  39.0 0.1 compare_and_fusion
  39.0 0.1 and.16
  39.1 0.1 fusion.1
  39.2 0.1 min.12
  39.3 0.7 gather_fusion
  40.0 0.5 log_select_fusion.logw_ref
  40.5 1.4 collective-permute-start.2
  42.0 0.1 constant_dynamic-slice_fusion
  42.0 0.6 reshape.94.reach_ref
  42.6 20.0 %all-to-all-done.1 = bf16[32,4,48,128]{3,2,1,0:T(8,128)(2,1)S(1)} async-done(((bf16[32,4,48,128]{3,2,1,0:T(8,128)(2,1)}), bf16[32,4,48,128]{3,2,1,0:T(8,128)(2,1)S(1)}, u32[]{:S(2)}, u32[]{:S(2)}) %all-to-all-start.1) | async-done | bytes 1572896 | tf_op jit(solution)/shard_map/all_to_all | solution.py:305
  62.7 1.1 copy-done.4
  63.8 36.1 %shard_map.95 = (bf16[2,16,4,48,128]{4,3,2,1,0:T(8,128)(2,1)}, bf16[2,16,4,48,128]{4,3,2,1,0:T(8,128)(2,1)}, bf16[16,6,48,128]{3,2,1,0:T(8,128)(2,1)}, bf16[16,2,48,128]{3,2,1,0:T(8,128)(2,1)}) custom-call(s32[1]{0:T(128)} %bitcast.half_ref, s32[8]{0:T(128)} %reshape.94.reach_ref, f32[16]{0:T(128)} %log_select_fusion.logw_ref, ...), custom_call_target="tpu_custom_call" | custom-call | flops 40000000000 | bytes 10000000 | tf_op jit(solution)/shard_map/pallas_call | solution.py:252
  99.9 4.1 %all-to-all-start.2 = ((bf16[32,4,48,128]{3,2,1,0:T(8,128)(2,1)}), bf16[32,4,48,128]{3,2,1,0:T(8,128)(2,1)S(1)}, u32[]{:S(2)}, u32[]{:S(2)}) async-start(bf16[32,4,48,128]{3,2,1,0:T(8,128)(2,1)} %bitcast.26), calls=%async_computation.2 | async-start | bytes 3145728 | tf_op jit(solution)/shard_map/all_to_all | solution.py:305
  104.0 0.2 collective-permute-start.3
  104.2 0.7 collective-permute-start.4
  104.9 2.2 %collective-permute-done.3.partner_ref = bf16[16,6,48,128]{3,2,1,0:T(8,128)(2,1)S(1)} collective-permute-done((bf16[16,6,48,128]{3,2,1,0:T(8,128)(2,1)}, bf16[16,6,48,128]{3,2,1,0:T(8,128)(2,1)S(1)}, u32[]{:S(2)}, u32[]{:S(2)}) %collective-permute-start.3) | collective-permute-done | bytes 1179680 | tf_op jit(solution)/shard_map/ppermute | solution.py:309
  107.1 1.0 copy-done.5
  108.2 3.9 %shard_map.97 = bf16[2,16,4,48,128]{4,3,2,1,0:T(8,128)(2,1)} custom-call(s32[1]{0:T(128)} %bitcast.half_ref, bf16[2,16,4,48,128]{4,3,2,1,0:T(8,128)(2,1)} %get-tuple-element.15.own_ref, bf16[16,6,48,128]{3,2,1,0:T(8,128)(2,1)} %copy-done.5, bf16[16,2,48,128]{3,2,1,0:T(8,128)(2,1)} %copy-done.6), custom_call_target="tpu_custom_call" | custom-call | tf_op jit(solution)/shard_map/pallas_call | solution.py:295
  112.1 15.8 %all-to-all-done.2 = bf16[32,4,48,128]{3,2,1,0:T(8,128)(2,1)S(1)} async-done(((bf16[32,4,48,128]{3,2,1,0:T(8,128)(2,1)}), bf16[32,4,48,128]{3,2,1,0:T(8,128)(2,1)S(1)}, u32[]{:S(2)}, u32[]{:S(2)}) %all-to-all-start.2) | async-done | bytes 1572896 | tf_op jit(solution)/shard_map/all_to_all | solution.py:305
  127.9 1.2 copy-done.1
  129.1 4.0 %all-to-all-start.3 = ((bf16[32,4,48,128]{3,2,1,0:T(8,128)(2,1)}), bf16[32,4,48,128]{3,2,1,0:T(8,128)(2,1)S(1)}, u32[]{:S(2)}, u32[]{:S(2)}) async-start(bf16[32,4,48,128]{3,2,1,0:T(8,128)(2,1)} %bitcast.20), calls=%async_computation.3 | async-start | bytes 3145728 | tf_op jit(solution)/shard_map/all_to_all | solution.py:305
  133.1 2.6 %shard_map.96 = (bf16[8,48,1024]{2,1,0:T(8,128)(2,1)}, bf16[8,48,1024]{2,1,0:T(8,128)(2,1)}) custom-call(bf16[16,8,48,128]{3,2,1,0:T(8,128)(2,1)} %bitcast.19), custom_call_target="tpu_custom_call" | custom-call | tf_op jit(solution)/shard_map/pallas_call | solution.py:66
  135.7 21.3 %all-to-all-done.3 = bf16[32,4,48,128]{3,2,1,0:T(8,128)(2,1)S(1)} async-done(((bf16[32,4,48,128]{3,2,1,0:T(8,128)(2,1)}), bf16[32,4,48,128]{3,2,1,0:T(8,128)(2,1)S(1)}, u32[]{:S(2)}, u32[]{:S(2)}) %all-to-all-start.3) | async-done | bytes 1572896 | tf_op jit(solution)/shard_map/all_to_all | solution.py:305
  157.0 1.2 copy-done.2
  158.2 2.6 %shard_map.98 = (bf16[8,48,1024]{2,1,0:T(8,128)(2,1)}, bf16[8,48,1024]{2,1,0:T(8,128)(2,1)}) custom-call(bf16[16,8,48,128]{3,2,1,0:T(8,128)(2,1)} %bitcast.21), custom_call_target="tpu_custom_call" | custom-call | tf_op jit(solution)/shard_map/pallas_call | solution.py:66
  (24 shorter events, 0.1 us)
Async XLA Ops:
  0.6 38.7 %copy-start = (f32[64]{0:T(128)S(1)}, f32[64]{0:T(128)}, u32[]{:S(2)}) copy-start(f32[64]{0:T(128)} %param.10) | copy-start | bytes 772
  3.3 7.5 %copy-start.7 = (s32[8]{0:T(128)S(1)}, s32[8]{0:T(128)}, u32[]{:S(2)}) copy-start(s32[8]{0:T(128)} %param.11) | copy-start | bytes 100
  3.3 31.5 %all-to-all-start = ((bf16[32,4,48,128]{3,2,1,0:T(8,128)(2,1)}), bf16[32,4,48,128]{3,2,1,0:T(8,128)(2,1)S(1)}, u32[]{:S(2)}, u32[]{:S(2)}) async-start(bf16[32,4,48,128]{3,2,1,0:T(8,128)(2,1)} %bitcast.18), calls=%async_computation | async-start | bytes 3145728 | tf_op jit(solution)/shard_map/all_to_all | solution.py:305
  10.8 31.1 %collective-permute-start = (s32[8]{0:T(128)S(1)}, s32[8]{0:T(128)S(1)}, u32[]{:S(2)}, u32[]{:S(2)}) collective-permute-start(s32[8]{0:T(128)S(1)} %copy-done.7), channel_id=1, source_target_pairs={{0,16},{16,0},{1,17},{17,1},{2,18},{18,2},{3,19},{19,3},{4,20},{20... | collective-permute-start | bytes 104 | tf_op jit(solution)/shard_map/ppermute | solution.py:330
  34.7 5.8 %copy-start.3 = (bf16[32,4,48,128]{3,2,1,0:T(8,128)(2,1)}, bf16[32,4,48,128]{3,2,1,0:T(8,128)(2,1)S(1)}, u32[]{:S(2)}) copy-start(bf16[32,4,48,128]{3,2,1,0:T(8,128)(2,1)S(1)} %all-to-all-done) | copy-start | bytes 4718596
  34.7 27.9 %all-to-all-start.1 = ((bf16[32,4,48,128]{3,2,1,0:T(8,128)(2,1)}), bf16[32,4,48,128]{3,2,1,0:T(8,128)(2,1)S(1)}, u32[]{:S(2)}, u32[]{:S(2)}) async-start(bf16[32,4,48,128]{3,2,1,0:T(8,128)(2,1)} %bitcast.17), calls=%async_computation.1 | async-start | bytes 3145728 | tf_op jit(solution)/shard_map/all_to_all | solution.py:305
  38.7 23.9 %collective-permute-start.1 = (bf16[2,16,4,48,128]{4,3,2,1,0:T(8,128)(2,1)S(1)}, bf16[2,16,4,48,128]{4,3,2,1,0:T(8,128)(2,1)}, u32[]{:S(2)}, u32[]{:S(2)}) collective-permute-start(bf16[2,16,4,48,128]{4,3,2,1,0:T(8,128)(2,1)S(1)} %bitcast.22), channel_id=1, source_target_pairs={{0,1},{1,0},{2,3},{3,2},{4,5},{5,4},{6,7},{7,6},{8,9},{9,8},{10,11... | collective-permute-start | bytes 4718600 | tf_op jit(solution)/shard_map/ppermute | solution.py:309
  40.5 22.1 %collective-permute-start.2 = (bf16[16,2,48,128]{3,2,1,0:T(8,128)(2,1)S(1)}, bf16[16,2,48,128]{3,2,1,0:T(8,128)(2,1)}, u32[]{:S(2)}, u32[]{:S(2)}) collective-permute-start(bf16[16,2,48,128]{3,2,1,0:T(8,128)(2,1)S(1)} %fusion), channel_id=1, source_target_pairs={{1,32},{32,1},{3,34},{34,3},{5,36},{36,5},{7,38},{38,7},{9,40},{40... | collective-permute-start | bytes 1179656 | tf_op jit(solution)/shard_map/ppermute | solution.py:319
  62.7 1.2 copy-start.4
  99.9 4.4 %copy-start.8 = (bf16[16,2,48,128]{3,2,1,0:T(8,128)(2,1)S(1)}, bf16[16,2,48,128]{3,2,1,0:T(8,128)(2,1)}, u32[]{:S(2)}) copy-start(bf16[16,2,48,128]{3,2,1,0:T(8,128)(2,1)} %get-tuple-element.17) | copy-start | bytes 1179652
  99.9 28.0 %all-to-all-start.2 = ((bf16[32,4,48,128]{3,2,1,0:T(8,128)(2,1)}), bf16[32,4,48,128]{3,2,1,0:T(8,128)(2,1)S(1)}, u32[]{:S(2)}, u32[]{:S(2)}) async-start(bf16[32,4,48,128]{3,2,1,0:T(8,128)(2,1)} %bitcast.26), calls=%async_computation.2 | async-start | bytes 3145728 | tf_op jit(solution)/shard_map/all_to_all | solution.py:305
  104.0 3.1 %collective-permute-start.3 = (bf16[16,6,48,128]{3,2,1,0:T(8,128)(2,1)}, bf16[16,6,48,128]{3,2,1,0:T(8,128)(2,1)S(1)}, u32[]{:S(2)}, u32[]{:S(2)}) collective-permute-start(bf16[16,6,48,128]{3,2,1,0:T(8,128)(2,1)} %get-tuple-element.16), channel_id=1, source_target_pairs={{0,1},{1,0},{2,3},{3,2},{4,5},{5,4},{6,7},{7,6},{8,9},{9,8},{10,11... | collective-permute-start | bytes 3538952 | tf_op jit(solution)/shard_map/ppermute | solution.py:309
  104.2 0.7 collective-permute-start.4
  104.9 2.2 %copy-start.6 = (bf16[16,2,48,128]{3,2,1,0:T(8,128)(2,1)}, bf16[16,2,48,128]{3,2,1,0:T(8,128)(2,1)S(1)}, u32[]{:S(2)}) copy-start(bf16[16,2,48,128]{3,2,1,0:T(8,128)(2,1)S(1)} %collective-permute-done.4.plane_ref) | copy-start | bytes 1179652
  107.1 1.0 copy-start.5
  127.9 1.2 copy-start.1
  129.1 27.9 %all-to-all-start.3 = ((bf16[32,4,48,128]{3,2,1,0:T(8,128)(2,1)}), bf16[32,4,48,128]{3,2,1,0:T(8,128)(2,1)S(1)}, u32[]{:S(2)}, u32[]{:S(2)}) async-start(bf16[32,4,48,128]{3,2,1,0:T(8,128)(2,1)} %bitcast.20), calls=%async_computation.3 | async-start | bytes 3145728 | tf_op jit(solution)/shard_map/all_to_all | solution.py:305
  157.0 1.2 copy-start.2

commit v5 on v4

--- a/solution.py
+++ b/solution.py
@@ -12,10 +12,11 @@
 HALF = 64
 TAPS = 2 * HALO + 2
 WINDOW = HALF + 2 * REACH
-INTERLEAVE = 4
+INTERLEAVE = 6
 CLASSES = (48, 64, 80, 96)
 FAR = -1e30
-VMEM_BYTES = 56 * 1024 * 1024
+VMEM_BYTES = 60 * 1024 * 1024
+SMALL_BYTES = 8 * 1024 * 1024
 NT = (((1,), (1,)), ((), ()))
 
 
@@ -25,6 +26,10 @@
 
 def smem():
     return pl.BlockSpec(memory_space=pltpu.SMEM)
+
+
+def params(limit):
+    return pltpu.CompilerParams(vmem_limit_bytes=limit)
 
 
 def pack_pair(left, right):
@@ -45,6 +50,7 @@
         in_specs=[block, block],
         out_specs=pl.BlockSpec((heads, step, cols, 2 * HEAD_DIM), lambda i: (0, i, 0, 0)),
         out_shape=jax.ShapeDtypeStruct((heads, rows, cols, 2 * HEAD_DIM), left.dtype),
+        compiler_params=params(SMALL_BYTES),
     )(left, right)
 
 
@@ -69,6 +75,7 @@
         in_specs=[pl.BlockSpec((heads, step, cols, lanes), lambda i: (0, i, 0, 0))],
         out_specs=[out, out],
         out_shape=[shape, shape],
+        compiler_params=params(SMALL_BYTES),
     )(packed)
 
 
@@ -263,7 +270,7 @@
             pltpu.VMEM((TAPS, WINDOW, 2 * HALF), jnp.float32),
             pltpu.VMEM((2 * rows, ring, lanes), jnp.bfloat16),
         ],
-        compiler_params=pltpu.CompilerParams(vmem_limit_bytes=VMEM_BYTES),
+        compiler_params=params(VMEM_BYTES),
         cost_estimate=pl.CostEstimate(flops=40_000_000_000, bytes_accessed=10_000_000, transcendentals=5_000_000),
     )(second_half, reach, log_weight, kv, kv_partner, kv_plane, qc)
 
@@ -298,6 +305,7 @@
         in_specs=[smem(), block, side(3 * HALO), side(HALO)],
         out_specs=block,
         out_shape=jax.ShapeDtypeStruct(own.shape, own.dtype),
+        compiler_params=params(SMALL_BYTES),
     )(second_half, own, partner, plane)
 
 

time: 163 us -> 159 us (0.975); the launches traced: 161 us -> 159 us
  Pallas kernels: 50.4 us -> 44.4 us
  waiting for transfers between devices: 77.3 us -> 82.4 us
    all_to_all x4, waiting for transfers between devices: 75.1 us -> 80.2 us  [exchange(): return lax.all_to_all(packed, ('band', 'lon'), 0, 0)]
    pallas_call x2, Pallas kernels: 5.22 us -> 2.98 us  [pack_pair(): pl.pallas_call(body, grid=(2,), in_specs=[block, block], out_specs=pl.Blo...]
    pallas_call x2, Pallas kernels: 5.22 us -> 3.19 us  [unpack_pair(): pl.pallas_call(body, grid=(2,), in_specs=[pl.BlockSpec((heads, step, cols...]
    pallas_call x1, Pallas kernels: 3.95 us -> 1.97 us  [add_home(): pl.pallas_call(body, grid=(4,), in_specs=[smem(), block, side(3 * HALO),...]
    unnamed x18 -> x20, local copies, waits for them, and re-layouts: 4.55 us -> 3.49 us
  transfers between devices with their start and end apart: 9 -> 9, of which waited for: 5 -> 5; matrix products, arithmetic and copies ran while one was open for 1% -> 1% of each run, Pallas kernels for 6% -> 3%
where the time goes in v5:
time: 159 us
  waiting for transfers between devices  82.4 us (52%)
  Pallas kernels  44.4 us (28%)
  starting transfers between devices  25.5 us (16%)
  local copies, waits for them, and re-layouts  4.99 us (3%)
    all_to_all x4, waiting for transfers between devices, exchange(): return lax.all_to_all(packed, ('band', 'lon'), 0, 0)  80.2 us
    pallas_call x1, Pallas kernels, attend(): pl.pallas_call(body, in_specs=[smem(), smem(), smem(), vmem(), vmem(), vm...  36.2 us
    all_to_all x4, starting transfers between devices, exchange(): return lax.all_to_all(packed, ('band', 'lon'), 0, 0)  19.6 us
    unnamed x20, local copies, waits for them, and re-layouts  3.49 us
    ppermute x1, starting transfers between devices, on_device(): other_reach = lax.ppermute(lon_reach, 'band', [(0, 1), (1, 0)])  3.38 us
    pallas_call x2, Pallas kernels, unpack_pair(): pl.pallas_call(body, grid=(2,), in_specs=[pl.BlockSpec((heads, step, cols...  3.19 us
  transfers between devices with their start and end apart: 9, of which 5 were waited for; matrix products, arithmetic and copies ran while one was open for 1% of the time, Pallas kernels for 3%

profile of v5, /device:TPU:0, one launch (start us, length us, event | category | flops | bytes accessed | tf_op | source)
XLA Modules:
  0.0 158.8 jit_solution(12713864243419512878)
XLA Ops:
  0.6 0.0 copy-start
  0.7 1.1 copy-done.2
  1.8 1.1 copy-done.3
  2.9 1.5 shard_map.93
  4.4 7.5 %all-to-all-start = ((bf16[32,4,48,128]{3,2,1,0:T(8,128)(2,1)}), bf16[32,4,48,128]{3,2,1,0:T(8,128)(2,1)S(1)}, u32[]{:S(2)}, u32[]{:S(2)}) async-start(bf16[32,4,48,128]{3,2,1,0:T(8,128)(2,1)} %bitcast.4), calls=%async_computation | async-start | bytes 3145728 | tf_op jit(solution)/shard_map/all_to_all | solution.py:313
  12.0 3.4 %collective-permute-start = (s32[8]{0:T(128)S(1)}, s32[8]{0:T(128)S(1)}, u32[]{:S(2)}, u32[]{:S(2)}) collective-permute-start(s32[8]{0:T(128)S(1)} %copy-done.8), channel_id=1, source_target_pairs={{0,16},{16,0},{1,17},{17,1},{2,18},{18,2},{3,19},{19,3},{4,20},{20... | collective-permute-start | bytes 104 | tf_op jit(solution)/shard_map/ppermute | solution.py:338
  15.4 1.5 shard_map.94
  16.9 19.0 %all-to-all-done = bf16[32,4,48,128]{3,2,1,0:T(8,128)(2,1)S(1)} async-done(((bf16[32,4,48,128]{3,2,1,0:T(8,128)(2,1)}), bf16[32,4,48,128]{3,2,1,0:T(8,128)(2,1)S(1)}, u32[]{:S(2)}, u32[]{:S(2)}) %all-to-all-start) | async-done | bytes 1572896 | tf_op jit(solution)/shard_map/all_to_all | solution.py:313
  35.9 4.0 %all-to-all-start.1 = ((bf16[32,4,48,128]{3,2,1,0:T(8,128)(2,1)}), bf16[32,4,48,128]{3,2,1,0:T(8,128)(2,1)S(1)}, u32[]{:S(2)}, u32[]{:S(2)}) async-start(bf16[32,4,48,128]{3,2,1,0:T(8,128)(2,1)} %bitcast.7), calls=%async_computation.1 | async-start | bytes 3145728 | tf_op jit(solution)/shard_map/all_to_all | solution.py:313
  39.9 0.2 collective-permute-start.1
  40.1 0.1 compare_and_fusion
  40.2 0.1 and.16
  40.3 0.1 fusion.1
  40.3 0.1 min.12
  40.5 0.7 gather_fusion
  41.1 0.5 log_select_fusion.logw_ref
  41.7 1.4 collective-permute-start.2
  43.1 0.1 constant_dynamic-slice_fusion
  43.2 0.6 reshape.94.reach_ref
  43.8 20.0 %all-to-all-done.1 = bf16[32,4,48,128]{3,2,1,0:T(8,128)(2,1)S(1)} async-done(((bf16[32,4,48,128]{3,2,1,0:T(8,128)(2,1)}), bf16[32,4,48,128]{3,2,1,0:T(8,128)(2,1)S(1)}, u32[]{:S(2)}, u32[]{:S(2)}) %all-to-all-start.1) | async-done | bytes 1572896 | tf_op jit(solution)/shard_map/all_to_all | solution.py:313
  63.8 1.2 copy-done.7
  65.0 36.2 %shard_map.95 = (bf16[2,16,4,48,128]{4,3,2,1,0:T(8,128)(2,1)}, bf16[2,16,4,48,128]{4,3,2,1,0:T(8,128)(2,1)}, bf16[16,6,48,128]{3,2,1,0:T(8,128)(2,1)}, bf16[16,2,48,128]{3,2,1,0:T(8,128)(2,1)}) custom-call(s32[1]{0:T(128)} %bitcast.half_ref, s32[8]{0:T(128)} %reshape.94.reach_ref, f32[16]{0:T(128)} %log_select_fusion.logw_ref, ...), custom_call_target="tpu_custom_call" | custom-call | flops 40000000000 | bytes 10000000 | tf_op jit(solution)/shard_map/pallas_call | solution.py:259
  101.2 4.1 %all-to-all-start.2 = ((bf16[32,4,48,128]{3,2,1,0:T(8,128)(2,1)}), bf16[32,4,48,128]{3,2,1,0:T(8,128)(2,1)S(1)}, u32[]{:S(2)}, u32[]{:S(2)}) async-start(bf16[32,4,48,128]{3,2,1,0:T(8,128)(2,1)} %bitcast.23), calls=%async_computation.2 | async-start | bytes 3145728 | tf_op jit(solution)/shard_map/all_to_all | solution.py:313
  105.4 0.2 collective-permute-start.3
  105.6 0.7 collective-permute-start.4
  106.3 2.2 %collective-permute-done.3.partner_ref = bf16[16,6,48,128]{3,2,1,0:T(8,128)(2,1)S(1)} collective-permute-done((bf16[16,6,48,128]{3,2,1,0:T(8,128)(2,1)}, bf16[16,6,48,128]{3,2,1,0:T(8,128)(2,1)S(1)}, u32[]{:S(2)}, u32[]{:S(2)}) %collective-permute-start.3) | collective-permute-done | bytes 1179680 | tf_op jit(solution)/shard_map/ppermute | solution.py:317
  108.5 2.0 %shard_map.97 = bf16[2,16,4,48,128]{4,3,2,1,0:T(8,128)(2,1)} custom-call(s32[1]{0:T(128)} %bitcast.half_ref, bf16[2,16,4,48,128]{4,3,2,1,0:T(8,128)(2,1)S(1)} %copy-done.1, bf16[16,6,48,128]{3,2,1,0:T(8,128)(2,1)S(1)} %collective-permute-done.3.partner_ref, bf16[16,2,48,128]{3,2,1,0:T(8,128)(2,1)S(1)} %collective-permute-done.4.plane_ref), custom_call_target="tpu_custom_call" | custom-call | tf_op jit(solution)/shard_map/pallas_call | solution.py:302
  110.5 18.8 %all-to-all-done.2 = bf16[32,4,48,128]{3,2,1,0:T(8,128)(2,1)S(1)} async-done(((bf16[32,4,48,128]{3,2,1,0:T(8,128)(2,1)}), bf16[32,4,48,128]{3,2,1,0:T(8,128)(2,1)S(1)}, u32[]{:S(2)}, u32[]{:S(2)}) %all-to-all-start.2) | async-done | bytes 1572896 | tf_op jit(solution)/shard_map/all_to_all | solution.py:313
  129.3 4.0 %all-to-all-start.3 = ((bf16[32,4,48,128]{3,2,1,0:T(8,128)(2,1)}), bf16[32,4,48,128]{3,2,1,0:T(8,128)(2,1)S(1)}, u32[]{:S(2)}, u32[]{:S(2)}) async-start(bf16[32,4,48,128]{3,2,1,0:T(8,128)(2,1)} %bitcast.11), calls=%async_computation.3 | async-start | bytes 3145728 | tf_op jit(solution)/shard_map/all_to_all | solution.py:313
  133.3 1.6 %shard_map.96 = (bf16[8,48,1024]{2,1,0:T(8,128)(2,1)}, bf16[8,48,1024]{2,1,0:T(8,128)(2,1)}) custom-call(bf16[16,8,48,128]{3,2,1,0:T(8,128)(2,1)S(1)} %bitcast.17), custom_call_target="tpu_custom_call" | custom-call | tf_op jit(solution)/shard_map/pallas_call | solution.py:72
  134.9 22.3 %all-to-all-done.3 = bf16[32,4,48,128]{3,2,1,0:T(8,128)(2,1)S(1)} async-done(((bf16[32,4,48,128]{3,2,1,0:T(8,128)(2,1)}), bf16[32,4,48,128]{3,2,1,0:T(8,128)(2,1)S(1)}, u32[]{:S(2)}, u32[]{:S(2)}) %all-to-all-start.3) | async-done | bytes 1572896 | tf_op jit(solution)/shard_map/all_to_all | solution.py:313
  157.2 1.6 %shard_map.98 = (bf16[8,48,1024]{2,1,0:T(8,128)(2,1)}, bf16[8,48,1024]{2,1,0:T(8,128)(2,1)}) custom-call(bf16[16,8,48,128]{3,2,1,0:T(8,128)(2,1)S(1)} %bitcast.18), custom_call_target="tpu_custom_call" | custom-call | tf_op jit(solution)/shard_map/pallas_call | solution.py:72
  (26 shorter events, 0.1 us)
Async XLA Ops:
  0.6 39.8 %copy-start = (f32[64]{0:T(128)S(1)}, f32[64]{0:T(128)}, u32[]{:S(2)}) copy-start(f32[64]{0:T(128)} %param.10) | copy-start | bytes 772
  0.6 1.1 copy-start.2
  1.8 1.1 copy-start.3
  4.4 7.6 %copy-start.8 = (s32[8]{0:T(128)S(1)}, s32[8]{0:T(128)}, u32[]{:S(2)}) copy-start(s32[8]{0:T(128)} %param.11) | copy-start | bytes 100
  4.4 10.9 %copy-start.4 = (bf16[8,48,1024]{2,1,0:T(8,128)(2,1)S(1)}, bf16[8,48,1024]{2,1,0:T(8,128)(2,1)}, u32[]{:S(2)}) copy-start(bf16[8,48,1024]{2,1,0:T(8,128)(2,1)} %left_ref.3) | copy-start | bytes 2359300
  4.4 10.9 %copy-start.5 = (bf16[8,48,1024]{2,1,0:T(8,128)(2,1)S(1)}, bf16[8,48,1024]{2,1,0:T(8,128)(2,1)}, u32[]{:S(2)}) copy-start(bf16[8,48,1024]{2,1,0:T(8,128)(2,1)} %right_ref.3) | copy-start | bytes 2359300
  4.4 31.5 %all-to-all-start = ((bf16[32,4,48,128]{3,2,1,0:T(8,128)(2,1)}), bf16[32,4,48,128]{3,2,1,0:T(8,128)(2,1)S(1)}, u32[]{:S(2)}, u32[]{:S(2)}) async-start(bf16[32,4,48,128]{3,2,1,0:T(8,128)(2,1)} %bitcast.4), calls=%async_computation | async-start | bytes 3145728 | tf_op jit(solution)/shard_map/all_to_all | solution.py:313
  12.0 31.1 %collective-permute-start = (s32[8]{0:T(128)S(1)}, s32[8]{0:T(128)S(1)}, u32[]{:S(2)}, u32[]{:S(2)}) collective-permute-start(s32[8]{0:T(128)S(1)} %copy-done.8), channel_id=1, source_target_pairs={{0,16},{16,0},{1,17},{17,1},{2,18},{18,2},{3,19},{19,3},{4,20},{20... | collective-permute-start | bytes 104 | tf_op jit(solution)/shard_map/ppermute | solution.py:338
  35.9 5.8 %copy-start.6 = (bf16[32,4,48,128]{3,2,1,0:T(8,128)(2,1)}, bf16[32,4,48,128]{3,2,1,0:T(8,128)(2,1)S(1)}, u32[]{:S(2)}) copy-start(bf16[32,4,48,128]{3,2,1,0:T(8,128)(2,1)S(1)} %all-to-all-done) | copy-start | bytes 4718596
  35.9 27.9 %all-to-all-start.1 = ((bf16[32,4,48,128]{3,2,1,0:T(8,128)(2,1)}), bf16[32,4,48,128]{3,2,1,0:T(8,128)(2,1)S(1)}, u32[]{:S(2)}, u32[]{:S(2)}) async-start(bf16[32,4,48,128]{3,2,1,0:T(8,128)(2,1)} %bitcast.7), calls=%async_computation.1 | async-start | bytes 3145728 | tf_op jit(solution)/shard_map/all_to_all | solution.py:313
  39.9 23.9 %collective-permute-start.1 = (bf16[2,16,4,48,128]{4,3,2,1,0:T(8,128)(2,1)S(1)}, bf16[2,16,4,48,128]{4,3,2,1,0:T(8,128)(2,1)}, u32[]{:S(2)}, u32[]{:S(2)}) collective-permute-start(bf16[2,16,4,48,128]{4,3,2,1,0:T(8,128)(2,1)S(1)} %bitcast.19), channel_id=1, source_target_pairs={{0,1},{1,0},{2,3},{3,2},{4,5},{5,4},{6,7},{7,6},{8,9},{9,8},{10,11... | collective-permute-start | bytes 4718600 | tf_op jit(solution)/shard_map/ppermute | solution.py:317
  41.7 22.1 %collective-permute-start.2 = (bf16[16,2,48,128]{3,2,1,0:T(8,128)(2,1)S(1)}, bf16[16,2,48,128]{3,2,1,0:T(8,128)(2,1)}, u32[]{:S(2)}, u32[]{:S(2)}) collective-permute-start(bf16[16,2,48,128]{3,2,1,0:T(8,128)(2,1)S(1)} %fusion), channel_id=1, source_target_pairs={{1,32},{32,1},{3,34},{34,3},{5,36},{36,5},{7,38},{38,7},{9,40},{40... | collective-permute-start | bytes 1179656 | tf_op jit(solution)/shard_map/ppermute | solution.py:327
  63.8 1.2 copy-start.7
  101.2 4.4 %copy-start.9 = (bf16[16,2,48,128]{3,2,1,0:T(8,128)(2,1)S(1)}, bf16[16,2,48,128]{3,2,1,0:T(8,128)(2,1)}, u32[]{:S(2)}) copy-start(bf16[16,2,48,128]{3,2,1,0:T(8,128)(2,1)} %get-tuple-element.17) | copy-start | bytes 1179652
  101.2 7.3 %copy-start.1 = (bf16[2,16,4,48,128]{4,3,2,1,0:T(8,128)(2,1)S(1)}, bf16[2,16,4,48,128]{4,3,2,1,0:T(8,128)(2,1)}, u32[]{:S(2)}) copy-start(bf16[2,16,4,48,128]{4,3,2,1,0:T(8,128)(2,1)} %get-tuple-element.15.own_ref) | copy-start | bytes 4718596
  101.2 28.1 %all-to-all-start.2 = ((bf16[32,4,48,128]{3,2,1,0:T(8,128)(2,1)}), bf16[32,4,48,128]{3,2,1,0:T(8,128)(2,1)S(1)}, u32[]{:S(2)}, u32[]{:S(2)}) async-start(bf16[32,4,48,128]{3,2,1,0:T(8,128)(2,1)} %bitcast.23), calls=%async_computation.2 | async-start | bytes 3145728 | tf_op jit(solution)/shard_map/all_to_all | solution.py:313
  105.4 3.1 %collective-permute-start.3 = (bf16[16,6,48,128]{3,2,1,0:T(8,128)(2,1)}, bf16[16,6,48,128]{3,2,1,0:T(8,128)(2,1)S(1)}, u32[]{:S(2)}, u32[]{:S(2)}) collective-permute-start(bf16[16,6,48,128]{3,2,1,0:T(8,128)(2,1)} %get-tuple-element.16), channel_id=1, source_target_pairs={{0,1},{1,0},{2,3},{3,2},{4,5},{5,4},{6,7},{7,6},{8,9},{9,8},{10,11... | collective-permute-start | bytes 3538952 | tf_op jit(solution)/shard_map/ppermute | solution.py:317
  105.6 0.7 collective-permute-start.4
  129.3 27.9 %all-to-all-start.3 = ((bf16[32,4,48,128]{3,2,1,0:T(8,128)(2,1)}), bf16[32,4,48,128]{3,2,1,0:T(8,128)(2,1)S(1)}, u32[]{:S(2)}, u32[]{:S(2)}) async-start(bf16[32,4,48,128]{3,2,1,0:T(8,128)(2,1)} %bitcast.11), calls=%async_computation.3 | async-start | bytes 3145728 | tf_op jit(solution)/shard_map/all_to_all | solution.py:313

commit v6 on v5

--- a/solution.py
+++ b/solution.py
@@ -15,8 +15,9 @@
 INTERLEAVE = 6
 CLASSES = (48, 64, 80, 96)
 FAR = -1e30
-VMEM_BYTES = 60 * 1024 * 1024
+VMEM_BYTES = 52 * 1024 * 1024
 SMALL_BYTES = 8 * 1024 * 1024
+LARGE_BYTES = 60 * 1024 * 1024
 NT = (((1,), (1,)), ((), ()))
 
 
@@ -50,7 +51,7 @@
         in_specs=[block, block],
         out_specs=pl.BlockSpec((heads, step, cols, 2 * HEAD_DIM), lambda i: (0, i, 0, 0)),
         out_shape=jax.ShapeDtypeStruct((heads, rows, cols, 2 * HEAD_DIM), left.dtype),
-        compiler_params=params(SMALL_BYTES),
+        compiler_params=params(LARGE_BYTES),
     )(left, right)
 
 

time: 159 us -> 161 us (1.013); the launches traced: 159 us -> 159 us
  Pallas kernels: 44.4 us -> 47 us
  local copies, waits for them, and re-layouts: 4.99 us -> 3.17 us
    pallas_call x2, Pallas kernels: 2.98 us -> 5.18 us  [pack_pair(): pl.pallas_call(body, grid=(2,), in_specs=[block, block], out_specs=pl.Blo...]
    unnamed x20 -> x12, local copies, waits for them, and re-layouts: 3.49 us -> 2.18 us
  transfers between devices with their start and end apart: 9 -> 9, of which waited for: 5 -> 5; matrix products, arithmetic and copies ran while one was open for 1% -> 1% of each run, Pallas kernels for 3% -> 4%
where the time goes in v6:
time: 161 us; the launch traced here: 159 us
  waiting for transfers between devices  82.3 us (51%)
  Pallas kernels  47 us (29%)
  starting transfers between devices  24.8 us (15%)
  local copies, waits for them, and re-layouts  3.17 us (2%)
    all_to_all x4, waiting for transfers between devices, exchange(): return lax.all_to_all(packed, ('band', 'lon'), 0, 0)  80.1 us
    pallas_call x1, Pallas kernels, attend(): pl.pallas_call(body, in_specs=[smem(), smem(), smem(), vmem(), vmem(), vm...  36.6 us
    all_to_all x4, starting transfers between devices, exchange(): return lax.all_to_all(packed, ('band', 'lon'), 0, 0)  19.6 us
    pallas_call x2, Pallas kernels, pack_pair(): pl.pallas_call(body, grid=(2,), in_specs=[block, block], out_specs=pl.Blo...  5.18 us
    ppermute x1, starting transfers between devices, on_device(): other_reach = lax.ppermute(lon_reach, 'band', [(0, 1), (1, 0)])  3.38 us
  transfers between devices with their start and end apart: 9, of which 5 were waited for; matrix products, arithmetic and copies ran while one was open for 1% of the time, Pallas kernels for 4%

profile of v6, /device:TPU:0, one launch (start us, length us, event | category | flops | bytes accessed | tf_op | source)
XLA Modules:
  0.0 159.0 jit_solution(7562964689067987076)
XLA Ops:
  0.6 0.0 copy-start
  0.6 2.6 %shard_map.93 = bf16[16,8,48,128]{3,2,1,0:T(8,128)(2,1)} custom-call(bf16[8,48,1024]{2,1,0:T(8,128)(2,1)} %left_ref.2, bf16[8,48,1024]{2,1,0:T(8,128)(2,1)} %right_ref.2), custom_call_target="tpu_custom_call" | custom-call | tf_op jit(solution)/shard_map/pallas_call | solution.py:48
  3.2 7.5 %all-to-all-start = ((bf16[32,4,48,128]{3,2,1,0:T(8,128)(2,1)}), bf16[32,4,48,128]{3,2,1,0:T(8,128)(2,1)S(1)}, u32[]{:S(2)}, u32[]{:S(2)}) async-start(bf16[32,4,48,128]{3,2,1,0:T(8,128)(2,1)} %bitcast.20), calls=%async_computation | async-start | bytes 3145728 | tf_op jit(solution)/shard_map/all_to_all | solution.py:314
  10.8 3.4 %collective-permute-start = (s32[8]{0:T(128)S(1)}, s32[8]{0:T(128)S(1)}, u32[]{:S(2)}, u32[]{:S(2)}) collective-permute-start(s32[8]{0:T(128)S(1)} %copy-done.5), channel_id=1, source_target_pairs={{0,16},{16,0},{1,17},{17,1},{2,18},{18,2},{3,19},{19,3},{4,20},{20... | collective-permute-start | bytes 104 | tf_op jit(solution)/shard_map/ppermute | solution.py:339
  14.2 2.6 %shard_map.94 = bf16[16,8,48,128]{3,2,1,0:T(8,128)(2,1)} custom-call(bf16[8,48,1024]{2,1,0:T(8,128)(2,1)} %left_ref.3, bf16[8,48,1024]{2,1,0:T(8,128)(2,1)} %right_ref.3), custom_call_target="tpu_custom_call" | custom-call | tf_op jit(solution)/shard_map/pallas_call | solution.py:48
  16.8 17.9 %all-to-all-done = bf16[32,4,48,128]{3,2,1,0:T(8,128)(2,1)S(1)} async-done(((bf16[32,4,48,128]{3,2,1,0:T(8,128)(2,1)}), bf16[32,4,48,128]{3,2,1,0:T(8,128)(2,1)S(1)}, u32[]{:S(2)}, u32[]{:S(2)}) %all-to-all-start) | async-done | bytes 1572896 | tf_op jit(solution)/shard_map/all_to_all | solution.py:314
  34.7 4.0 %all-to-all-start.1 = ((bf16[32,4,48,128]{3,2,1,0:T(8,128)(2,1)}), bf16[32,4,48,128]{3,2,1,0:T(8,128)(2,1)S(1)}, u32[]{:S(2)}, u32[]{:S(2)}) async-start(bf16[32,4,48,128]{3,2,1,0:T(8,128)(2,1)} %bitcast.19), calls=%async_computation.1 | async-start | bytes 3145728 | tf_op jit(solution)/shard_map/all_to_all | solution.py:314
  38.7 0.2 collective-permute-start.1
  38.9 0.1 compare_and_fusion
  39.0 0.1 and.16
  39.1 0.1 fusion.1
  39.2 0.1 min.12
  39.3 0.7 gather_fusion
  40.0 0.8 fusion
  40.8 0.7 collective-permute-start.2
  41.4 0.0 collective-permute-done
  41.5 0.1 constant_dynamic-slice_fusion
  41.6 0.1 reshape.94.reach_ref
  41.6 21.0 %all-to-all-done.1 = bf16[32,4,48,128]{3,2,1,0:T(8,128)(2,1)S(1)} async-done(((bf16[32,4,48,128]{3,2,1,0:T(8,128)(2,1)}), bf16[32,4,48,128]{3,2,1,0:T(8,128)(2,1)S(1)}, u32[]{:S(2)}, u32[]{:S(2)}) %all-to-all-start.1) | async-done | bytes 1572896 | tf_op jit(solution)/shard_map/all_to_all | solution.py:314
  62.6 1.1 copy-done.4
  63.8 36.6 %shard_map.95 = (bf16[2,16,4,48,128]{4,3,2,1,0:T(8,128)(2,1)}, bf16[2,16,4,48,128]{4,3,2,1,0:T(8,128)(2,1)}, bf16[16,6,48,128]{3,2,1,0:T(8,128)(2,1)S(1)}, bf16[16,2,48,128]{3,2,1,0:T(8,128)(2,1)S(1)}) custom-call(s32[1]{0:T(128)} %bitcast.half_ref, s32[8]{0:T(128)S(1)} %reshape.94.reach_ref, f32[16]{0:T(128)S(1)} %log_select_fusion.logw_ref, ...), custom_call_target="tpu_custom_call" | custom-call | flops 40000000000 | bytes 10000000 | tf_op jit(solution)/shard_map/pallas_call | solution.py:260
  100.4 1.0 copy-done.2
  101.4 4.1 %all-to-all-start.2 = ((bf16[32,4,48,128]{3,2,1,0:T(8,128)(2,1)}), bf16[32,4,48,128]{3,2,1,0:T(8,128)(2,1)S(1)}, u32[]{:S(2)}, u32[]{:S(2)}) async-start(bf16[32,4,48,128]{3,2,1,0:T(8,128)(2,1)} %bitcast.25), calls=%async_computation.2 | async-start | bytes 3145728 | tf_op jit(solution)/shard_map/all_to_all | solution.py:314
  105.5 0.2 collective-permute-start.3
  105.8 0.7 collective-permute-start.4
  106.5 2.2 %collective-permute-done.3.partner_ref = bf16[16,6,48,128]{3,2,1,0:T(8,128)(2,1)S(1)} collective-permute-done((bf16[16,6,48,128]{3,2,1,0:T(8,128)(2,1)}, bf16[16,6,48,128]{3,2,1,0:T(8,128)(2,1)S(1)}, u32[]{:S(2)}, u32[]{:S(2)}) %collective-permute-start.3) | collective-permute-done | bytes 1179680 | tf_op jit(solution)/shard_map/ppermute | solution.py:318
  108.7 2.0 %shard_map.97 = bf16[2,16,4,48,128]{4,3,2,1,0:T(8,128)(2,1)} custom-call(s32[1]{0:T(128)} %bitcast.half_ref, bf16[2,16,4,48,128]{4,3,2,1,0:T(8,128)(2,1)S(1)} %copy-done.1, bf16[16,6,48,128]{3,2,1,0:T(8,128)(2,1)S(1)} %collective-permute-done.3.partner_ref, bf16[16,2,48,128]{3,2,1,0:T(8,128)(2,1)S(1)} %collective-permute-done.4.plane_ref), custom_call_target="tpu_custom_call" | custom-call | tf_op jit(solution)/shard_map/pallas_call | solution.py:303
  110.7 18.8 %all-to-all-done.2 = bf16[32,4,48,128]{3,2,1,0:T(8,128)(2,1)S(1)} async-done(((bf16[32,4,48,128]{3,2,1,0:T(8,128)(2,1)}), bf16[32,4,48,128]{3,2,1,0:T(8,128)(2,1)S(1)}, u32[]{:S(2)}, u32[]{:S(2)}) %all-to-all-start.2) | async-done | bytes 1572896 | tf_op jit(solution)/shard_map/all_to_all | solution.py:314
  129.5 4.0 %all-to-all-start.3 = ((bf16[32,4,48,128]{3,2,1,0:T(8,128)(2,1)}), bf16[32,4,48,128]{3,2,1,0:T(8,128)(2,1)S(1)}, u32[]{:S(2)}, u32[]{:S(2)}) async-start(bf16[32,4,48,128]{3,2,1,0:T(8,128)(2,1)} %bitcast.11), calls=%async_computation.3 | async-start | bytes 3145728 | tf_op jit(solution)/shard_map/all_to_all | solution.py:314
  133.4 1.6 %shard_map.96 = (bf16[8,48,1024]{2,1,0:T(8,128)(2,1)}, bf16[8,48,1024]{2,1,0:T(8,128)(2,1)}) custom-call(bf16[16,8,48,128]{3,2,1,0:T(8,128)(2,1)S(1)} %bitcast.17), custom_call_target="tpu_custom_call" | custom-call | tf_op jit(solution)/shard_map/pallas_call | solution.py:73
  135.1 22.3 %all-to-all-done.3 = bf16[32,4,48,128]{3,2,1,0:T(8,128)(2,1)S(1)} async-done(((bf16[32,4,48,128]{3,2,1,0:T(8,128)(2,1)}), bf16[32,4,48,128]{3,2,1,0:T(8,128)(2,1)S(1)}, u32[]{:S(2)}, u32[]{:S(2)}) %all-to-all-start.3) | async-done | bytes 1572896 | tf_op jit(solution)/shard_map/all_to_all | solution.py:314
  157.4 1.6 shard_map.98
  (18 shorter events, 0.1 us)
Async XLA Ops:
  0.6 38.7 %copy-start = (f32[64]{0:T(128)S(1)}, f32[64]{0:T(128)}, u32[]{:S(2)}) copy-start(f32[64]{0:T(128)} %param.10) | copy-start | bytes 772
  3.2 7.5 %copy-start.5 = (s32[8]{0:T(128)S(1)}, s32[8]{0:T(128)}, u32[]{:S(2)}) copy-start(s32[8]{0:T(128)} %param.11) | copy-start | bytes 100
  3.2 31.5 %all-to-all-start = ((bf16[32,4,48,128]{3,2,1,0:T(8,128)(2,1)}), bf16[32,4,48,128]{3,2,1,0:T(8,128)(2,1)S(1)}, u32[]{:S(2)}, u32[]{:S(2)}) async-start(bf16[32,4,48,128]{3,2,1,0:T(8,128)(2,1)} %bitcast.20), calls=%async_computation | async-start | bytes 3145728 | tf_op jit(solution)/shard_map/all_to_all | solution.py:314
  10.8 30.6 %collective-permute-start = (s32[8]{0:T(128)S(1)}, s32[8]{0:T(128)S(1)}, u32[]{:S(2)}, u32[]{:S(2)}) collective-permute-start(s32[8]{0:T(128)S(1)} %copy-done.5), channel_id=1, source_target_pairs={{0,16},{16,0},{1,17},{17,1},{2,18},{18,2},{3,19},{19,3},{4,20},{20... | collective-permute-start | bytes 104 | tf_op jit(solution)/shard_map/ppermute | solution.py:339
  34.7 5.2 %copy-start.3 = (bf16[32,4,48,128]{3,2,1,0:T(8,128)(2,1)}, bf16[32,4,48,128]{3,2,1,0:T(8,128)(2,1)S(1)}, u32[]{:S(2)}) copy-start(bf16[32,4,48,128]{3,2,1,0:T(8,128)(2,1)S(1)} %all-to-all-done) | copy-start | bytes 4718596
  34.7 27.9 %all-to-all-start.1 = ((bf16[32,4,48,128]{3,2,1,0:T(8,128)(2,1)}), bf16[32,4,48,128]{3,2,1,0:T(8,128)(2,1)S(1)}, u32[]{:S(2)}, u32[]{:S(2)}) async-start(bf16[32,4,48,128]{3,2,1,0:T(8,128)(2,1)} %bitcast.19), calls=%async_computation.1 | async-start | bytes 3145728 | tf_op jit(solution)/shard_map/all_to_all | solution.py:314
  38.7 23.9 %collective-permute-start.1 = (bf16[2,16,4,48,128]{4,3,2,1,0:T(8,128)(2,1)S(1)}, bf16[2,16,4,48,128]{4,3,2,1,0:T(8,128)(2,1)}, u32[]{:S(2)}, u32[]{:S(2)}) collective-permute-start(bf16[2,16,4,48,128]{4,3,2,1,0:T(8,128)(2,1)S(1)} %bitcast.21), channel_id=1, source_target_pairs={{0,1},{1,0},{2,3},{3,2},{4,5},{5,4},{6,7},{7,6},{8,9},{9,8},{10,11... | collective-permute-start | bytes 4718600 | tf_op jit(solution)/shard_map/ppermute | solution.py:318
  40.8 21.9 %collective-permute-start.2 = (bf16[16,2,48,128]{3,2,1,0:T(8,128)(2,1)}, bf16[16,2,48,128]{3,2,1,0:T(8,128)(2,1)S(1)}, u32[]{:S(2)}, u32[]{:S(2)}) collective-permute-start(bf16[16,2,48,128]{3,2,1,0:T(8,128)(2,1)} %fusion), channel_id=1, source_target_pairs={{1,32},{32,1},{3,34},{34,3},{5,36},{36,5},{7,38},{38,7},{9,40},{40... | collective-permute-start | bytes 1179656 | tf_op jit(solution)/shard_map/ppermute | solution.py:328
  62.6 1.2 copy-start.4
  100.4 1.0 copy-start.2
  101.4 7.3 %copy-start.1 = (bf16[2,16,4,48,128]{4,3,2,1,0:T(8,128)(2,1)S(1)}, bf16[2,16,4,48,128]{4,3,2,1,0:T(8,128)(2,1)}, u32[]{:S(2)}) copy-start(bf16[2,16,4,48,128]{4,3,2,1,0:T(8,128)(2,1)} %get-tuple-element.15.own_ref) | copy-start | bytes 4718596
  101.4 28.0 %all-to-all-start.2 = ((bf16[32,4,48,128]{3,2,1,0:T(8,128)(2,1)}), bf16[32,4,48,128]{3,2,1,0:T(8,128)(2,1)S(1)}, u32[]{:S(2)}, u32[]{:S(2)}) async-start(bf16[32,4,48,128]{3,2,1,0:T(8,128)(2,1)} %bitcast.25), calls=%async_computation.2 | async-start | bytes 3145728 | tf_op jit(solution)/shard_map/all_to_all | solution.py:314
  105.5 3.1 %collective-permute-start.3 = (bf16[16,6,48,128]{3,2,1,0:T(8,128)(2,1)}, bf16[16,6,48,128]{3,2,1,0:T(8,128)(2,1)S(1)}, u32[]{:S(2)}, u32[]{:S(2)}) collective-permute-start(bf16[16,6,48,128]{3,2,1,0:T(8,128)(2,1)} %copy-done.2), channel_id=1, source_target_pairs={{0,1},{1,0},{2,3},{3,2},{4,5},{5,4},{6,7},{7,6},{8,9},{9,8},{10,11... | collective-permute-start | bytes 3538952 | tf_op jit(solution)/shard_map/ppermute | solution.py:318
  105.8 0.7 collective-permute-start.4
  129.5 27.9 %all-to-all-start.3 = ((bf16[32,4,48,128]{3,2,1,0:T(8,128)(2,1)}), bf16[32,4,48,128]{3,2,1,0:T(8,128)(2,1)S(1)}, u32[]{:S(2)}, u32[]{:S(2)}) async-start(bf16[32,4,48,128]{3,2,1,0:T(8,128)(2,1)} %bitcast.11), calls=%async_computation.3 | async-start | bytes 3145728 | tf_op jit(solution)/shard_map/all_to_all | solution.py:314
